TPU v7x, 256 devices: a whole 4x4x8 slice. The times are simulated.
256 devices in a mesh: section: 16 (over z, core), tp: 8 (over y, x_lo), dp: 2 (over x_hi).
Axes of the slice: x: 4 (x_hi: 2, x_lo: 2; x = x_hi * 2 + x_lo), y: 4, z: 8, core: 2. Of those that a mesh axis runs over, the one named last changes fastest.
Arguments:
- tokens: bfloat16 [1024, 8192], P('dp', 'tp'), parts along dimension 0, may hold values from -8 to 8
- ln_gain: float32 [16, 8192], P('section', 'tp'), may hold values from 0.5 to 1.5
- ln_bias: float32 [16, 8192], P('section', 'tp'), may hold values from -1.5 to 1.5
- w_qkv: bfloat16 [16, 8, 8192, 384], P('section', None, 'tp'), may hold values from -1 to 1
- w_out: bfloat16 [16, 1024, 8192], P('section', None, 'tp'), may hold values from -0.0625 to 0.0625
Outputs:
- states: bfloat16 [16, 1024, 8192], P('section', 'dp', 'tp'), parts along dimension 1
There are 2 independent parts, one for each index of `dp`. A program takes and returns all parts, laid end to end along the dimension named above; an argument that names none is the same for every part. Nothing has to cross between parts.
All inputs are finite; a program needn't handle non-finite values.
Results may differ from a plain program's by a relative error of at most 0.03.
Values may be sent and summed in bfloat16 or wider, within the bound.
No kernel may reach another device: no remote copies, remote signals or barrier semaphores. Data moves between devices by JAX's collectives and lax.ppermute only.
A program may use at most 64 MiB of HBM per device.

v0:
```python
import functools

import jax
import jax.numpy as jnp
from jax import lax
from jax.experimental import pallas as pl
from jax.experimental.pallas import tpu as pltpu
from jax.sharding import PartitionSpec as P

SPAN = 8
TP = 8
CHIPS = 4
EXTRA = 16
EPS = 1e-05
SEGMENT = 256
BLOCKS = 1
BF16 = jnp.bfloat16
F32 = jnp.float32
VMEM = pl.BlockSpec(memory_space=pltpu.VMEM)
SMEM = pl.BlockSpec(memory_space=pltpu.SMEM)
HBM = pl.BlockSpec(memory_space=pl.ANY)


def params(mib):
    return pltpu.CompilerParams(vmem_limit_bytes=mib * 1024 * 1024)


def segments_of(rows):
    size = min(rows, SEGMENT)
    return [(start, size) for start in range(0, rows, size)]


def split_parts(value, count):
    parts = []
    for _ in range(count):
        part = value.astype(BF16).astype(F32)
        parts.append(part)
        value = value - part
    return parts


def ending(head_line, offset_line, first, second, width):
    vectors = split_parts(head_line, 2) + split_parts(offset_line, 2)
    for line in (first, second):
        for start, size in segments_of(line.shape[1]):
            for part in split_parts(line[:, start : start + size], 3):
                vectors.append(jnp.concatenate([part, jnp.zeros((1, width - size), F32)], axis=1))
    row = lax.broadcasted_iota(jnp.int32, (EXTRA, width), 0)
    table = jnp.zeros((EXTRA, width), F32)
    for number, vector in enumerate(vectors):
        table = table + jnp.where(row == number, vector, 0.0)
    return table


def combine(pieces, features):
    rows, width = pieces[0].shape[0] - EXTRA, pieces[0].shape[1]
    segments = segments_of(rows)
    total = jnp.zeros((rows, width), F32)
    heads, firsts, offset, second = [], [], 0.0, 0.0
    for piece in pieces:
        total = total + piece[0:rows, :].astype(F32)
        ends = piece[rows : rows + EXTRA, :].astype(F32)
        heads.append(ends[0:1] + ends[1:2])
        offset = offset + (ends[2:3] + ends[3:4])
        lines = []
        for kind in range(2):
            spans = []
            for number, (_, size) in enumerate(segments):
                slot = 4 + (kind * len(segments) + number) * 3
                spans.append((ends[slot : slot + 1] + ends[slot + 1 : slot + 2] + ends[slot + 2 : slot + 3])[:, :size])
            lines.append(jnp.concatenate(spans, axis=1) if len(spans) > 1 else spans[0])
        firsts.append(lines[0])
        second = second + lines[1]
    first = sum(firsts)
    count = features * len(pieces)
    average = first * (1.0 / count)
    variance = second * (1.0 / count) - average * average
    scale = lax.rsqrt(jnp.maximum(variance, 0.0) + EPS)
    line_row = lax.broadcasted_iota(jnp.int32, (128, rows), 0)
    table = jnp.where(line_row == TP, scale, 0.0)
    head_row = lax.broadcasted_iota(jnp.int32, (128, width), 0)
    matrix = jnp.zeros((128, width), F32)
    for number in range(len(pieces)):
        table = jnp.where(line_row == number, firsts[number] * (1.0 / features) - average, table)
        matrix = jnp.where(head_row == number, heads[number], matrix)
    turned = table.T
    total = total + jnp.dot(
        turned, matrix, preferred_element_type=F32, precision=lax.Precision.HIGHEST
    )
    return total, turned[:, TP : TP + 1], offset


def cheap():
    return pl.CostEstimate(flops=1, bytes_accessed=1, transcendentals=0)


def qkv_kernel(block, layered, after_count, *refs):
    refs = list(refs)
    place, x_ref = refs.pop(0), refs.pop(0)
    pieces = [refs.pop(0) for _ in range(2)] if layered else []
    gain_ref, bias_ref, w_ref = refs.pop(0), refs.pop(0), refs.pop(0)
    del refs[:after_count]
    base_ref = refs.pop(0) if layered else None
    out_ref, lhs, w_buf, sems = refs
    core, layer = place[1], place[3]
    columns = x_ref.shape[1]
    rows = lhs.shape[0] - EXTRA
    width = w_buf.shape[2]

    copies = []
    for head in range(TP):
        copy = pltpu.make_async_copy(w_ref.at[head], w_buf.at[head], sems.at[head])
        copy.start()
        copies.append(copy)

    if layered:
        half_rows = rows // 2
        for half, piece in ((core, pieces[0]), (1 - core, pieces[1])):
            target = pl.ds(pl.multiple_of(half * half_rows, half_rows), half_rows)
            tokens = x_ref[target, :].astype(F32)
            added = tokens + piece[...].astype(F32)
            base_ref[target, :] = jnp.where(layer == 1, added, tokens).astype(BF16)
        source = base_ref
    else:
        source = x_ref

    gain = gain_ref[...]
    bias = bias_ref[...]
    value = source[...].astype(F32)
    first = jnp.sum(value, axis=1, keepdims=True)
    second = jnp.sum(value * value, axis=1, keepdims=True)
    lhs[0:rows, :] = ((value - first * (1.0 / columns)) * gain).astype(BF16)
    lane = lax.broadcasted_iota(jnp.int32, (rows, 128), 1)
    turned = jnp.where(lane == 0, first, jnp.where(lane == 1, second, 0.0)).T
    row16 = lax.broadcasted_iota(jnp.int32, (EXTRA, columns), 0)
    tail = jnp.zeros((EXTRA, columns), F32)
    for number, vector in enumerate(split_parts(gain, 2) + split_parts(bias, 2)):
        tail = tail + jnp.where(row16 == number, vector, 0.0)
    lhs[rows : rows + EXTRA, :] = tail.astype(BF16)
    blank = jnp.zeros((1, width), F32)
    lines = ending(blank, blank, turned[0:1, :], turned[1:2, :], width)
    out_row = lax.broadcasted_iota(jnp.int32, (EXTRA, width), 0)

    for head in range(TP):
        copies[head].wait()
        result = jnp.dot(lhs[...], w_buf[head], preferred_element_type=F32)
        ends = result[rows : rows + EXTRA, :]
        table = lines
        vectors = split_parts(ends[0:1] + ends[1:2], 2) + split_parts(ends[2:3] + ends[3:4], 2)
        for number, vector in enumerate(vectors):
            table = table + jnp.where(out_row == number, vector, 0.0)
        out_ref[head, 0:rows, :] = result[0:rows, :].astype(BF16)
        out_ref[head, rows : rows + EXTRA, :] = table.astype(BF16)


def whole(shape):
    return pl.BlockSpec(shape, lambda _: (0,) * len(shape))


def qkv(place, x, block, pieces, gain, bias, w, after):
    rows, columns = x.shape[0] // BLOCKS, x.shape[1]
    heads, _, width = w.shape
    shapes = [jax.ShapeDtypeStruct((heads, rows + EXTRA, width), BF16)]
    if pieces:
        shapes = [jax.ShapeDtypeStruct((rows, columns), BF16)] + shapes
    out = pl.pallas_call(
        functools.partial(qkv_kernel, block, bool(pieces), len(after)),
        grid=(1,),
        out_shape=shapes,
        in_specs=[SMEM, pl.BlockSpec((rows, columns), lambda _: (block, 0))]
        + [whole(value.shape) for value in pieces]
        + [whole(gain.shape), whole(bias.shape), HBM]
        + [HBM] * len(after),
        out_specs=[whole(shape.shape) for shape in shapes],
        scratch_shapes=[
            pltpu.VMEM((rows + EXTRA, columns), BF16),
            pltpu.VMEM((heads, columns, width), BF16),
            pltpu.SemaphoreType.DMA((TP,)),
        ],
        compiler_params=params(48),
        cost_estimate=cheap(),
        name="qkv",
    )(place, x, *pieces, gain, bias, w, *after)
    return out if pieces else (None, out[0])


def attention_kernel(previous, features, after_count, *refs):
    refs = list(refs)
    pieces_ref = refs.pop(0)
    old_keys = [refs.pop(0) for _ in range(previous)]
    old_values = [refs.pop(0) for _ in range(previous)]
    del refs[:after_count]
    out_ref, key_ref, value_ref = refs
    rows, head_dim = out_ref.shape
    total, scale, offset = combine([pieces_ref.at[t] for t in range(TP)], features // TP)
    joined = (total * scale + offset).astype(BF16)
    query = joined[:, :head_dim]
    key = joined[:, head_dim : 2 * head_dim]
    value = joined[:, 2 * head_dim :]
    key_ref[...] = key
    value_ref[...] = value
    keys = jnp.concatenate([old[...] for old in old_keys] + [key], axis=0) if previous else key
    values = jnp.concatenate([old[...] for old in old_values] + [value], axis=0) if previous else value
    length = (previous + 1) * rows
    scores = lax.dot_general(
        query, keys, (((1,), (1,)), ((), ())), preferred_element_type=F32
    ) * (1.0 / head_dim**0.5)
    at_query = lax.broadcasted_iota(jnp.int32, (rows, length), 0) + previous * rows
    at_key = lax.broadcasted_iota(jnp.int32, (rows, length), 1)
    scores = jnp.where(at_key <= at_query, scores, -1e30)
    highest = jnp.max(scores, axis=1, keepdims=True)
    lifted = jnp.exp(scores - highest)
    weights = (lifted * (1.0 / jnp.sum(lifted, axis=1, keepdims=True))).astype(BF16)
    out_ref[...] = jnp.dot(weights, values, preferred_element_type=F32).astype(BF16)


def attention(pieces, old, features, after):
    rows = pieces.shape[1] - EXTRA
    head_dim = pieces.shape[2] // 3
    shape = jax.ShapeDtypeStruct((rows, head_dim), BF16)
    return pl.pallas_call(
        functools.partial(attention_kernel, len(old), features, len(after)),
        out_shape=[shape] * 3,
        in_specs=[VMEM] * (1 + 2 * len(old)) + [HBM] * len(after),
        out_specs=[VMEM] * 3,
        compiler_params=params(24),
        cost_estimate=cheap(),
        name="attention",
    )(pieces, *[k for k, _ in old], *[v for _, v in old], *after)


def project_kernel(passing, after_count, place, *refs):
    refs = list(refs)
    pieces = [refs.pop(0) for _ in range(TP)]
    w_ref = refs.pop(0)
    old = [refs.pop(0) for _ in range(2)] if passing else None
    del refs[:after_count]
    keep_ref, send_ref, side = refs
    me, core, layer = place[0], place[1], place[3]
    rows, head_dim = pieces[0].shape

    def work():
        for d in range(TP):
            start = pl.multiple_of(jnp.bitwise_xor(me, d) * head_dim, head_dim)
            side[:, pl.ds(start, head_dim)] = pieces[d][...]
        for half, target in ((1 - core, send_ref), (core, keep_ref)):
            place_rows = pl.ds(pl.multiple_of(half * (rows // 2), rows // 2), rows // 2)
            target[...] = jnp.dot(
                side[place_rows, :], w_ref[...], preferred_element_type=F32
            ).astype(BF16)

    if passing:
        pl.when(layer == 1)(work)

        @pl.when(layer == 0)
        def _():
            keep_ref[...] = old[0][...]
            send_ref[...] = old[1][...]
    else:
        work()


def project(place, pieces, w, old, after):
    rows, head_dim = pieces[0].shape
    columns = w.shape[1]
    shape = jax.ShapeDtypeStruct((rows // 2, columns), BF16)
    old = list(old) if old else []
    return pl.pallas_call(
        functools.partial(project_kernel, bool(old), len(after)),
        out_shape=[shape] * 2,
        in_specs=[SMEM] + [VMEM] * (TP + 1 + len(old)) + [HBM] * len(after),
        out_specs=[VMEM] * 2,
        scratch_shapes=[pltpu.VMEM((rows, TP * head_dim), BF16)],
        compiler_params=params(24),
        cost_estimate=cheap(),
        name="project",
    )(place, *pieces, w, *old, *after)


def quarters_kernel(place, keep_ref, got_ref, *outs):
    chip = place[2]
    size = outs[0].shape[0]
    for d in range(CHIPS):
        rows = pl.ds(pl.multiple_of(jnp.bitwise_xor(chip, d) * size, size), size)
        outs[d][...] = (keep_ref[rows, :].astype(F32) + got_ref[rows, :].astype(F32)).astype(BF16)


def quarters(place, keep, got):
    rows, columns = keep.shape
    return pl.pallas_call(
        quarters_kernel,
        out_shape=[jax.ShapeDtypeStruct((rows // CHIPS, columns), BF16)] * CHIPS,
        in_specs=[SMEM, VMEM, VMEM],
        out_specs=[VMEM] * CHIPS,
        compiler_params=params(16),
        cost_estimate=cheap(),
        name="quarters",
    )(place, keep, got)


def arrange_kernel(after_count, place, *refs):
    chip = place[2]
    out_ref = refs[CHIPS + after_count]
    size = out_ref.shape[0] // CHIPS
    for d in range(CHIPS):
        rows = pl.ds(pl.multiple_of(jnp.bitwise_xor(chip, d) * size, size), size)
        out_ref[rows, :] = refs[d][...]


def arrange(place, pieces, after):
    rows, columns = pieces[0].shape
    return pl.pallas_call(
        functools.partial(arrange_kernel, len(after)),
        out_shape=jax.ShapeDtypeStruct((rows * CHIPS, columns), BF16),
        in_specs=[SMEM] + [VMEM] * CHIPS + [HBM] * len(after),
        out_specs=VMEM,
        compiler_params=params(16),
        cost_estimate=cheap(),
        name="arrange",
    )(place, *pieces, *after)


def finish_kernel(place, base_ref, keep_ref, got_ref, send_ref, other_keep_ref, own_ref, other_ref, out_ref):
    core = place[1]
    half_rows = keep_ref.shape[0]
    second = core.astype(F32)
    for half, sums, mine, theirs in (
        (core, own_ref, keep_ref, got_ref),
        (1 - core, other_ref, send_ref, other_keep_ref),
    ):
        rows = pl.ds(pl.multiple_of(half * half_rows, half_rows), half_rows)
        out_ref[rows, :] = (
            base_ref[rows, :].astype(F32)
            + sums[...].astype(F32)
            + mine[...].astype(F32)
            + second * theirs[...].astype(F32)
        ).astype(BF16)


def finish(place, base, *values):
    return pl.pallas_call(
        finish_kernel,
        out_shape=jax.ShapeDtypeStruct(base.shape, BF16),
        in_specs=[SMEM] + [VMEM] * (1 + len(values)),
        out_specs=VMEM,
        compiler_params=params(24),
        cost_estimate=cheap(),
        name="finish",
    )(place, base, *values)


def over_tp(value):
    return lax.all_to_all(value, "tp", 0, 0, tiled=True)


def over_cores(value):
    return lax.ppermute(value, "section", [(s, s ^ 1) for s in range(2 * SPAN)])


def over_chips(value, d):
    return lax.ppermute(value, "section", [(s, s ^ (2 * d)) for s in range(2 * SPAN)])


def spread(value):
    return [value] + [
        lax.ppermute(value, "tp", [(t, t ^ d) for t in range(TP)]) for d in range(1, TP)
    ]


def over_layer(values):
    return [values[0]] + [over_chips(values[d], d) for d in range(1, CHIPS)]


def on_device(tokens, ln_gain, ln_bias, w_qkv, w_out):
    section = lax.axis_index("section")
    me = lax.axis_index("tp")
    core = section % 2
    chip = (section // 2) % CHIPS
    layer = section // SPAN
    place = jnp.stack([me, core, chip, layer]).astype(jnp.int32)
    weight_in = w_qkv[0]
    weight_back = w_out[0]
    features = tokens.shape[1] * TP

    vectors = jnp.concatenate([ln_gain, ln_bias], axis=0)
    even = vectors
    for d in range(1, CHIPS):
        even = jnp.where(chip == d, over_chips(vectors, d), even)
    vectors = jnp.where(core == 0, even, over_cores(even))
    gain, bias = vectors[0:1], vectors[1:2]

    steps = range(BLOCKS)
    pieces, kept, sums, totals = [], [], [], []
    after = []
    for block in steps:
        _, part = qkv(place, tokens, block, [], gain, bias, weight_in, after)
        pieces.append(over_tp(part))
        after = [part]
    old, after = [], []
    for block in steps:
        out, key, value = attention(pieces[block], old, features, after)
        old.append((key, value))
        keep, send = project(place, spread(out), weight_back, None, totals[-1:])
        kept.append((keep, send))
        quarter = quarters(place, keep, over_cores(send))
        after = [quarter[0]]
        total = sum(value.astype(F32) for value in over_layer(quarter)).astype(BF16)
        totals.append(total)
        half = arrange(place, [over_chips(total, CHIPS ^ d) for d in range(CHIPS)], [])
        sums.append((half, over_cores(half)))

    bases, pieces, old, after = [], [], [], totals[-1:]
    for block in steps:
        base, part = qkv(place, tokens, block, sums[block], gain, bias, weight_in, after)
        bases.append(base)
        pieces.append(over_tp(part))
        after = [part]
    outputs, gate = [], []
    for block in steps:
        out, key, value = attention(pieces[block], old, features, after)
        old.append((key, value))
        keep, send = project(place, spread(out), weight_back, kept[block], gate)
        got = over_cores(send)
        other_keep = over_cores(keep)
        quarter = quarters(place, keep, got)
        after = [quarter[0]]
        arrived = over_layer(quarter)
        before = []
        for d in range(CHIPS):
            target = jnp.bitwise_xor(chip, d)
            before.append(
                sum(
                    jnp.where(jnp.bitwise_xor(chip, e) < target, arrived[e].astype(F32), 0.0)
                    for e in range(CHIPS)
                ).astype(BF16)
            )
        gate = [before[0]]
        own = arrange(place, over_layer(before), [])
        outputs.append(finish(place, bases[block], keep, got, send, other_keep, own, over_cores(own)))
    return (outputs[0] if BLOCKS == 1 else jnp.concatenate(outputs, axis=0))[None]


def solution(mesh):
    return jax.shard_map(
        on_device,
        mesh=mesh,
        in_specs=(
            P("dp", "tp"),
            P("section", "tp"),
            P("section", "tp"),
            P("section", None, "tp", None),
            P("section", None, "tp"),
        ),
        out_specs=P("section", "dp", "tp"),
        check_vma=False,
    )
```

profile of v0, /device:TPU:1, one launch (start us, length us, event | category | flops | bytes accessed | tf_op | source)
XLA Modules:
  0.0 247.6 jit_solution(10271515264807934099)
XLA Ops:
  0.0 0.7 pad_maximum_fusion
  0.7 5.3 %collective-permute-start = (f32[2,1024]{1,0:T(2,128)S(1)}, f32[2,1024]{1,0:T(2,128)S(1)}, u32[]{:S(2)}, u32[]{:S(2)}) collective-permute-start(f32[2,1024]{1,0:T(2,128)S(1)} %pad_maximum_fusion), channel_id=1, source_target_pairs={{0,96},{16,112},{32,64},{48,80},{64,32},{80,48},{96,0},{112,16},{1... | collective-permute-start | bytes 24584 | tf_op jit(solution)/shard_map/ppermute | solution.py:361
  6.4 0.7 collective-permute-done
  7.0 2.4 collective-permute-done.1
  9.4 0.7 select_select_fusion
  10.1 2.2 collective-permute-start.3
  12.4 0.8 collective-permute-done.3
  13.2 1.2 copy-done.2
  14.4 7.6 %qkv.2 = bf16[8,528,384]{2,1,0:T(8,128)(2,1)S(1)} custom-call(s32[4]{0:T(128)S(1)} %pad_add_fusion.refs_0_.place, bf16[512,1024]{1,0:T(8,128)(2,1)S(1)} %copy-done.2, f32[1,1024]{1,0:T(1,128)S(1)} %get-tuple-element.42.refs_2_.refs_4_, f32[1,1024]{1,0:T(1,128)S(1)} %get-tuple-element.41.refs_3_.refs_5_, bf16[8,1024,384]{2,1,0:T(8,128)(2,1)} %bitcast.9), custom_call_target="tpu_custom_call" | custom-call | flops 1 | bytes 1 | tf_op jit(solution)/shard_map/qkv/pallas_call | solution.py:166
  22.0 43.6 %all_to_all.10.refs_0_ = bf16[8,528,384]{2,1,0:T(8,128)(2,1)S(1)} all-to-all(bf16[8,528,384]{2,1,0:T(8,128)(2,1)S(1)} %qkv.2), channel_id=1, replica_groups=mesh['section'=16,'tp'=8,'dp'=2] {'tp'}, dimensions={0} | all-to-all | bytes 6488064 | tf_op jit(solution)/shard_map/all_to_all | solution.py:353
  65.6 2.1 attention.2
  67.7 1.0 collective-permute-start.4
  69.0 1.3 collective-permute-start.6
  70.4 0.9 collective-permute-start.7
  71.3 2.7 %collective-permute-start.8 = (bf16[512,128]{1,0:T(8,128)(2,1)S(1)}, bf16[512,128]{1,0:T(8,128)(2,1)S(1)}, u32[]{:S(2)}, u32[]{:S(2)}) collective-permute-start(bf16[512,128]{1,0:T(8,128)(2,1)S(1)} %get-tuple-element.21.refs_0_), channel_id=1, source_target_pairs={{0,10},{2,8},{4,14},{6,12},{8,2},{10,0},{12,6},{14,4},{1,11},{3,9}... | collective-permute-start | bytes 393224 | tf_op jit(solution)/shard_map/ppermute | solution.py:366
  74.0 1.0 collective-permute-start.9
  75.0 2.0 collective-permute-start.10
  76.9 6.0 %collective-permute-done.7.refs_4_ = bf16[512,128]{1,0:T(8,128)(2,1)S(1)} collective-permute-done((bf16[512,128]{1,0:T(8,128)(2,1)S(1)}, bf16[512,128]{1,0:T(8,128)(2,1)S(1)}, u32[]{:S(2)}, u32[]{:S(2)}) %collective-permute-start.7) | collective-permute-done | bytes 131104 | tf_op jit(solution)/shard_map/ppermute | solution.py:366
  83.0 3.1 %collective-permute-done.9.refs_6_ = bf16[512,128]{1,0:T(8,128)(2,1)S(1)} collective-permute-done((bf16[512,128]{1,0:T(8,128)(2,1)S(1)}, bf16[512,128]{1,0:T(8,128)(2,1)S(1)}, u32[]{:S(2)}, u32[]{:S(2)}) %collective-permute-start.9) | collective-permute-done | bytes 131104 | tf_op jit(solution)/shard_map/ppermute | solution.py:366
  86.0 2.1 project.2
  88.1 2.9 %collective-permute-start.11 = (bf16[256,1024]{1,0:T(8,128)(2,1)S(1)}, bf16[256,1024]{1,0:T(8,128)(2,1)S(1)}, u32[]{:S(2)}, u32[]{:S(2)}) collective-permute-start(bf16[256,1024]{1,0:T(8,128)(2,1)S(1)} %get-tuple-element.23.refs_10_), channel_id=1, source_target_pairs={{0,16},{16,0},{32,48},{48,32},{64,80},{80,64},{96,112},{112,96},{1... | collective-permute-start | bytes 1572872 | tf_op jit(solution)/shard_map/ppermute | solution.py:357
  91.0 1.5 collective-permute-done.11.got_ref
  92.5 0.7 quarters.2
  93.2 1.3 collective-permute-start.14
  94.5 0.7 collective-permute-start.13
  95.1 1.7 collective-permute-start.12
  96.8 3.0 %collective-permute-done.14 = bf16[64,1024]{1,0:T(8,128)(2,1)S(1)} collective-permute-done((bf16[64,1024]{1,0:T(8,128)(2,1)S(1)}, bf16[64,1024]{1,0:T(8,128)(2,1)S(1)}, u32[]{:S(2)}, u32[]{:S(2)}) %collective-permute-start.14) | collective-permute-done | bytes 131104 | tf_op jit(solution)/shard_map/ppermute | solution.py:361
  99.8 7.2 %collective-permute-done.13 = bf16[64,1024]{1,0:T(8,128)(2,1)S(1)} collective-permute-done((bf16[64,1024]{1,0:T(8,128)(2,1)S(1)}, bf16[64,1024]{1,0:T(8,128)(2,1)S(1)}, u32[]{:S(2)}, u32[]{:S(2)}) %collective-permute-start.13) | collective-permute-done | bytes 131104 | tf_op jit(solution)/shard_map/ppermute | solution.py:361
  107.1 4.7 %collective-permute-start.15 = (bf16[64,1024]{1,0:T(8,128)(2,1)S(1)}, bf16[64,1024]{1,0:T(8,128)(2,1)S(1)}, u32[]{:S(2)}, u32[]{:S(2)}) collective-permute-start(bf16[64,1024]{1,0:T(8,128)(2,1)S(1)} %add_convert_fusion.refs_7_), channel_id=1, source_target_pairs={{0,128},{16,144},{32,160},{48,176},{64,192},{80,208},{96,224},{112... | collective-permute-start | bytes 393224 | tf_op jit(solution)/shard_map/ppermute | solution.py:361
  111.8 4.0 %collective-permute-start.17 = (bf16[64,1024]{1,0:T(8,128)(2,1)S(1)}, bf16[64,1024]{1,0:T(8,128)(2,1)S(1)}, u32[]{:S(2)}, u32[]{:S(2)}) collective-permute-start(bf16[64,1024]{1,0:T(8,128)(2,1)S(1)} %add_convert_fusion.refs_7_), channel_id=1, source_target_pairs={{0,192},{16,208},{32,224},{48,240},{64,128},{80,144},{96,160},{112... | collective-permute-start | bytes 393224 | tf_op jit(solution)/shard_map/ppermute | solution.py:361
  115.8 11.6 %collective-permute-done.16.refs_1_ = bf16[64,1024]{1,0:T(8,128)(2,1)S(1)} collective-permute-done((bf16[64,1024]{1,0:T(8,128)(2,1)S(1)}, bf16[64,1024]{1,0:T(8,128)(2,1)S(1)}, u32[]{:S(2)}, u32[]{:S(2)}) %collective-permute-start.16) | collective-permute-done | bytes 131104 | tf_op jit(solution)/shard_map/ppermute | solution.py:361
  127.5 2.8 %collective-permute-done.17.refs_2_ = bf16[64,1024]{1,0:T(8,128)(2,1)S(1)} collective-permute-done((bf16[64,1024]{1,0:T(8,128)(2,1)S(1)}, bf16[64,1024]{1,0:T(8,128)(2,1)S(1)}, u32[]{:S(2)}, u32[]{:S(2)}) %collective-permute-start.17) | collective-permute-done | bytes 131104 | tf_op jit(solution)/shard_map/ppermute | solution.py:361
  130.3 2.8 %collective-permute-done.18.refs_3_ = bf16[64,1024]{1,0:T(8,128)(2,1)S(1)} collective-permute-done((bf16[64,1024]{1,0:T(8,128)(2,1)S(1)}, bf16[64,1024]{1,0:T(8,128)(2,1)S(1)}, u32[]{:S(2)}, u32[]{:S(2)}) %collective-permute-start.18) | collective-permute-done | bytes 131104 | tf_op jit(solution)/shard_map/ppermute | solution.py:361
  133.7 0.9 collective-permute-start.19
  134.5 1.5 collective-permute-done.19.refs_3_
  136.1 9.4 %qkv.3 = (bf16[512,1024]{1,0:T(8,128)(2,1)S(1)}, bf16[8,528,384]{2,1,0:T(8,128)(2,1)}) custom-call(s32[4]{0:T(128)S(1)} %pad_add_fusion.refs_0_.place, bf16[512,1024]{1,0:T(8,128)(2,1)S(1)} %copy-done.2, bf16[256,1024]{1,0:T(8,128)(2,1)S(1)} %arrange.2.refs_2_, bf16[256,1024]{1,0:T(8,128)(2,1)S(1)} %collective-permute-done.19.refs_3_, ...), custom_call_target="tpu_custom_call" | custom-call | flops 1 | bytes 1 | tf_op jit(solution)/shard_map/qkv/pallas_call | solution.py:166
  145.5 42.8 %all_to_all.11.refs_0_ = bf16[8,528,384]{2,1,0:T(8,128)(2,1)S(1)} all-to-all(bf16[8,528,384]{2,1,0:T(8,128)(2,1)} %get-tuple-element.29.refs_1_), channel_id=1, replica_groups=mesh['section'=16,'tp'=8,'dp'=2] {'tp'}, dimensions={0} | all-to-all | bytes 6488064 | tf_op jit(solution)/shard_map/all_to_all | solution.py:353
  188.3 2.1 attention.3
  190.4 0.7 collective-permute-start.20
  191.5 1.6 collective-permute-start.22
  193.1 0.9 collective-permute-start.23
  194.0 2.5 collective-permute-start.24
  196.5 1.0 collective-permute-start.25
  197.4 2.2 collective-permute-start.26
  199.6 6.1 %collective-permute-done.23.refs_4_ = bf16[512,128]{1,0:T(8,128)(2,1)S(1)} collective-permute-done((bf16[512,128]{1,0:T(8,128)(2,1)S(1)}, bf16[512,128]{1,0:T(8,128)(2,1)S(1)}, u32[]{:S(2)}, u32[]{:S(2)}) %collective-permute-start.23) | collective-permute-done | bytes 131104 | tf_op jit(solution)/shard_map/ppermute | solution.py:366
  205.7 2.9 %collective-permute-done.25.refs_6_ = bf16[512,128]{1,0:T(8,128)(2,1)S(1)} collective-permute-done((bf16[512,128]{1,0:T(8,128)(2,1)S(1)}, bf16[512,128]{1,0:T(8,128)(2,1)S(1)}, u32[]{:S(2)}, u32[]{:S(2)}) %collective-permute-start.25) | collective-permute-done | bytes 131104 | tf_op jit(solution)/shard_map/ppermute | solution.py:366
  208.6 0.6 project.3
  209.2 2.8 %collective-permute-start.27 = (bf16[256,1024]{1,0:T(8,128)(2,1)S(1)}, bf16[256,1024]{1,0:T(8,128)(2,1)S(1)}, u32[]{:S(2)}, u32[]{:S(2)}) collective-permute-start(bf16[256,1024]{1,0:T(8,128)(2,1)S(1)} %get-tuple-element.32.send_ref), channel_id=1, source_target_pairs={{0,16},{16,0},{32,48},{48,32},{64,80},{80,64},{96,112},{112,96},{1... | collective-permute-start | bytes 1572872 | tf_op jit(solution)/shard_map/ppermute | solution.py:357
  212.0 1.5 collective-permute-done.27.got_ref
  213.5 0.7 quarters.3
  214.3 2.7 %collective-permute-start.30 = (bf16[64,1024]{1,0:T(8,128)(2,1)S(1)}, bf16[64,1024]{1,0:T(8,128)(2,1)S(1)}, u32[]{:S(2)}, u32[]{:S(2)}) collective-permute-start(bf16[64,1024]{1,0:T(8,128)(2,1)S(1)} %get-tuple-element.34), channel_id=1, source_target_pairs={{0,64},{16,80},{32,96},{48,112},{64,0},{80,16},{96,32},{112,48},{1... | collective-permute-start | bytes 393224 | tf_op jit(solution)/shard_map/ppermute | solution.py:361
  217.0 0.8 collective-permute-start.31
  217.9 3.4 %collective-permute-done.29 = bf16[64,1024]{1,0:T(8,128)(2,1)S(1)} collective-permute-done((bf16[64,1024]{1,0:T(8,128)(2,1)S(1)}, bf16[64,1024]{1,0:T(8,128)(2,1)S(1)}, u32[]{:S(2)}, u32[]{:S(2)}) %collective-permute-start.29) | collective-permute-done | bytes 131104 | tf_op jit(solution)/shard_map/ppermute | solution.py:361
  221.3 4.7 %collective-permute-done.31 = bf16[64,1024]{1,0:T(8,128)(2,1)S(1)} collective-permute-done((bf16[64,1024]{1,0:T(8,128)(2,1)S(1)}, bf16[64,1024]{1,0:T(8,128)(2,1)S(1)}, u32[]{:S(2)}, u32[]{:S(2)}) %collective-permute-start.31) | collective-permute-done | bytes 131104 | tf_op jit(solution)/shard_map/ppermute | solution.py:361
  226.2 3.1 %collective-permute-start.32 = (bf16[64,1024]{1,0:T(8,128)(2,1)S(1)}, bf16[64,1024]{1,0:T(8,128)(2,1)S(1)}, u32[]{:S(2)}, u32[]{:S(2)}) collective-permute-start(bf16[64,1024]{1,0:T(8,128)(2,1)S(1)} %get-tuple-element.38), channel_id=1, source_target_pairs={{0,32},{16,48},{32,0},{48,16},{64,96},{80,112},{96,64},{112,80},{1... | collective-permute-start | bytes 393224 | tf_op jit(solution)/shard_map/ppermute | solution.py:361
  229.3 1.1 collective-permute-start.33
  230.4 1.1 collective-permute-start.34
  231.5 1.8 collective-permute-start.28
  233.3 1.4 collective-permute-done.33.refs_2_
  234.7 4.5 %collective-permute-done.34.refs_3_ = bf16[64,1024]{1,0:T(8,128)(2,1)S(1)} collective-permute-done((bf16[64,1024]{1,0:T(8,128)(2,1)S(1)}, bf16[64,1024]{1,0:T(8,128)(2,1)S(1)}, u32[]{:S(2)}, u32[]{:S(2)}) %collective-permute-start.34) | collective-permute-done | bytes 131104 | tf_op jit(solution)/shard_map/ppermute | solution.py:361
  239.2 0.6 arrange.3.own_ref
  239.8 4.1 %collective-permute-start.35 = (bf16[256,1024]{1,0:T(8,128)(2,1)S(1)}, bf16[256,1024]{1,0:T(8,128)(2,1)S(1)}, u32[]{:S(2)}, u32[]{:S(2)}) collective-permute-start(bf16[256,1024]{1,0:T(8,128)(2,1)S(1)} %arrange.3.own_ref), channel_id=1, source_target_pairs={{0,16},{16,0},{32,48},{48,32},{64,80},{80,64},{96,112},{112,96},{1... | collective-permute-start | bytes 1572872 | tf_op jit(solution)/shard_map/ppermute | solution.py:357
  243.9 1.5 collective-permute-done.35.other_ref
  245.4 2.1 finish.1
  (34 shorter events, 2.2 us)
Async XLA Ops:
  0.7 6.3 %collective-permute-start = (f32[2,1024]{1,0:T(2,128)S(1)}, f32[2,1024]{1,0:T(2,128)S(1)}, u32[]{:S(2)}, u32[]{:S(2)}) collective-permute-start(f32[2,1024]{1,0:T(2,128)S(1)} %pad_maximum_fusion), channel_id=1, source_target_pairs={{0,96},{16,112},{32,64},{48,80},{64,32},{80,48},{96,0},{112,16},{1... | collective-permute-start | bytes 24584 | tf_op jit(solution)/shard_map/ppermute | solution.py:361
  6.0 3.4 %collective-permute-start.1 = (f32[2,1024]{1,0:T(2,128)S(1)}, f32[2,1024]{1,0:T(2,128)S(1)}, u32[]{:S(2)}, u32[]{:S(2)}) collective-permute-start(f32[2,1024]{1,0:T(2,128)S(1)} %pad_maximum_fusion), channel_id=1, source_target_pairs={{0,64},{16,80},{32,96},{48,112},{64,0},{80,16},{96,32},{112,48},{1... | collective-permute-start | bytes 24584 | tf_op jit(solution)/shard_map/ppermute | solution.py:361
  6.0 3.4 %collective-permute-start.2 = (f32[2,1024]{1,0:T(2,128)S(1)}, f32[2,1024]{1,0:T(2,128)S(1)}, u32[]{:S(2)}, u32[]{:S(2)}) collective-permute-start(f32[2,1024]{1,0:T(2,128)S(1)} %pad_maximum_fusion), channel_id=1, source_target_pairs={{0,32},{16,48},{32,0},{48,16},{64,96},{80,112},{96,64},{112,80},{1... | collective-permute-start | bytes 24584 | tf_op jit(solution)/shard_map/ppermute | solution.py:361
  10.1 3.0 %collective-permute-start.3 = (f32[2,1024]{1,0:T(2,128)S(1)}, f32[2,1024]{1,0:T(2,128)S(1)}, u32[]{:S(2)}, u32[]{:S(2)}) collective-permute-start(f32[2,1024]{1,0:T(2,128)S(1)} %select_select_fusion), channel_id=1, source_target_pairs={{0,16},{16,0},{32,48},{48,32},{64,80},{80,64},{96,112},{112,96},{1... | collective-permute-start | bytes 24584 | tf_op jit(solution)/shard_map/ppermute | solution.py:357
  13.1 1.2 copy-start.2
  65.6 20.4 %copy-start.1 = (bf16[1,1024,1024]{2,1,0:T(8,128)(2,1)S(1)}, bf16[1,1024,1024]{2,1,0:T(8,128)(2,1)}, u32[]{:S(2)}) copy-start(bf16[1,1024,1024]{2,1,0:T(8,128)(2,1)} %param.9) | copy-start | bytes 6291460
  67.7 6.3 %collective-permute-start.4 = (bf16[512,128]{1,0:T(8,128)(2,1)S(1)}, bf16[512,128]{1,0:T(8,128)(2,1)S(1)}, u32[]{:S(2)}, u32[]{:S(2)}) collective-permute-start(bf16[512,128]{1,0:T(8,128)(2,1)S(1)} %get-tuple-element.21.refs_0_), channel_id=1, source_target_pairs={{0,2},{2,0},{4,6},{6,4},{8,10},{10,8},{12,14},{14,12},{1,3},{3,1},... | collective-permute-start | bytes 393224 | tf_op jit(solution)/shard_map/ppermute | solution.py:366
  68.7 6.3 %collective-permute-start.5 = (bf16[512,128]{1,0:T(8,128)(2,1)S(1)}, bf16[512,128]{1,0:T(8,128)(2,1)S(1)}, u32[]{:S(2)}, u32[]{:S(2)}) collective-permute-start(bf16[512,128]{1,0:T(8,128)(2,1)S(1)} %get-tuple-element.21.refs_0_), channel_id=1, source_target_pairs={{0,4},{2,6},{4,0},{6,2},{8,12},{10,14},{12,8},{14,10},{1,5},{3,7},... | collective-permute-start | bytes 393224 | tf_op jit(solution)/shard_map/ppermute | solution.py:366
  69.0 7.9 %collective-permute-start.6 = (bf16[512,128]{1,0:T(8,128)(2,1)S(1)}, bf16[512,128]{1,0:T(8,128)(2,1)S(1)}, u32[]{:S(2)}, u32[]{:S(2)}) collective-permute-start(bf16[512,128]{1,0:T(8,128)(2,1)S(1)} %get-tuple-element.21.refs_0_), channel_id=1, source_target_pairs={{0,6},{2,4},{4,2},{6,0},{8,14},{10,12},{12,10},{14,8},{1,7},{3,5},... | collective-permute-start | bytes 393224 | tf_op jit(solution)/shard_map/ppermute | solution.py:366
  70.4 12.6 %collective-permute-start.7 = (bf16[512,128]{1,0:T(8,128)(2,1)S(1)}, bf16[512,128]{1,0:T(8,128)(2,1)S(1)}, u32[]{:S(2)}, u32[]{:S(2)}) collective-permute-start(bf16[512,128]{1,0:T(8,128)(2,1)S(1)} %get-tuple-element.21.refs_0_), channel_id=1, source_target_pairs={{0,8},{2,10},{4,12},{6,14},{8,0},{10,2},{12,4},{14,6},{1,9},{3,11}... | collective-permute-start | bytes 393224 | tf_op jit(solution)/shard_map/ppermute | solution.py:366
  71.3 11.6 %collective-permute-start.8 = (bf16[512,128]{1,0:T(8,128)(2,1)S(1)}, bf16[512,128]{1,0:T(8,128)(2,1)S(1)}, u32[]{:S(2)}, u32[]{:S(2)}) collective-permute-start(bf16[512,128]{1,0:T(8,128)(2,1)S(1)} %get-tuple-element.21.refs_0_), channel_id=1, source_target_pairs={{0,10},{2,8},{4,14},{6,12},{8,2},{10,0},{12,6},{14,4},{1,11},{3,9}... | collective-permute-start | bytes 393224 | tf_op jit(solution)/shard_map/ppermute | solution.py:366
  74.0 12.0 %collective-permute-start.9 = (bf16[512,128]{1,0:T(8,128)(2,1)S(1)}, bf16[512,128]{1,0:T(8,128)(2,1)S(1)}, u32[]{:S(2)}, u32[]{:S(2)}) collective-permute-start(bf16[512,128]{1,0:T(8,128)(2,1)S(1)} %get-tuple-element.21.refs_0_), channel_id=1, source_target_pairs={{0,12},{2,14},{4,8},{6,10},{8,4},{10,6},{12,0},{14,2},{1,13},{3,15... | collective-permute-start | bytes 393224 | tf_op jit(solution)/shard_map/ppermute | solution.py:366
  75.0 11.0 %collective-permute-start.10 = (bf16[512,128]{1,0:T(8,128)(2,1)S(1)}, bf16[512,128]{1,0:T(8,128)(2,1)S(1)}, u32[]{:S(2)}, u32[]{:S(2)}) collective-permute-start(bf16[512,128]{1,0:T(8,128)(2,1)S(1)} %get-tuple-element.21.refs_0_), channel_id=1, source_target_pairs={{0,14},{2,12},{4,10},{6,8},{8,6},{10,4},{12,2},{14,0},{1,15},{3,13... | collective-permute-start | bytes 393224 | tf_op jit(solution)/shard_map/ppermute | solution.py:366
  88.1 4.4 %collective-permute-start.11 = (bf16[256,1024]{1,0:T(8,128)(2,1)S(1)}, bf16[256,1024]{1,0:T(8,128)(2,1)S(1)}, u32[]{:S(2)}, u32[]{:S(2)}) collective-permute-start(bf16[256,1024]{1,0:T(8,128)(2,1)S(1)} %get-tuple-element.23.refs_10_), channel_id=1, source_target_pairs={{0,16},{16,0},{32,48},{48,32},{64,80},{80,64},{96,112},{112,96},{1... | collective-permute-start | bytes 1572872 | tf_op jit(solution)/shard_map/ppermute | solution.py:357
  93.2 6.6 %collective-permute-start.14 = (bf16[64,1024]{1,0:T(8,128)(2,1)S(1)}, bf16[64,1024]{1,0:T(8,128)(2,1)S(1)}, u32[]{:S(2)}, u32[]{:S(2)}) collective-permute-start(bf16[64,1024]{1,0:T(8,128)(2,1)S(1)} %get-tuple-element.27), channel_id=1, source_target_pairs={{0,96},{16,112},{32,64},{48,80},{64,32},{80,48},{96,0},{112,16},{1... | collective-permute-start | bytes 393224 | tf_op jit(solution)/shard_map/ppermute | solution.py:361
  94.5 12.6 %collective-permute-start.13 = (bf16[64,1024]{1,0:T(8,128)(2,1)S(1)}, bf16[64,1024]{1,0:T(8,128)(2,1)S(1)}, u32[]{:S(2)}, u32[]{:S(2)}) collective-permute-start(bf16[64,1024]{1,0:T(8,128)(2,1)S(1)} %get-tuple-element.26), channel_id=1, source_target_pairs={{0,64},{16,80},{32,96},{48,112},{64,0},{80,16},{96,32},{112,48},{1... | collective-permute-start | bytes 393224 | tf_op jit(solution)/shard_map/ppermute | solution.py:361
  95.1 11.9 %collective-permute-start.12 = (bf16[64,1024]{1,0:T(8,128)(2,1)S(1)}, bf16[64,1024]{1,0:T(8,128)(2,1)S(1)}, u32[]{:S(2)}, u32[]{:S(2)}) collective-permute-start(bf16[64,1024]{1,0:T(8,128)(2,1)S(1)} %get-tuple-element.25), channel_id=1, source_target_pairs={{0,32},{16,48},{32,0},{48,16},{64,96},{80,112},{96,64},{112,80},{1... | collective-permute-start | bytes 393224 | tf_op jit(solution)/shard_map/ppermute | solution.py:361
  107.1 8.7 %collective-permute-start.15 = (bf16[64,1024]{1,0:T(8,128)(2,1)S(1)}, bf16[64,1024]{1,0:T(8,128)(2,1)S(1)}, u32[]{:S(2)}, u32[]{:S(2)}) collective-permute-start(bf16[64,1024]{1,0:T(8,128)(2,1)S(1)} %add_convert_fusion.refs_7_), channel_id=1, source_target_pairs={{0,128},{16,144},{32,160},{48,176},{64,192},{80,208},{96,224},{112... | collective-permute-start | bytes 393224 | tf_op jit(solution)/shard_map/ppermute | solution.py:361
  111.8 15.7 %collective-permute-start.16 = (bf16[64,1024]{1,0:T(8,128)(2,1)S(1)}, bf16[64,1024]{1,0:T(8,128)(2,1)S(1)}, u32[]{:S(2)}, u32[]{:S(2)}) collective-permute-start(bf16[64,1024]{1,0:T(8,128)(2,1)S(1)} %add_convert_fusion.refs_7_), channel_id=1, source_target_pairs={{0,160},{16,176},{32,128},{48,144},{64,224},{80,240},{96,192},{112... | collective-permute-start | bytes 393224 | tf_op jit(solution)/shard_map/ppermute | solution.py:361
  111.8 18.5 %collective-permute-start.17 = (bf16[64,1024]{1,0:T(8,128)(2,1)S(1)}, bf16[64,1024]{1,0:T(8,128)(2,1)S(1)}, u32[]{:S(2)}, u32[]{:S(2)}) collective-permute-start(bf16[64,1024]{1,0:T(8,128)(2,1)S(1)} %add_convert_fusion.refs_7_), channel_id=1, source_target_pairs={{0,192},{16,208},{32,224},{48,240},{64,128},{80,144},{96,160},{112... | collective-permute-start | bytes 393224 | tf_op jit(solution)/shard_map/ppermute | solution.py:361
  115.8 17.2 %collective-permute-start.18 = (bf16[64,1024]{1,0:T(8,128)(2,1)S(1)}, bf16[64,1024]{1,0:T(8,128)(2,1)S(1)}, u32[]{:S(2)}, u32[]{:S(2)}) collective-permute-start(bf16[64,1024]{1,0:T(8,128)(2,1)S(1)} %add_convert_fusion.refs_7_), channel_id=1, source_target_pairs={{0,224},{16,240},{32,192},{48,208},{64,160},{80,176},{96,128},{112... | collective-permute-start | bytes 393224 | tf_op jit(solution)/shard_map/ppermute | solution.py:361
  133.7 2.4 collective-permute-start.19
  145.5 42.8 %copy-start = (bf16[8,528,384]{2,1,0:T(8,128)(2,1)S(1)}, bf16[8,528,384]{2,1,0:T(8,128)(2,1)}, u32[]{:S(2)}) copy-start(bf16[8,528,384]{2,1,0:T(8,128)(2,1)} %get-tuple-element.29.refs_1_) | copy-start | bytes 9732100
  190.4 6.1 %collective-permute-start.20 = (bf16[512,128]{1,0:T(8,128)(2,1)S(1)}, bf16[512,128]{1,0:T(8,128)(2,1)S(1)}, u32[]{:S(2)}, u32[]{:S(2)}) collective-permute-start(bf16[512,128]{1,0:T(8,128)(2,1)S(1)} %get-tuple-element.30.refs_0_), channel_id=1, source_target_pairs={{0,2},{2,0},{4,6},{6,4},{8,10},{10,8},{12,14},{14,12},{1,3},{3,1},... | collective-permute-start | bytes 393224 | tf_op jit(solution)/shard_map/ppermute | solution.py:366
  191.1 6.3 %collective-permute-start.21 = (bf16[512,128]{1,0:T(8,128)(2,1)S(1)}, bf16[512,128]{1,0:T(8,128)(2,1)S(1)}, u32[]{:S(2)}, u32[]{:S(2)}) collective-permute-start(bf16[512,128]{1,0:T(8,128)(2,1)S(1)} %get-tuple-element.30.refs_0_), channel_id=1, source_target_pairs={{0,4},{2,6},{4,0},{6,2},{8,12},{10,14},{12,8},{14,10},{1,5},{3,7},... | collective-permute-start | bytes 393224 | tf_op jit(solution)/shard_map/ppermute | solution.py:366
  191.5 8.1 %collective-permute-start.22 = (bf16[512,128]{1,0:T(8,128)(2,1)S(1)}, bf16[512,128]{1,0:T(8,128)(2,1)S(1)}, u32[]{:S(2)}, u32[]{:S(2)}) collective-permute-start(bf16[512,128]{1,0:T(8,128)(2,1)S(1)} %get-tuple-element.30.refs_0_), channel_id=1, source_target_pairs={{0,6},{2,4},{4,2},{6,0},{8,14},{10,12},{12,10},{14,8},{1,7},{3,5},... | collective-permute-start | bytes 393224 | tf_op jit(solution)/shard_map/ppermute | solution.py:366
  193.1 12.6 %collective-permute-start.23 = (bf16[512,128]{1,0:T(8,128)(2,1)S(1)}, bf16[512,128]{1,0:T(8,128)(2,1)S(1)}, u32[]{:S(2)}, u32[]{:S(2)}) collective-permute-start(bf16[512,128]{1,0:T(8,128)(2,1)S(1)} %get-tuple-element.30.refs_0_), channel_id=1, source_target_pairs={{0,8},{2,10},{4,12},{6,14},{8,0},{10,2},{12,4},{14,6},{1,9},{3,11}... | collective-permute-start | bytes 393224 | tf_op jit(solution)/shard_map/ppermute | solution.py:366
  194.0 11.7 %collective-permute-start.24 = (bf16[512,128]{1,0:T(8,128)(2,1)S(1)}, bf16[512,128]{1,0:T(8,128)(2,1)S(1)}, u32[]{:S(2)}, u32[]{:S(2)}) collective-permute-start(bf16[512,128]{1,0:T(8,128)(2,1)S(1)} %get-tuple-element.30.refs_0_), channel_id=1, source_target_pairs={{0,10},{2,8},{4,14},{6,12},{8,2},{10,0},{12,6},{14,4},{1,11},{3,9}... | collective-permute-start | bytes 393224 | tf_op jit(solution)/shard_map/ppermute | solution.py:366
  196.5 12.1 %collective-permute-start.25 = (bf16[512,128]{1,0:T(8,128)(2,1)S(1)}, bf16[512,128]{1,0:T(8,128)(2,1)S(1)}, u32[]{:S(2)}, u32[]{:S(2)}) collective-permute-start(bf16[512,128]{1,0:T(8,128)(2,1)S(1)} %get-tuple-element.30.refs_0_), channel_id=1, source_target_pairs={{0,12},{2,14},{4,8},{6,10},{8,4},{10,6},{12,0},{14,2},{1,13},{3,15... | collective-permute-start | bytes 393224 | tf_op jit(solution)/shard_map/ppermute | solution.py:366
  197.4 11.2 %collective-permute-start.26 = (bf16[512,128]{1,0:T(8,128)(2,1)S(1)}, bf16[512,128]{1,0:T(8,128)(2,1)S(1)}, u32[]{:S(2)}, u32[]{:S(2)}) collective-permute-start(bf16[512,128]{1,0:T(8,128)(2,1)S(1)} %get-tuple-element.30.refs_0_), channel_id=1, source_target_pairs={{0,14},{2,12},{4,10},{6,8},{8,6},{10,4},{12,2},{14,0},{1,15},{3,13... | collective-permute-start | bytes 393224 | tf_op jit(solution)/shard_map/ppermute | solution.py:366
  209.2 4.3 %collective-permute-start.27 = (bf16[256,1024]{1,0:T(8,128)(2,1)S(1)}, bf16[256,1024]{1,0:T(8,128)(2,1)S(1)}, u32[]{:S(2)}, u32[]{:S(2)}) collective-permute-start(bf16[256,1024]{1,0:T(8,128)(2,1)S(1)} %get-tuple-element.32.send_ref), channel_id=1, source_target_pairs={{0,16},{16,0},{32,48},{48,32},{64,80},{80,64},{96,112},{112,96},{1... | collective-permute-start | bytes 1572872 | tf_op jit(solution)/shard_map/ppermute | solution.py:357
  214.2 7.0 %collective-permute-start.29 = (bf16[64,1024]{1,0:T(8,128)(2,1)S(1)}, bf16[64,1024]{1,0:T(8,128)(2,1)S(1)}, u32[]{:S(2)}, u32[]{:S(2)}) collective-permute-start(bf16[64,1024]{1,0:T(8,128)(2,1)S(1)} %get-tuple-element.33), channel_id=1, source_target_pairs={{0,32},{16,48},{32,0},{48,16},{64,96},{80,112},{96,64},{112,80},{1... | collective-permute-start | bytes 393224 | tf_op jit(solution)/shard_map/ppermute | solution.py:361
  214.3 6.9 %collective-permute-start.30 = (bf16[64,1024]{1,0:T(8,128)(2,1)S(1)}, bf16[64,1024]{1,0:T(8,128)(2,1)S(1)}, u32[]{:S(2)}, u32[]{:S(2)}) collective-permute-start(bf16[64,1024]{1,0:T(8,128)(2,1)S(1)} %get-tuple-element.34), channel_id=1, source_target_pairs={{0,64},{16,80},{32,96},{48,112},{64,0},{80,16},{96,32},{112,48},{1... | collective-permute-start | bytes 393224 | tf_op jit(solution)/shard_map/ppermute | solution.py:361
  217.0 8.9 %collective-permute-start.31 = (bf16[64,1024]{1,0:T(8,128)(2,1)S(1)}, bf16[64,1024]{1,0:T(8,128)(2,1)S(1)}, u32[]{:S(2)}, u32[]{:S(2)}) collective-permute-start(bf16[64,1024]{1,0:T(8,128)(2,1)S(1)} %get-tuple-element.35), channel_id=1, source_target_pairs={{0,96},{16,112},{32,64},{48,80},{64,32},{80,48},{96,0},{112,16},{1... | collective-permute-start | bytes 393224 | tf_op jit(solution)/shard_map/ppermute | solution.py:361
  226.2 7.1 %collective-permute-start.32 = (bf16[64,1024]{1,0:T(8,128)(2,1)S(1)}, bf16[64,1024]{1,0:T(8,128)(2,1)S(1)}, u32[]{:S(2)}, u32[]{:S(2)}) collective-permute-start(bf16[64,1024]{1,0:T(8,128)(2,1)S(1)} %get-tuple-element.38), channel_id=1, source_target_pairs={{0,32},{16,48},{32,0},{48,16},{64,96},{80,112},{96,64},{112,80},{1... | collective-permute-start | bytes 393224 | tf_op jit(solution)/shard_map/ppermute | solution.py:361
  229.3 5.3 %collective-permute-start.33 = (bf16[64,1024]{1,0:T(8,128)(2,1)S(1)}, bf16[64,1024]{1,0:T(8,128)(2,1)S(1)}, u32[]{:S(2)}, u32[]{:S(2)}) collective-permute-start(bf16[64,1024]{1,0:T(8,128)(2,1)S(1)} %get-tuple-element.39), channel_id=1, source_target_pairs={{0,64},{16,80},{32,96},{48,112},{64,0},{80,16},{96,32},{112,48},{1... | collective-permute-start | bytes 393224 | tf_op jit(solution)/shard_map/ppermute | solution.py:361
  230.4 8.7 %collective-permute-start.34 = (bf16[64,1024]{1,0:T(8,128)(2,1)S(1)}, bf16[64,1024]{1,0:T(8,128)(2,1)S(1)}, u32[]{:S(2)}, u32[]{:S(2)}) collective-permute-start(bf16[64,1024]{1,0:T(8,128)(2,1)S(1)} %get-tuple-element.37), channel_id=1, source_target_pairs={{0,96},{16,112},{32,64},{48,80},{64,32},{80,48},{96,0},{112,16},{1... | collective-permute-start | bytes 393224 | tf_op jit(solution)/shard_map/ppermute | solution.py:361
  231.5 12.4 %collective-permute-start.28 = (bf16[256,1024]{1,0:T(8,128)(2,1)S(1)}, bf16[256,1024]{1,0:T(8,128)(2,1)S(1)}, u32[]{:S(2)}, u32[]{:S(2)}) collective-permute-start(bf16[256,1024]{1,0:T(8,128)(2,1)S(1)} %get-tuple-element.31.keep_ref), channel_id=1, source_target_pairs={{0,16},{16,0},{32,48},{48,32},{64,80},{80,64},{96,112},{112,96},{1... | collective-permute-start | bytes 1572872 | tf_op jit(solution)/shard_map/ppermute | solution.py:357
  239.8 5.7 %collective-permute-start.35 = (bf16[256,1024]{1,0:T(8,128)(2,1)S(1)}, bf16[256,1024]{1,0:T(8,128)(2,1)S(1)}, u32[]{:S(2)}, u32[]{:S(2)}) collective-permute-start(bf16[256,1024]{1,0:T(8,128)(2,1)S(1)} %arrange.3.own_ref), channel_id=1, source_target_pairs={{0,16},{16,0},{32,48},{48,32},{64,80},{80,64},{96,112},{112,96},{1... | collective-permute-start | bytes 1572872 | tf_op jit(solution)/shard_map/ppermute | solution.py:357
where the time goes:
time: 248 us
  blocking collectives  86.4 us (35%)
  waiting for transfers between devices  69.4 us (28%)
  starting transfers between devices  60 us (24%)
  Pallas kernels  28.5 us (11%)
    all_to_all x2, blocking collectives, over_tp(): return lax.all_to_all(value, 'tp', 0, 0, tiled=True)  86.4 us
    ppermute x16, waiting for transfers between devices, over_chips(): lax.ppermute(value, 'section', [(s, s ^ 2 * d) for s in range(2 * SPAN)])  44.5 us
    ppermute x16, starting transfers between devices, over_chips(): lax.ppermute(value, 'section', [(s, s ^ 2 * d) for s in range(2 * SPAN)])  27 us
    ppermute x14, starting transfers between devices, spread(): lax.ppermute(value, 'tp', [(t, t ^ d) for t in range(TP)])  18.5 us
    ppermute x14, waiting for transfers between devices, spread(): lax.ppermute(value, 'tp', [(t, t ^ d) for t in range(TP)])  18 us
    pallas_call x2, Pallas kernels, qkv(): pl.pallas_call(functools.partial(qkv_kernel, block, bool(pieces), len(aft...  17.1 us
    ppermute x6, starting transfers between devices, over_cores(): return lax.ppermute(value, 'section', [(s, s ^ 1) for s in range(2 * SPAN)])  14.6 us
    ppermute x6, waiting for transfers between devices, over_cores(): return lax.ppermute(value, 'section', [(s, s ^ 1) for s in range(2 * SPAN)])  6.9 us
  transfers between devices with their start and end apart: 36, of which 20 were waited for; matrix products, arithmetic and copies ran while one was open for 0% of the time, Pallas kernels for 0%

commit v1 on v0

v1 whole, which is shorter than its diff:
```python
import functools

import jax
import jax.numpy as jnp
from jax import lax
from jax.experimental import pallas as pl
from jax.experimental.pallas import tpu as pltpu
from jax.sharding import PartitionSpec as P

SPAN = 8
TP = 8
CHIPS = 4
EXTRA = 16
EPS = 1e-05
SEGMENT = 256
BF16 = jnp.bfloat16
F32 = jnp.float32
VMEM = pl.BlockSpec(memory_space=pltpu.VMEM)
SMEM = pl.BlockSpec(memory_space=pltpu.SMEM)
HBM = pl.BlockSpec(memory_space=pl.ANY)


def params(mib):
    return pltpu.CompilerParams(vmem_limit_bytes=mib * 1024 * 1024)


def segments_of(rows):
    size = min(rows, SEGMENT)
    return [(start, size) for start in range(0, rows, size)]


def split_parts(value, count):
    parts = []
    for _ in range(count):
        part = value.astype(BF16).astype(F32)
        parts.append(part)
        value = value - part
    return parts


def ending(head_line, offset_line, first, second, width):
    vectors = split_parts(head_line, 2) + split_parts(offset_line, 2)
    for line in (first, second):
        for start, size in segments_of(line.shape[1]):
            for part in split_parts(line[:, start : start + size], 3):
                vectors.append(jnp.concatenate([part, jnp.zeros((1, width - size), F32)], axis=1))
    row = lax.broadcasted_iota(jnp.int32, (EXTRA, width), 0)
    table = jnp.zeros((EXTRA, width), F32)
    for number, vector in enumerate(vectors):
        table = table + jnp.where(row == number, vector, 0.0)
    return table


def combine(pieces, features):
    rows, width = pieces[0].shape[0] - EXTRA, pieces[0].shape[1]
    segments = segments_of(rows)
    total = jnp.zeros((rows, width), F32)
    heads, firsts, offset, second = [], [], 0.0, 0.0
    for piece in pieces:
        total = total + piece[0:rows, :].astype(F32)
        ends = piece[rows : rows + EXTRA, :].astype(F32)
        heads.append(ends[0:1] + ends[1:2])
        offset = offset + (ends[2:3] + ends[3:4])
        lines = []
        for kind in range(2):
            spans = []
            for number, (_, size) in enumerate(segments):
                slot = 4 + (kind * len(segments) + number) * 3
                spans.append((ends[slot : slot + 1] + ends[slot + 1 : slot + 2] + ends[slot + 2 : slot + 3])[:, :size])
            lines.append(jnp.concatenate(spans, axis=1) if len(spans) > 1 else spans[0])
        firsts.append(lines[0])
        second = second + lines[1]
    first = sum(firsts)
    count = features * len(pieces)
    average = first * (1.0 / count)
    variance = second * (1.0 / count) - average * average
    scale = lax.rsqrt(jnp.maximum(variance, 0.0) + EPS)
    line_row = lax.broadcasted_iota(jnp.int32, (128, rows), 0)
    table = jnp.where(line_row == TP, scale, 0.0)
    head_row = lax.broadcasted_iota(jnp.int32, (128, width), 0)
    matrix = jnp.zeros((128, width), F32)
    for number in range(len(pieces)):
        table = jnp.where(line_row == number, firsts[number] * (1.0 / features) - average, table)
        matrix = jnp.where(head_row == number, heads[number], matrix)
    turned = table.T
    total = total + jnp.dot(
        turned, matrix, preferred_element_type=F32, precision=lax.Precision.HIGHEST
    )
    return total, turned[:, TP : TP + 1], offset


def cheap():
    return pl.CostEstimate(flops=1, bytes_accessed=1, transcendentals=0)


def stage_kernel(w_ref, x_ref, w_out, x_out, sems):
    copies = [
        pltpu.make_async_copy(w_ref, w_out, sems.at[0]),
        pltpu.make_async_copy(x_ref, x_out, sems.at[1]),
    ]
    for copy in copies:
        copy.start()
    for copy in copies:
        copy.wait()


def stage(w, x):
    return pl.pallas_call(
        stage_kernel,
        out_shape=[jax.ShapeDtypeStruct(w.shape, w.dtype), jax.ShapeDtypeStruct(x.shape, x.dtype)],
        in_specs=[HBM, HBM],
        out_specs=[HBM, HBM],
        scratch_shapes=[pltpu.SemaphoreType.DMA((2,))],
        compiler_params=params(4),
        cost_estimate=cheap(),
        name="stage",
    )(w, x)


def pick_kernel(place, own_ref, *refs):
    chip = place[2]
    out_ref = refs[-1]
    value = own_ref[...]
    for d in range(1, CHIPS):
        value = jnp.where(chip == d, refs[d - 1][...], value)
    out_ref[...] = value


def pick(place, own, received, after):
    return pl.pallas_call(
        pick_kernel,
        out_shape=jax.ShapeDtypeStruct(own.shape, own.dtype),
        in_specs=[SMEM] + [VMEM] * CHIPS + [HBM] * len(after),
        out_specs=VMEM,
        compiler_params=params(4),
        cost_estimate=cheap(),
        name="pick",
    )(place, own, *received, *after)


def qkv_kernel(layered, *refs):
    refs = list(refs)
    place, x_ref = refs.pop(0), refs.pop(0)
    pieces = [refs.pop(0) for _ in range(2)] if layered else []
    even_ref, odd_ref, w_ref = refs.pop(0), refs.pop(0), refs.pop(0)
    base_ref = refs.pop(0) if layered else None
    out_ref, lhs = refs
    core, layer = place[1], place[3]
    rows, columns = x_ref.shape
    width = w_ref.shape[2]

    vectors = jnp.where(core == 0, even_ref[...], odd_ref[...])
    gain, bias = vectors[0:1, :], vectors[1:2, :]
    row16 = lax.broadcasted_iota(jnp.int32, (EXTRA, columns), 0)
    tail = jnp.zeros((EXTRA, columns), F32)
    for number, vector in enumerate(split_parts(gain, 2) + split_parts(bias, 2)):
        tail = tail + jnp.where(row16 == number, vector, 0.0)
    lhs[rows : rows + EXTRA, :] = tail.astype(BF16)

    if layered:
        half_rows = rows // 2
        for half, piece in ((core, pieces[0]), (1 - core, pieces[1])):
            place_rows = pl.ds(pl.multiple_of(half * half_rows, half_rows), half_rows)
            tokens = x_ref[place_rows, :].astype(F32)
            added = tokens + piece[...].astype(F32)
            base_ref[place_rows, :] = jnp.where(layer == 1, added, tokens).astype(BF16)
    source = base_ref if layered else x_ref
    firsts, seconds = [], []
    for start, size in segments_of(rows):
        value = source[start : start + size, :].astype(F32)
        first = jnp.sum(value, axis=1, keepdims=True)
        second = jnp.sum(value * value, axis=1, keepdims=True)
        lhs[start : start + size, :] = ((value - first * (1.0 / columns)) * gain).astype(BF16)
        lane = lax.broadcasted_iota(jnp.int32, (size, 128), 1)
        turned = jnp.where(lane == 0, first, jnp.where(lane == 1, second, 0.0)).T
        firsts.append(turned[0:1, :])
        seconds.append(turned[1:2, :])
    blank = jnp.zeros((1, width), F32)
    joined = lambda lines: jnp.concatenate(lines, axis=1) if len(lines) > 1 else lines[0]
    lines = ending(blank, blank, joined(firsts), joined(seconds), width)
    out_row = lax.broadcasted_iota(jnp.int32, (EXTRA, width), 0)

    for pair in range(TP // 2):
        weights = jnp.concatenate([w_ref[2 * pair], w_ref[2 * pair + 1]], axis=1)
        result = jnp.dot(lhs[...], weights, preferred_element_type=F32)
        for side in range(2):
            head = 2 * pair + side
            part = result[:, side * width : (side + 1) * width]
            ends = part[rows : rows + EXTRA, :]
            table = lines
            vectors = split_parts(ends[0:1] + ends[1:2], 2) + split_parts(ends[2:3] + ends[3:4], 2)
            for number, vector in enumerate(vectors):
                table = table + jnp.where(out_row == number, vector, 0.0)
            out_ref[head, 0:rows, :] = part[0:rows, :].astype(BF16)
            out_ref[head, rows : rows + EXTRA, :] = table.astype(BF16)


def qkv(place, x, pieces, even, odd, w):
    rows, columns = x.shape
    heads, _, width = w.shape
    shapes = [jax.ShapeDtypeStruct((heads, rows + EXTRA, width), BF16)]
    if pieces:
        shapes = [jax.ShapeDtypeStruct((rows, columns), BF16)] + shapes
    out = pl.pallas_call(
        functools.partial(qkv_kernel, bool(pieces)),
        out_shape=shapes,
        in_specs=[SMEM] + [VMEM] * (len(pieces) + 4),
        out_specs=[VMEM] * len(shapes),
        scratch_shapes=[pltpu.VMEM((rows + EXTRA, columns), BF16)],
        compiler_params=params(24),
        cost_estimate=cheap(),
        name="qkv",
    )(place, x, *pieces, even, odd, w)
    return out if pieces else (None, out[0])


def attention_kernel(features, pieces_ref, out_ref):
    rows, head_dim = out_ref.shape
    total, scale, offset = combine([pieces_ref.at[t] for t in range(TP)], features // TP)
    joined = (total * scale + offset).astype(BF16)
    query = joined[:, :head_dim]
    key = joined[:, head_dim : 2 * head_dim]
    value = joined[:, 2 * head_dim :]
    scores = lax.dot_general(
        query, key, (((1,), (1,)), ((), ())), preferred_element_type=F32
    ) * (1.0 / head_dim**0.5)
    at_query = lax.broadcasted_iota(jnp.int32, (rows, rows), 0)
    at_key = lax.broadcasted_iota(jnp.int32, (rows, rows), 1)
    scores = jnp.where(at_key <= at_query, scores, -1e30)
    highest = jnp.max(scores, axis=1, keepdims=True)
    lifted = jnp.exp(scores - highest)
    weights = (lifted * (1.0 / jnp.sum(lifted, axis=1, keepdims=True))).astype(BF16)
    out_ref[...] = jnp.dot(weights, value, preferred_element_type=F32).astype(BF16)


def attention(pieces, features):
    rows = pieces.shape[1] - EXTRA
    head_dim = pieces.shape[2] // 3
    return pl.pallas_call(
        functools.partial(attention_kernel, features),
        out_shape=jax.ShapeDtypeStruct((rows, head_dim), BF16),
        in_specs=[VMEM],
        out_specs=VMEM,
        compiler_params=params(24),
        cost_estimate=cheap(),
        name="attention",
    )(pieces)


def project_kernel(passing, place, *refs):
    refs = list(refs)
    pieces = [refs.pop(0) for _ in range(TP)]
    w_ref = refs.pop(0)
    old = [refs.pop(0) for _ in range(2)] if passing else None
    keep_ref, send_ref, side = refs
    me, core, layer = place[0], place[1], place[3]
    rows, head_dim = pieces[0].shape

    def work():
        for d in range(TP):
            start = pl.multiple_of(jnp.bitwise_xor(me, d) * head_dim, head_dim)
            side[:, pl.ds(start, head_dim)] = pieces[d][...]
        for half, target in ((1 - core, send_ref), (core, keep_ref)):
            place_rows = pl.ds(pl.multiple_of(half * (rows // 2), rows // 2), rows // 2)
            target[...] = jnp.dot(
                side[place_rows, :], w_ref[...], preferred_element_type=F32
            ).astype(BF16)

    if passing:
        pl.when(layer == 1)(work)

        @pl.when(layer == 0)
        def _():
            keep_ref[...] = old[0][...]
            send_ref[...] = old[1][...]
    else:
        work()


def project(place, pieces, w, old):
    rows, head_dim = pieces[0].shape
    columns = w.shape[1]
    shape = jax.ShapeDtypeStruct((rows // 2, columns), BF16)
    old = list(old) if old else []
    return pl.pallas_call(
        functools.partial(project_kernel, bool(old)),
        out_shape=[shape] * 2,
        in_specs=[SMEM] + [VMEM] * (TP + 1 + len(old)),
        out_specs=[VMEM] * 2,
        scratch_shapes=[pltpu.VMEM((rows, TP * head_dim), BF16)],
        compiler_params=params(24),
        cost_estimate=cheap(),
        name="project",
    )(place, *pieces, w, *old)


def quarters_kernel(place, keep_ref, got_ref, *outs):
    chip = place[2]
    size = outs[0].shape[0]
    for d in range(CHIPS):
        rows = pl.ds(pl.multiple_of(jnp.bitwise_xor(chip, d) * size, size), size)
        outs[d][...] = (keep_ref[rows, :].astype(F32) + got_ref[rows, :].astype(F32)).astype(BF16)


def quarters(place, keep, got):
    rows, columns = keep.shape
    return pl.pallas_call(
        quarters_kernel,
        out_shape=[jax.ShapeDtypeStruct((rows // CHIPS, columns), BF16)] * CHIPS,
        in_specs=[SMEM, VMEM, VMEM],
        out_specs=[VMEM] * CHIPS,
        compiler_params=params(16),
        cost_estimate=cheap(),
        name="quarters",
    )(place, keep, got)


def arrange_kernel(place, *refs):
    chip = place[2]
    out_ref = refs[CHIPS]
    size = out_ref.shape[0] // CHIPS
    for d in range(CHIPS):
        rows = pl.ds(pl.multiple_of(jnp.bitwise_xor(chip, d) * size, size), size)
        out_ref[rows, :] = refs[d][...]


def arrange(place, pieces):
    rows, columns = pieces[0].shape
    return pl.pallas_call(
        arrange_kernel,
        out_shape=jax.ShapeDtypeStruct((rows * CHIPS, columns), BF16),
        in_specs=[SMEM] + [VMEM] * CHIPS,
        out_specs=VMEM,
        compiler_params=params(16),
        cost_estimate=cheap(),
        name="arrange",
    )(place, *pieces)


def finish_kernel(place, base_ref, keep_ref, got_ref, send_ref, other_keep_ref, own_ref, other_ref, out_ref):
    core = place[1]
    half_rows = keep_ref.shape[0]
    second = core.astype(F32)
    for half, sums, mine, theirs in (
        (core, own_ref, keep_ref, got_ref),
        (1 - core, other_ref, send_ref, other_keep_ref),
    ):
        rows = pl.ds(pl.multiple_of(half * half_rows, half_rows), half_rows)
        out_ref[rows, :] = (
            base_ref[rows, :].astype(F32)
            + sums[...].astype(F32)
            + mine[...].astype(F32)
            + second * theirs[...].astype(F32)
        ).astype(BF16)


def finish(place, base, *values):
    return pl.pallas_call(
        finish_kernel,
        out_shape=jax.ShapeDtypeStruct(base.shape, BF16),
        in_specs=[SMEM] + [VMEM] * (1 + len(values)),
        out_specs=VMEM,
        compiler_params=params(24),
        cost_estimate=cheap(),
        name="finish",
    )(place, base, *values)


def over_tp(value):
    return lax.all_to_all(value, "tp", 0, 0, tiled=True)


def over_cores(value):
    return lax.ppermute(value, "section", [(s, s ^ 1) for s in range(2 * SPAN)])


def over_chips(value, d):
    return lax.ppermute(value, "section", [(s, s ^ (2 * d)) for s in range(2 * SPAN)])


def spread(value):
    got = {0: value}
    for d in (5, 7, 3, 1, 4, 6, 2):
        got[d] = lax.ppermute(value, "tp", [(t, t ^ d) for t in range(TP)])
    return [got[d] for d in range(TP)]


def over_layer(values):
    return [values[0]] + [over_chips(values[d], d) for d in range(1, CHIPS)]


def on_device(tokens, ln_gain, ln_bias, w_qkv, w_out):
    section = lax.axis_index("section")
    me = lax.axis_index("tp")
    core = section % 2
    chip = (section // 2) % CHIPS
    layer = section // SPAN
    place = jnp.stack([me, core, chip, layer]).astype(jnp.int32)
    weight_in = w_qkv[0]
    weight_back = w_out[0]
    features = tokens.shape[1] * TP

    vectors = jnp.concatenate([ln_gain, ln_bias], axis=0)
    weight_in, tokens = stage(weight_in, tokens)
    received = [over_chips(vectors, d) for d in range(1, CHIPS)]
    even = pick(place, vectors, received, [weight_in])
    odd = over_cores(even)

    _, part = qkv(place, tokens, [], even, odd, weight_in)
    out = attention(over_tp(part), features)
    kept = project(place, spread(out), weight_back, None)
    keep, send = kept
    quarter = quarters(place, keep, over_cores(send))
    total = sum(value.astype(F32) for value in over_layer(quarter)).astype(BF16)
    half = arrange(place, over_layer([over_chips(total, CHIPS)] * CHIPS))

    base, part = qkv(place, tokens, [half, over_cores(half)], even, odd, weight_in)
    out = attention(over_tp(part), features)
    keep, send = project(place, spread(out), weight_back, kept)
    got = over_cores(send)
    other_keep = over_cores(keep)
    arrived = over_layer(quarters(place, keep, got))
    before = []
    for d in range(CHIPS):
        target = jnp.bitwise_xor(chip, d)
        before.append(
            sum(
                jnp.where(jnp.bitwise_xor(chip, e) < target, arrived[e].astype(F32), 0.0)
                for e in range(CHIPS)
            ).astype(BF16)
        )
    own = arrange(place, over_layer(before))
    return finish(place, base, keep, got, send, other_keep, own, over_cores(own))[None]


def solution(mesh):
    return jax.shard_map(
        on_device,
        mesh=mesh,
        in_specs=(
            P("dp", "tp"),
            P("section", "tp"),
            P("section", "tp"),
            P("section", None, "tp", None),
            P("section", None, "tp"),
        ),
        out_specs=P("section", "dp", "tp"),
        check_vma=False,
    )
```

time: 248 us -> 238 us (0.960)
  waiting for transfers between devices: 69.4 us -> 55.9 us
  starting transfers between devices: 60 us -> 69.2 us
  Pallas kernels: 28.5 us -> 22 us
  local copies, waits for them, and re-layouts: 1.24 us -> 4.01 us
    ppermute x16, waiting for transfers between devices: 44.5 us -> 34.5 us  [over_chips(): lax.ppermute(value, 'section', [(s, s ^ 2 * d) for s in range(2 * SPAN)])]
    pallas_call x8 -> x10, Pallas kernels: 25 us -> 18.6 us  [the longest x2 9.63 us: qkv(): pl.pallas_call(functools.partial(qkv_kernel, bool(pieces)), out_shape=sha...]
    ppermute x6, starting transfers between devices: 14.6 us -> 20.4 us  [over_cores(): return lax.ppermute(value, 'section', [(s, s ^ 1) for s in range(2 * SPAN)])]
    ppermute x14, waiting for transfers between devices: 18 us -> 14.5 us  [spread(): got[d] = lax.ppermute(value, 'tp', [(t, t ^ d) for t in range(TP)])]
    ppermute x16, starting transfers between devices: 27 us -> 30.5 us  [over_chips(): lax.ppermute(value, 'section', [(s, s ^ 2 * d) for s in range(2 * SPAN)])]
    unnamed x6, local copies, waits for them, and re-layouts: 1.23 us -> 4.01 us
where the time goes in v1:
time: 238 us
  blocking collectives  85.2 us (36%)
  starting transfers between devices  69.2 us (29%)
  waiting for transfers between devices  55.9 us (23%)
  Pallas kernels  22 us (9%)
  local copies, waits for them, and re-layouts  4.01 us (2%)
    all_to_all x2, blocking collectives, over_tp(): return lax.all_to_all(value, 'tp', 0, 0, tiled=True)  85.2 us
    ppermute x16, waiting for transfers between devices, over_chips(): lax.ppermute(value, 'section', [(s, s ^ 2 * d) for s in range(2 * SPAN)])  34.5 us
    ppermute x16, starting transfers between devices, over_chips(): lax.ppermute(value, 'section', [(s, s ^ 2 * d) for s in range(2 * SPAN)])  30.5 us
    ppermute x6, starting transfers between devices, over_cores(): return lax.ppermute(value, 'section', [(s, s ^ 1) for s in range(2 * SPAN)])  20.4 us
    ppermute x14, starting transfers between devices, spread(): got[d] = lax.ppermute(value, 'tp', [(t, t ^ d) for t in range(TP)])  18.3 us
    ppermute x14, waiting for transfers between devices, spread(): got[d] = lax.ppermute(value, 'tp', [(t, t ^ d) for t in range(TP)])  14.5 us
    pallas_call x2, Pallas kernels, qkv(): pl.pallas_call(functools.partial(qkv_kernel, bool(pieces)), out_shape=sha...  9.63 us
    ppermute x6, waiting for transfers between devices, over_cores(): return lax.ppermute(value, 'section', [(s, s ^ 1) for s in range(2 * SPAN)])  6.98 us
  transfers between devices with their start and end apart: 36, of which 20 were waited for; matrix products, arithmetic and copies ran while one was open for 0% of the time, Pallas kernels for 0%

profile of v1, /device:TPU:1, one launch (start us, length us, event | category | flops | bytes accessed | tf_op | source)
XLA Modules:
  0.0 237.6 jit_solution(14471176527288764871)
XLA Ops:
  0.0 0.7 pad_maximum_fusion.own_ref
  0.7 2.6 %collective-permute-start = (f32[2,1024]{1,0:T(2,128)S(1)}, f32[2,1024]{1,0:T(2,128)S(1)}, u32[]{:S(2)}, u32[]{:S(2)}) collective-permute-start(f32[2,1024]{1,0:T(2,128)S(1)} %pad_maximum_fusion.own_ref), channel_id=1, source_target_pairs={{0,32},{16,48},{32,0},{48,16},{64,96},{80,112},{96,64},{112,80},{1... | collective-permute-start | bytes 24584 | tf_op jit(solution)/shard_map/ppermute | solution.py:378
  3.3 3.0 %collective-permute-start.1 = (f32[2,1024]{1,0:T(2,128)S(1)}, f32[2,1024]{1,0:T(2,128)S(1)}, u32[]{:S(2)}, u32[]{:S(2)}) collective-permute-start(f32[2,1024]{1,0:T(2,128)S(1)} %pad_maximum_fusion.own_ref), channel_id=1, source_target_pairs={{0,64},{16,80},{32,96},{48,112},{64,0},{80,16},{96,32},{112,48},{1... | collective-permute-start | bytes 24584 | tf_op jit(solution)/shard_map/ppermute | solution.py:378
  6.3 2.8 %copy-done.1 = bf16[1,8,1024,384]{3,2,1,0:T(8,128)(2,1)S(1)} copy-done((bf16[1,8,1024,384]{3,2,1,0:T(8,128)(2,1)S(1)}, bf16[1,8,1024,384]{3,2,1,0:T(8,128)(2,1)}, u32[]{:S(2)}) %copy-start.1) | copy-done | bytes 6291480
  9.1 1.2 copy-done.2
  11.5 2.3 collective-permute-start.3
  13.7 0.8 collective-permute-done.3.refs_3_.refs_5_
  14.5 4.5 %qkv.2 = bf16[8,528,384]{2,1,0:T(8,128)(2,1)S(1)} custom-call(s32[4]{0:T(128)S(1)} %pad_add_fusion.place.refs_0_, bf16[512,1024]{1,0:T(8,128)(2,1)S(1)} %get-tuple-element.21.refs_1_, f32[2,1024]{1,0:T(2,128)S(1)} %pick.1.refs_2_.refs_4_, f32[2,1024]{1,0:T(2,128)S(1)} %collective-permute-done.3.refs_3_.refs_5_, ...), custom_call_target="tpu_custom_call" | custom-call | flops 1 | bytes 1 | tf_op jit(solution)/shard_map/qkv/pallas_call | solution.py:204
  19.0 43.5 %all_to_all.10.pieces_ref = bf16[8,528,384]{2,1,0:T(8,128)(2,1)S(1)} all-to-all(bf16[8,528,384]{2,1,0:T(8,128)(2,1)S(1)} %qkv.2), channel_id=1, replica_groups=mesh['section'=16,'tp'=8,'dp'=2] {'tp'}, dimensions={0} | all-to-all | bytes 6488064 | tf_op jit(solution)/shard_map/all_to_all | solution.py:370
  62.5 2.0 attention.2.refs_0_
  64.5 1.7 collective-permute-start.10
  66.4 2.4 %collective-permute-start.6 = (bf16[512,128]{1,0:T(8,128)(2,1)S(1)}, bf16[512,128]{1,0:T(8,128)(2,1)S(1)}, u32[]{:S(2)}, u32[]{:S(2)}) collective-permute-start(bf16[512,128]{1,0:T(8,128)(2,1)S(1)} %attention.2.refs_0_), channel_id=1, source_target_pairs={{0,6},{2,4},{4,2},{6,0},{8,14},{10,12},{12,10},{14,8},{1,7},{3,5},... | collective-permute-start | bytes 393224 | tf_op jit(solution)/shard_map/ppermute | solution.py:384
  68.8 1.4 collective-permute-start.7
  70.5 1.2 collective-permute-start.8
  71.8 2.0 collective-permute-start.9
  73.8 5.2 %collective-permute-done.7.refs_4_ = bf16[512,128]{1,0:T(8,128)(2,1)S(1)} collective-permute-done((bf16[512,128]{1,0:T(8,128)(2,1)S(1)}, bf16[512,128]{1,0:T(8,128)(2,1)S(1)}, u32[]{:S(2)}, u32[]{:S(2)}) %collective-permute-start.7) | collective-permute-done | bytes 131104 | tf_op jit(solution)/shard_map/ppermute | solution.py:384
  79.0 2.1 project.2
  81.1 5.4 %collective-permute-start.11 = (bf16[256,1024]{1,0:T(8,128)(2,1)S(1)}, bf16[256,1024]{1,0:T(8,128)(2,1)S(1)}, u32[]{:S(2)}, u32[]{:S(2)}) collective-permute-start(bf16[256,1024]{1,0:T(8,128)(2,1)S(1)} %get-tuple-element.24.refs_10_), channel_id=1, source_target_pairs={{0,16},{16,0},{32,48},{48,32},{64,80},{80,64},{96,112},{112,96},{1... | collective-permute-start | bytes 1572872 | tf_op jit(solution)/shard_map/ppermute | solution.py:374
  86.5 1.5 collective-permute-done.11.got_ref
  88.0 0.7 quarters.2
  88.8 3.0 %collective-permute-start.13 = (bf16[64,1024]{1,0:T(8,128)(2,1)S(1)}, bf16[64,1024]{1,0:T(8,128)(2,1)S(1)}, u32[]{:S(2)}, u32[]{:S(2)}) collective-permute-start(bf16[64,1024]{1,0:T(8,128)(2,1)S(1)} %get-tuple-element.27), channel_id=1, source_target_pairs={{0,64},{16,80},{32,96},{48,112},{64,0},{80,16},{96,32},{112,48},{1... | collective-permute-start | bytes 393224 | tf_op jit(solution)/shard_map/ppermute | solution.py:378
  92.3 3.3 %collective-permute-done.12 = bf16[64,1024]{1,0:T(8,128)(2,1)S(1)} collective-permute-done((bf16[64,1024]{1,0:T(8,128)(2,1)S(1)}, bf16[64,1024]{1,0:T(8,128)(2,1)S(1)}, u32[]{:S(2)}, u32[]{:S(2)}) %collective-permute-start.12) | collective-permute-done | bytes 131104 | tf_op jit(solution)/shard_map/ppermute | solution.py:378
  95.6 5.1 %collective-permute-done.14 = bf16[64,1024]{1,0:T(8,128)(2,1)S(1)} collective-permute-done((bf16[64,1024]{1,0:T(8,128)(2,1)S(1)}, bf16[64,1024]{1,0:T(8,128)(2,1)S(1)}, u32[]{:S(2)}, u32[]{:S(2)}) %collective-permute-start.14) | collective-permute-done | bytes 131104 | tf_op jit(solution)/shard_map/ppermute | solution.py:378
  100.8 4.2 %collective-permute-start.15 = (bf16[64,1024]{1,0:T(8,128)(2,1)S(1)}, bf16[64,1024]{1,0:T(8,128)(2,1)S(1)}, u32[]{:S(2)}, u32[]{:S(2)}) collective-permute-start(bf16[64,1024]{1,0:T(8,128)(2,1)S(1)} %add_convert_fusion), channel_id=1, source_target_pairs={{0,128},{16,144},{32,160},{48,176},{64,192},{80,208},{96,224},{112... | collective-permute-start | bytes 393224 | tf_op jit(solution)/shard_map/ppermute | solution.py:378
  105.0 3.6 %collective-permute-done.15.refs_0_ = bf16[64,1024]{1,0:T(8,128)(2,1)S(1)} collective-permute-done((bf16[64,1024]{1,0:T(8,128)(2,1)S(1)}, bf16[64,1024]{1,0:T(8,128)(2,1)S(1)}, u32[]{:S(2)}, u32[]{:S(2)}) %collective-permute-start.15) | collective-permute-done | bytes 131104 | tf_op jit(solution)/shard_map/ppermute | solution.py:378
  108.6 5.4 %collective-permute-start.16 = (bf16[64,1024]{1,0:T(8,128)(2,1)S(1)}, bf16[64,1024]{1,0:T(8,128)(2,1)S(1)}, u32[]{:S(2)}, u32[]{:S(2)}) collective-permute-start(bf16[64,1024]{1,0:T(8,128)(2,1)S(1)} %collective-permute-done.15.refs_0_), channel_id=1, source_target_pairs={{0,32},{16,48},{32,0},{48,16},{64,96},{80,112},{96,64},{112,80},{1... | collective-permute-start | bytes 393224 | tf_op jit(solution)/shard_map/ppermute | solution.py:378
  114.1 1.1 collective-permute-start.17
  115.2 1.2 collective-permute-start.18
  116.4 2.7 %collective-permute-done.17.refs_2_ = bf16[64,1024]{1,0:T(8,128)(2,1)S(1)} collective-permute-done((bf16[64,1024]{1,0:T(8,128)(2,1)S(1)}, bf16[64,1024]{1,0:T(8,128)(2,1)S(1)}, u32[]{:S(2)}, u32[]{:S(2)}) %collective-permute-start.17) | collective-permute-done | bytes 131104 | tf_op jit(solution)/shard_map/ppermute | solution.py:378
  119.1 5.1 %collective-permute-done.18.refs_3_ = bf16[64,1024]{1,0:T(8,128)(2,1)S(1)} collective-permute-done((bf16[64,1024]{1,0:T(8,128)(2,1)S(1)}, bf16[64,1024]{1,0:T(8,128)(2,1)S(1)}, u32[]{:S(2)}, u32[]{:S(2)}) %collective-permute-start.18) | collective-permute-done | bytes 131104 | tf_op jit(solution)/shard_map/ppermute | solution.py:378
  124.2 0.6 arrange.2.refs_2_
  124.8 3.9 %collective-permute-start.19 = (bf16[256,1024]{1,0:T(8,128)(2,1)S(1)}, bf16[256,1024]{1,0:T(8,128)(2,1)S(1)}, u32[]{:S(2)}, u32[]{:S(2)}) collective-permute-start(bf16[256,1024]{1,0:T(8,128)(2,1)S(1)} %arrange.2.refs_2_), channel_id=1, source_target_pairs={{0,16},{16,0},{32,48},{48,32},{64,80},{80,64},{96,112},{112,96},{1... | collective-permute-start | bytes 1572872 | tf_op jit(solution)/shard_map/ppermute | solution.py:374
  128.6 1.5 collective-permute-done.19.refs_3_
  130.2 5.2 %qkv.3 = (bf16[512,1024]{1,0:T(8,128)(2,1)S(1)}, bf16[8,528,384]{2,1,0:T(8,128)(2,1)S(1)}) custom-call(s32[4]{0:T(128)S(1)} %pad_add_fusion.place.refs_0_, bf16[512,1024]{1,0:T(8,128)(2,1)S(1)} %get-tuple-element.21.refs_1_, bf16[256,1024]{1,0:T(8,128)(2,1)S(1)} %arrange.2.refs_2_, bf16[256,1024]{1,0:T(8,128)(2,1)S(1)} %collective-permute-done.19.refs_3_, ...), custom_call_target="tpu_custom_call" | custom-call | flops 1 | bytes 1 | tf_op jit(solution)/shard_map/qkv/pallas_call | solution.py:204
  135.3 41.7 %all_to_all.11.pieces_ref = bf16[8,528,384]{2,1,0:T(8,128)(2,1)S(1)} all-to-all(bf16[8,528,384]{2,1,0:T(8,128)(2,1)S(1)} %get-tuple-element.30), channel_id=1, replica_groups=mesh['section'=16,'tp'=8,'dp'=2] {'tp'}, dimensions={0} | all-to-all | bytes 6488064 | tf_op jit(solution)/shard_map/all_to_all | solution.py:370
  177.0 2.0 attention.3.refs_0_
  179.1 1.1 collective-permute-start.20
  180.4 1.4 collective-permute-start.22
  181.8 0.9 collective-permute-start.23
  182.7 2.7 %collective-permute-start.24 = (bf16[512,128]{1,0:T(8,128)(2,1)S(1)}, bf16[512,128]{1,0:T(8,128)(2,1)S(1)}, u32[]{:S(2)}, u32[]{:S(2)}) collective-permute-start(bf16[512,128]{1,0:T(8,128)(2,1)S(1)} %attention.3.refs_0_), channel_id=1, source_target_pairs={{0,10},{2,8},{4,14},{6,12},{8,2},{10,0},{12,6},{14,4},{1,11},{3,9}... | collective-permute-start | bytes 393224 | tf_op jit(solution)/shard_map/ppermute | solution.py:384
  185.5 0.9 collective-permute-start.25
  186.4 2.0 collective-permute-start.26
  188.4 6.0 %collective-permute-done.23.refs_4_ = bf16[512,128]{1,0:T(8,128)(2,1)S(1)} collective-permute-done((bf16[512,128]{1,0:T(8,128)(2,1)S(1)}, bf16[512,128]{1,0:T(8,128)(2,1)S(1)}, u32[]{:S(2)}, u32[]{:S(2)}) %collective-permute-start.23) | collective-permute-done | bytes 131104 | tf_op jit(solution)/shard_map/ppermute | solution.py:384
  194.4 3.0 %collective-permute-done.25.refs_6_ = bf16[512,128]{1,0:T(8,128)(2,1)S(1)} collective-permute-done((bf16[512,128]{1,0:T(8,128)(2,1)S(1)}, bf16[512,128]{1,0:T(8,128)(2,1)S(1)}, u32[]{:S(2)}, u32[]{:S(2)}) %collective-permute-start.25) | collective-permute-done | bytes 131104 | tf_op jit(solution)/shard_map/ppermute | solution.py:384
  197.4 0.6 project.3
  198.0 2.9 %collective-permute-start.27 = (bf16[256,1024]{1,0:T(8,128)(2,1)S(1)}, bf16[256,1024]{1,0:T(8,128)(2,1)S(1)}, u32[]{:S(2)}, u32[]{:S(2)}) collective-permute-start(bf16[256,1024]{1,0:T(8,128)(2,1)S(1)} %get-tuple-element.32.send_ref), channel_id=1, source_target_pairs={{0,16},{16,0},{32,48},{48,32},{64,80},{80,64},{96,112},{112,96},{1... | collective-permute-start | bytes 1572872 | tf_op jit(solution)/shard_map/ppermute | solution.py:374
  201.0 1.5 collective-permute-done.27.got_ref
  202.5 0.7 quarters.3
  203.2 1.8 collective-permute-start.29
  204.9 1.1 collective-permute-start.30
  206.1 1.1 collective-permute-start.31
  207.2 1.3 collective-permute-done.29
  208.5 1.9 collective-permute-done.30
  210.3 5.7 %collective-permute-done.31 = bf16[64,1024]{1,0:T(8,128)(2,1)S(1)} collective-permute-done((bf16[64,1024]{1,0:T(8,128)(2,1)S(1)}, bf16[64,1024]{1,0:T(8,128)(2,1)S(1)}, u32[]{:S(2)}, u32[]{:S(2)}) %collective-permute-start.31) | collective-permute-done | bytes 131104 | tf_op jit(solution)/shard_map/ppermute | solution.py:378
  216.3 3.0 %collective-permute-start.32 = (bf16[64,1024]{1,0:T(8,128)(2,1)S(1)}, bf16[64,1024]{1,0:T(8,128)(2,1)S(1)}, u32[]{:S(2)}, u32[]{:S(2)}) collective-permute-start(bf16[64,1024]{1,0:T(8,128)(2,1)S(1)} %get-tuple-element.38), channel_id=1, source_target_pairs={{0,32},{16,48},{32,0},{48,16},{64,96},{80,112},{96,64},{112,80},{1... | collective-permute-start | bytes 393224 | tf_op jit(solution)/shard_map/ppermute | solution.py:378
  219.4 1.3 collective-permute-start.33
  220.6 1.1 collective-permute-start.34
  221.7 1.9 collective-permute-start.28
  223.6 0.6 collective-permute-done.33.refs_2_
  224.2 5.1 %collective-permute-done.34.refs_3_ = bf16[64,1024]{1,0:T(8,128)(2,1)S(1)} collective-permute-done((bf16[64,1024]{1,0:T(8,128)(2,1)S(1)}, bf16[64,1024]{1,0:T(8,128)(2,1)S(1)}, u32[]{:S(2)}, u32[]{:S(2)}) %collective-permute-start.34) | collective-permute-done | bytes 131104 | tf_op jit(solution)/shard_map/ppermute | solution.py:378
  229.2 0.6 arrange.3.own_ref
  229.8 4.1 %collective-permute-start.35 = (bf16[256,1024]{1,0:T(8,128)(2,1)S(1)}, bf16[256,1024]{1,0:T(8,128)(2,1)S(1)}, u32[]{:S(2)}, u32[]{:S(2)}) collective-permute-start(bf16[256,1024]{1,0:T(8,128)(2,1)S(1)} %arrange.3.own_ref), channel_id=1, source_target_pairs={{0,16},{16,0},{32,48},{48,32},{64,80},{80,64},{96,112},{112,96},{1... | collective-permute-start | bytes 1572872 | tf_op jit(solution)/shard_map/ppermute | solution.py:374
  233.9 1.5 collective-permute-done.35.other_ref
  235.5 2.1 finish.1
  (33 shorter events, 2.9 us)
Async XLA Ops:
  0.7 10.2 %collective-permute-start = (f32[2,1024]{1,0:T(2,128)S(1)}, f32[2,1024]{1,0:T(2,128)S(1)}, u32[]{:S(2)}, u32[]{:S(2)}) collective-permute-start(f32[2,1024]{1,0:T(2,128)S(1)} %pad_maximum_fusion.own_ref), channel_id=1, source_target_pairs={{0,32},{16,48},{32,0},{48,16},{64,96},{80,112},{96,64},{112,80},{1... | collective-permute-start | bytes 24584 | tf_op jit(solution)/shard_map/ppermute | solution.py:378
  3.3 7.6 %collective-permute-start.1 = (f32[2,1024]{1,0:T(2,128)S(1)}, f32[2,1024]{1,0:T(2,128)S(1)}, u32[]{:S(2)}, u32[]{:S(2)}) collective-permute-start(f32[2,1024]{1,0:T(2,128)S(1)} %pad_maximum_fusion.own_ref), channel_id=1, source_target_pairs={{0,64},{16,80},{32,96},{48,112},{64,0},{80,16},{96,32},{112,48},{1... | collective-permute-start | bytes 24584 | tf_op jit(solution)/shard_map/ppermute | solution.py:378
  6.3 4.6 %collective-permute-start.2 = (f32[2,1024]{1,0:T(2,128)S(1)}, f32[2,1024]{1,0:T(2,128)S(1)}, u32[]{:S(2)}, u32[]{:S(2)}) collective-permute-start(f32[2,1024]{1,0:T(2,128)S(1)} %pad_maximum_fusion.own_ref), channel_id=1, source_target_pairs={{0,96},{16,112},{32,64},{48,80},{64,32},{80,48},{96,0},{112,16},{1... | collective-permute-start | bytes 24584 | tf_op jit(solution)/shard_map/ppermute | solution.py:378
  6.3 2.8 %copy-start.1 = (bf16[1,8,1024,384]{3,2,1,0:T(8,128)(2,1)S(1)}, bf16[1,8,1024,384]{3,2,1,0:T(8,128)(2,1)}, u32[]{:S(2)}) copy-start(bf16[1,8,1024,384]{3,2,1,0:T(8,128)(2,1)} %param.8) | copy-start | bytes 18874372
  9.1 1.2 copy-start.2
  11.5 3.1 %collective-permute-start.3 = (f32[2,1024]{1,0:T(2,128)S(1)}, f32[2,1024]{1,0:T(2,128)S(1)}, u32[]{:S(2)}, u32[]{:S(2)}) collective-permute-start(f32[2,1024]{1,0:T(2,128)S(1)} %pick.1.refs_2_.refs_4_), channel_id=1, source_target_pairs={{0,16},{16,0},{32,48},{48,32},{64,80},{80,64},{96,112},{112,96},{1... | collective-permute-start | bytes 24584 | tf_op jit(solution)/shard_map/ppermute | solution.py:374
  62.5 16.5 %copy-start = (bf16[1,1024,1024]{2,1,0:T(8,128)(2,1)S(1)}, bf16[1,1024,1024]{2,1,0:T(8,128)(2,1)}, u32[]{:S(2)}) copy-start(bf16[1,1024,1024]{2,1,0:T(8,128)(2,1)} %param.9) | copy-start | bytes 6291460
  64.5 6.0 %collective-permute-start.10 = (bf16[512,128]{1,0:T(8,128)(2,1)S(1)}, bf16[512,128]{1,0:T(8,128)(2,1)S(1)}, u32[]{:S(2)}, u32[]{:S(2)}) collective-permute-start(bf16[512,128]{1,0:T(8,128)(2,1)S(1)} %attention.2.refs_0_), channel_id=1, source_target_pairs={{0,14},{2,12},{4,10},{6,8},{8,6},{10,4},{12,2},{14,0},{1,15},{3,13... | collective-permute-start | bytes 393224 | tf_op jit(solution)/shard_map/ppermute | solution.py:384
  66.2 5.6 %collective-permute-start.4 = (bf16[512,128]{1,0:T(8,128)(2,1)S(1)}, bf16[512,128]{1,0:T(8,128)(2,1)S(1)}, u32[]{:S(2)}, u32[]{:S(2)}) collective-permute-start(bf16[512,128]{1,0:T(8,128)(2,1)S(1)} %attention.2.refs_0_), channel_id=1, source_target_pairs={{0,2},{2,0},{4,6},{6,4},{8,10},{10,8},{12,14},{14,12},{1,3},{3,1},... | collective-permute-start | bytes 393224 | tf_op jit(solution)/shard_map/ppermute | solution.py:384
  66.4 7.4 %collective-permute-start.5 = (bf16[512,128]{1,0:T(8,128)(2,1)S(1)}, bf16[512,128]{1,0:T(8,128)(2,1)S(1)}, u32[]{:S(2)}, u32[]{:S(2)}) collective-permute-start(bf16[512,128]{1,0:T(8,128)(2,1)S(1)} %attention.2.refs_0_), channel_id=1, source_target_pairs={{0,4},{2,6},{4,0},{6,2},{8,12},{10,14},{12,8},{14,10},{1,5},{3,7},... | collective-permute-start | bytes 393224 | tf_op jit(solution)/shard_map/ppermute | solution.py:384
  66.4 7.4 %collective-permute-start.6 = (bf16[512,128]{1,0:T(8,128)(2,1)S(1)}, bf16[512,128]{1,0:T(8,128)(2,1)S(1)}, u32[]{:S(2)}, u32[]{:S(2)}) collective-permute-start(bf16[512,128]{1,0:T(8,128)(2,1)S(1)} %attention.2.refs_0_), channel_id=1, source_target_pairs={{0,6},{2,4},{4,2},{6,0},{8,14},{10,12},{12,10},{14,8},{1,7},{3,5},... | collective-permute-start | bytes 393224 | tf_op jit(solution)/shard_map/ppermute | solution.py:384
  68.8 10.1 %collective-permute-start.7 = (bf16[512,128]{1,0:T(8,128)(2,1)S(1)}, bf16[512,128]{1,0:T(8,128)(2,1)S(1)}, u32[]{:S(2)}, u32[]{:S(2)}) collective-permute-start(bf16[512,128]{1,0:T(8,128)(2,1)S(1)} %attention.2.refs_0_), channel_id=1, source_target_pairs={{0,8},{2,10},{4,12},{6,14},{8,0},{10,2},{12,4},{14,6},{1,9},{3,11}... | collective-permute-start | bytes 393224 | tf_op jit(solution)/shard_map/ppermute | solution.py:384
  70.5 8.5 %collective-permute-start.8 = (bf16[512,128]{1,0:T(8,128)(2,1)S(1)}, bf16[512,128]{1,0:T(8,128)(2,1)S(1)}, u32[]{:S(2)}, u32[]{:S(2)}) collective-permute-start(bf16[512,128]{1,0:T(8,128)(2,1)S(1)} %attention.2.refs_0_), channel_id=1, source_target_pairs={{0,10},{2,8},{4,14},{6,12},{8,2},{10,0},{12,6},{14,4},{1,11},{3,9}... | collective-permute-start | bytes 393224 | tf_op jit(solution)/shard_map/ppermute | solution.py:384
  71.8 7.2 %collective-permute-start.9 = (bf16[512,128]{1,0:T(8,128)(2,1)S(1)}, bf16[512,128]{1,0:T(8,128)(2,1)S(1)}, u32[]{:S(2)}, u32[]{:S(2)}) collective-permute-start(bf16[512,128]{1,0:T(8,128)(2,1)S(1)} %attention.2.refs_0_), channel_id=1, source_target_pairs={{0,12},{2,14},{4,8},{6,10},{8,4},{10,6},{12,0},{14,2},{1,13},{3,15... | collective-permute-start | bytes 393224 | tf_op jit(solution)/shard_map/ppermute | solution.py:384
  81.1 6.9 %collective-permute-start.11 = (bf16[256,1024]{1,0:T(8,128)(2,1)S(1)}, bf16[256,1024]{1,0:T(8,128)(2,1)S(1)}, u32[]{:S(2)}, u32[]{:S(2)}) collective-permute-start(bf16[256,1024]{1,0:T(8,128)(2,1)S(1)} %get-tuple-element.24.refs_10_), channel_id=1, source_target_pairs={{0,16},{16,0},{32,48},{48,32},{64,80},{80,64},{96,112},{112,96},{1... | collective-permute-start | bytes 1572872 | tf_op jit(solution)/shard_map/ppermute | solution.py:374
  88.7 6.9 %collective-permute-start.12 = (bf16[64,1024]{1,0:T(8,128)(2,1)S(1)}, bf16[64,1024]{1,0:T(8,128)(2,1)S(1)}, u32[]{:S(2)}, u32[]{:S(2)}) collective-permute-start(bf16[64,1024]{1,0:T(8,128)(2,1)S(1)} %get-tuple-element.26), channel_id=1, source_target_pairs={{0,32},{16,48},{32,0},{48,16},{64,96},{80,112},{96,64},{112,80},{1... | collective-permute-start | bytes 393224 | tf_op jit(solution)/shard_map/ppermute | solution.py:378
  88.8 6.8 %collective-permute-start.13 = (bf16[64,1024]{1,0:T(8,128)(2,1)S(1)}, bf16[64,1024]{1,0:T(8,128)(2,1)S(1)}, u32[]{:S(2)}, u32[]{:S(2)}) collective-permute-start(bf16[64,1024]{1,0:T(8,128)(2,1)S(1)} %get-tuple-element.27), channel_id=1, source_target_pairs={{0,64},{16,80},{32,96},{48,112},{64,0},{80,16},{96,32},{112,48},{1... | collective-permute-start | bytes 393224 | tf_op jit(solution)/shard_map/ppermute | solution.py:378
  91.8 8.9 %collective-permute-start.14 = (bf16[64,1024]{1,0:T(8,128)(2,1)S(1)}, bf16[64,1024]{1,0:T(8,128)(2,1)S(1)}, u32[]{:S(2)}, u32[]{:S(2)}) collective-permute-start(bf16[64,1024]{1,0:T(8,128)(2,1)S(1)} %get-tuple-element.28), channel_id=1, source_target_pairs={{0,96},{16,112},{32,64},{48,80},{64,32},{80,48},{96,0},{112,16},{1... | collective-permute-start | bytes 393224 | tf_op jit(solution)/shard_map/ppermute | solution.py:378
  100.8 7.8 %collective-permute-start.15 = (bf16[64,1024]{1,0:T(8,128)(2,1)S(1)}, bf16[64,1024]{1,0:T(8,128)(2,1)S(1)}, u32[]{:S(2)}, u32[]{:S(2)}) collective-permute-start(bf16[64,1024]{1,0:T(8,128)(2,1)S(1)} %add_convert_fusion), channel_id=1, source_target_pairs={{0,128},{16,144},{32,160},{48,176},{64,192},{80,208},{96,224},{112... | collective-permute-start | bytes 393224 | tf_op jit(solution)/shard_map/ppermute | solution.py:378
  108.6 7.8 %collective-permute-start.16 = (bf16[64,1024]{1,0:T(8,128)(2,1)S(1)}, bf16[64,1024]{1,0:T(8,128)(2,1)S(1)}, u32[]{:S(2)}, u32[]{:S(2)}) collective-permute-start(bf16[64,1024]{1,0:T(8,128)(2,1)S(1)} %collective-permute-done.15.refs_0_), channel_id=1, source_target_pairs={{0,32},{16,48},{32,0},{48,16},{64,96},{80,112},{96,64},{112,80},{1... | collective-permute-start | bytes 393224 | tf_op jit(solution)/shard_map/ppermute | solution.py:378
  114.1 5.0 %collective-permute-start.17 = (bf16[64,1024]{1,0:T(8,128)(2,1)S(1)}, bf16[64,1024]{1,0:T(8,128)(2,1)S(1)}, u32[]{:S(2)}, u32[]{:S(2)}) collective-permute-start(bf16[64,1024]{1,0:T(8,128)(2,1)S(1)} %collective-permute-done.15.refs_0_), channel_id=1, source_target_pairs={{0,64},{16,80},{32,96},{48,112},{64,0},{80,16},{96,32},{112,48},{1... | collective-permute-start | bytes 393224 | tf_op jit(solution)/shard_map/ppermute | solution.py:378
  115.2 9.0 %collective-permute-start.18 = (bf16[64,1024]{1,0:T(8,128)(2,1)S(1)}, bf16[64,1024]{1,0:T(8,128)(2,1)S(1)}, u32[]{:S(2)}, u32[]{:S(2)}) collective-permute-start(bf16[64,1024]{1,0:T(8,128)(2,1)S(1)} %collective-permute-done.15.refs_0_), channel_id=1, source_target_pairs={{0,96},{16,112},{32,64},{48,80},{64,32},{80,48},{96,0},{112,16},{1... | collective-permute-start | bytes 393224 | tf_op jit(solution)/shard_map/ppermute | solution.py:378
  124.8 5.4 %collective-permute-start.19 = (bf16[256,1024]{1,0:T(8,128)(2,1)S(1)}, bf16[256,1024]{1,0:T(8,128)(2,1)S(1)}, u32[]{:S(2)}, u32[]{:S(2)}) collective-permute-start(bf16[256,1024]{1,0:T(8,128)(2,1)S(1)} %arrange.2.refs_2_), channel_id=1, source_target_pairs={{0,16},{16,0},{32,48},{48,32},{64,80},{80,64},{96,112},{112,96},{1... | collective-permute-start | bytes 1572872 | tf_op jit(solution)/shard_map/ppermute | solution.py:374
  179.1 6.4 %collective-permute-start.20 = (bf16[512,128]{1,0:T(8,128)(2,1)S(1)}, bf16[512,128]{1,0:T(8,128)(2,1)S(1)}, u32[]{:S(2)}, u32[]{:S(2)}) collective-permute-start(bf16[512,128]{1,0:T(8,128)(2,1)S(1)} %attention.3.refs_0_), channel_id=1, source_target_pairs={{0,2},{2,0},{4,6},{6,4},{8,10},{10,8},{12,14},{14,12},{1,3},{3,1},... | collective-permute-start | bytes 393224 | tf_op jit(solution)/shard_map/ppermute | solution.py:384
  180.1 6.3 %collective-permute-start.21 = (bf16[512,128]{1,0:T(8,128)(2,1)S(1)}, bf16[512,128]{1,0:T(8,128)(2,1)S(1)}, u32[]{:S(2)}, u32[]{:S(2)}) collective-permute-start(bf16[512,128]{1,0:T(8,128)(2,1)S(1)} %attention.3.refs_0_), channel_id=1, source_target_pairs={{0,4},{2,6},{4,0},{6,2},{8,12},{10,14},{12,8},{14,10},{1,5},{3,7},... | collective-permute-start | bytes 393224 | tf_op jit(solution)/shard_map/ppermute | solution.py:384
  180.4 7.9 %collective-permute-start.22 = (bf16[512,128]{1,0:T(8,128)(2,1)S(1)}, bf16[512,128]{1,0:T(8,128)(2,1)S(1)}, u32[]{:S(2)}, u32[]{:S(2)}) collective-permute-start(bf16[512,128]{1,0:T(8,128)(2,1)S(1)} %attention.3.refs_0_), channel_id=1, source_target_pairs={{0,6},{2,4},{4,2},{6,0},{8,14},{10,12},{12,10},{14,8},{1,7},{3,5},... | collective-permute-start | bytes 393224 | tf_op jit(solution)/shard_map/ppermute | solution.py:384
  181.8 12.6 %collective-permute-start.23 = (bf16[512,128]{1,0:T(8,128)(2,1)S(1)}, bf16[512,128]{1,0:T(8,128)(2,1)S(1)}, u32[]{:S(2)}, u32[]{:S(2)}) collective-permute-start(bf16[512,128]{1,0:T(8,128)(2,1)S(1)} %attention.3.refs_0_), channel_id=1, source_target_pairs={{0,8},{2,10},{4,12},{6,14},{8,0},{10,2},{12,4},{14,6},{1,9},{3,11}... | collective-permute-start | bytes 393224 | tf_op jit(solution)/shard_map/ppermute | solution.py:384
  182.7 11.7 %collective-permute-start.24 = (bf16[512,128]{1,0:T(8,128)(2,1)S(1)}, bf16[512,128]{1,0:T(8,128)(2,1)S(1)}, u32[]{:S(2)}, u32[]{:S(2)}) collective-permute-start(bf16[512,128]{1,0:T(8,128)(2,1)S(1)} %attention.3.refs_0_), channel_id=1, source_target_pairs={{0,10},{2,8},{4,14},{6,12},{8,2},{10,0},{12,6},{14,4},{1,11},{3,9}... | collective-permute-start | bytes 393224 | tf_op jit(solution)/shard_map/ppermute | solution.py:384
  185.5 11.9 %collective-permute-start.25 = (bf16[512,128]{1,0:T(8,128)(2,1)S(1)}, bf16[512,128]{1,0:T(8,128)(2,1)S(1)}, u32[]{:S(2)}, u32[]{:S(2)}) collective-permute-start(bf16[512,128]{1,0:T(8,128)(2,1)S(1)} %attention.3.refs_0_), channel_id=1, source_target_pairs={{0,12},{2,14},{4,8},{6,10},{8,4},{10,6},{12,0},{14,2},{1,13},{3,15... | collective-permute-start | bytes 393224 | tf_op jit(solution)/shard_map/ppermute | solution.py:384
  186.4 11.0 %collective-permute-start.26 = (bf16[512,128]{1,0:T(8,128)(2,1)S(1)}, bf16[512,128]{1,0:T(8,128)(2,1)S(1)}, u32[]{:S(2)}, u32[]{:S(2)}) collective-permute-start(bf16[512,128]{1,0:T(8,128)(2,1)S(1)} %attention.3.refs_0_), channel_id=1, source_target_pairs={{0,14},{2,12},{4,10},{6,8},{8,6},{10,4},{12,2},{14,0},{1,15},{3,13... | collective-permute-start | bytes 393224 | tf_op jit(solution)/shard_map/ppermute | solution.py:384
  198.0 4.5 %collective-permute-start.27 = (bf16[256,1024]{1,0:T(8,128)(2,1)S(1)}, bf16[256,1024]{1,0:T(8,128)(2,1)S(1)}, u32[]{:S(2)}, u32[]{:S(2)}) collective-permute-start(bf16[256,1024]{1,0:T(8,128)(2,1)S(1)} %get-tuple-element.32.send_ref), channel_id=1, source_target_pairs={{0,16},{16,0},{32,48},{48,32},{64,80},{80,64},{96,112},{112,96},{1... | collective-permute-start | bytes 1572872 | tf_op jit(solution)/shard_map/ppermute | solution.py:374
  203.2 5.3 %collective-permute-start.29 = (bf16[64,1024]{1,0:T(8,128)(2,1)S(1)}, bf16[64,1024]{1,0:T(8,128)(2,1)S(1)}, u32[]{:S(2)}, u32[]{:S(2)}) collective-permute-start(bf16[64,1024]{1,0:T(8,128)(2,1)S(1)} %get-tuple-element.33), channel_id=1, source_target_pairs={{0,32},{16,48},{32,0},{48,16},{64,96},{80,112},{96,64},{112,80},{1... | collective-permute-start | bytes 393224 | tf_op jit(solution)/shard_map/ppermute | solution.py:378
  204.9 5.4 %collective-permute-start.30 = (bf16[64,1024]{1,0:T(8,128)(2,1)S(1)}, bf16[64,1024]{1,0:T(8,128)(2,1)S(1)}, u32[]{:S(2)}, u32[]{:S(2)}) collective-permute-start(bf16[64,1024]{1,0:T(8,128)(2,1)S(1)} %get-tuple-element.34), channel_id=1, source_target_pairs={{0,64},{16,80},{32,96},{48,112},{64,0},{80,16},{96,32},{112,48},{1... | collective-permute-start | bytes 393224 | tf_op jit(solution)/shard_map/ppermute | solution.py:378
  206.1 10.0 %collective-permute-start.31 = (bf16[64,1024]{1,0:T(8,128)(2,1)S(1)}, bf16[64,1024]{1,0:T(8,128)(2,1)S(1)}, u32[]{:S(2)}, u32[]{:S(2)}) collective-permute-start(bf16[64,1024]{1,0:T(8,128)(2,1)S(1)} %get-tuple-element.35), channel_id=1, source_target_pairs={{0,96},{16,112},{32,64},{48,80},{64,32},{80,48},{96,0},{112,16},{1... | collective-permute-start | bytes 393224 | tf_op jit(solution)/shard_map/ppermute | solution.py:378
  216.3 7.3 %collective-permute-start.32 = (bf16[64,1024]{1,0:T(8,128)(2,1)S(1)}, bf16[64,1024]{1,0:T(8,128)(2,1)S(1)}, u32[]{:S(2)}, u32[]{:S(2)}) collective-permute-start(bf16[64,1024]{1,0:T(8,128)(2,1)S(1)} %get-tuple-element.38), channel_id=1, source_target_pairs={{0,32},{16,48},{32,0},{48,16},{64,96},{80,112},{96,64},{112,80},{1... | collective-permute-start | bytes 393224 | tf_op jit(solution)/shard_map/ppermute | solution.py:378
  219.4 4.8 %collective-permute-start.33 = (bf16[64,1024]{1,0:T(8,128)(2,1)S(1)}, bf16[64,1024]{1,0:T(8,128)(2,1)S(1)}, u32[]{:S(2)}, u32[]{:S(2)}) collective-permute-start(bf16[64,1024]{1,0:T(8,128)(2,1)S(1)} %get-tuple-element.39), channel_id=1, source_target_pairs={{0,64},{16,80},{32,96},{48,112},{64,0},{80,16},{96,32},{112,48},{1... | collective-permute-start | bytes 393224 | tf_op jit(solution)/shard_map/ppermute | solution.py:378
  220.6 8.6 %collective-permute-start.34 = (bf16[64,1024]{1,0:T(8,128)(2,1)S(1)}, bf16[64,1024]{1,0:T(8,128)(2,1)S(1)}, u32[]{:S(2)}, u32[]{:S(2)}) collective-permute-start(bf16[64,1024]{1,0:T(8,128)(2,1)S(1)} %get-tuple-element.37), channel_id=1, source_target_pairs={{0,96},{16,112},{32,64},{48,80},{64,32},{80,48},{96,0},{112,16},{1... | collective-permute-start | bytes 393224 | tf_op jit(solution)/shard_map/ppermute | solution.py:378
  221.7 12.2 %collective-permute-start.28 = (bf16[256,1024]{1,0:T(8,128)(2,1)S(1)}, bf16[256,1024]{1,0:T(8,128)(2,1)S(1)}, u32[]{:S(2)}, u32[]{:S(2)}) collective-permute-start(bf16[256,1024]{1,0:T(8,128)(2,1)S(1)} %get-tuple-element.31.keep_ref), channel_id=1, source_target_pairs={{0,16},{16,0},{32,48},{48,32},{64,80},{80,64},{96,112},{112,96},{1... | collective-permute-start | bytes 1572872 | tf_op jit(solution)/shard_map/ppermute | solution.py:374
  229.8 5.6 %collective-permute-start.35 = (bf16[256,1024]{1,0:T(8,128)(2,1)S(1)}, bf16[256,1024]{1,0:T(8,128)(2,1)S(1)}, u32[]{:S(2)}, u32[]{:S(2)}) collective-permute-start(bf16[256,1024]{1,0:T(8,128)(2,1)S(1)} %arrange.3.own_ref), channel_id=1, source_target_pairs={{0,16},{16,0},{32,48},{48,32},{64,80},{80,64},{96,112},{112,96},{1... | collective-permute-start | bytes 1572872 | tf_op jit(solution)/shard_map/ppermute | solution.py:374

commit v2 on v1

--- a/solution.py
+++ b/solution.py
@@ -141,58 +141,62 @@
 def qkv_kernel(layered, *refs):
     refs = list(refs)
     place, x_ref = refs.pop(0), refs.pop(0)
-    pieces = [refs.pop(0) for _ in range(2)] if layered else []
+    pieces = [refs.pop(0) for _ in range(2 * CHIPS)] if layered else []
     even_ref, odd_ref, w_ref = refs.pop(0), refs.pop(0), refs.pop(0)
     base_ref = refs.pop(0) if layered else None
     out_ref, lhs = refs
-    core, layer = place[1], place[3]
+    core, chip, layer = place[1], place[2], place[3]
     rows, columns = x_ref.shape
     width = w_ref.shape[2]
 
-    vectors = jnp.where(core == 0, even_ref[...], odd_ref[...])
-    gain, bias = vectors[0:1, :], vectors[1:2, :]
-    row16 = lax.broadcasted_iota(jnp.int32, (EXTRA, columns), 0)
-    tail = jnp.zeros((EXTRA, columns), F32)
-    for number, vector in enumerate(split_parts(gain, 2) + split_parts(bias, 2)):
-        tail = tail + jnp.where(row16 == number, vector, 0.0)
-    lhs[rows : rows + EXTRA, :] = tail.astype(BF16)
-
     if layered:
-        half_rows = rows // 2
-        for half, piece in ((core, pieces[0]), (1 - core, pieces[1])):
-            place_rows = pl.ds(pl.multiple_of(half * half_rows, half_rows), half_rows)
+        size = rows // (2 * CHIPS)
+        for number, piece in enumerate(pieces):
+            half = core if number < CHIPS else 1 - core
+            start = (half * CHIPS + jnp.bitwise_xor(chip, number % CHIPS)) * size
+            place_rows = pl.ds(pl.multiple_of(start, size), size)
             tokens = x_ref[place_rows, :].astype(F32)
             added = tokens + piece[...].astype(F32)
             base_ref[place_rows, :] = jnp.where(layer == 1, added, tokens).astype(BF16)
-    source = base_ref if layered else x_ref
-    firsts, seconds = [], []
-    for start, size in segments_of(rows):
-        value = source[start : start + size, :].astype(F32)
-        first = jnp.sum(value, axis=1, keepdims=True)
-        second = jnp.sum(value * value, axis=1, keepdims=True)
-        lhs[start : start + size, :] = ((value - first * (1.0 / columns)) * gain).astype(BF16)
-        lane = lax.broadcasted_iota(jnp.int32, (size, 128), 1)
-        turned = jnp.where(lane == 0, first, jnp.where(lane == 1, second, 0.0)).T
-        firsts.append(turned[0:1, :])
-        seconds.append(turned[1:2, :])
-    blank = jnp.zeros((1, width), F32)
-    joined = lambda lines: jnp.concatenate(lines, axis=1) if len(lines) > 1 else lines[0]
-    lines = ending(blank, blank, joined(firsts), joined(seconds), width)
-    out_row = lax.broadcasted_iota(jnp.int32, (EXTRA, width), 0)
-
-    for pair in range(TP // 2):
-        weights = jnp.concatenate([w_ref[2 * pair], w_ref[2 * pair + 1]], axis=1)
-        result = jnp.dot(lhs[...], weights, preferred_element_type=F32)
-        for side in range(2):
-            head = 2 * pair + side
-            part = result[:, side * width : (side + 1) * width]
-            ends = part[rows : rows + EXTRA, :]
-            table = lines
-            vectors = split_parts(ends[0:1] + ends[1:2], 2) + split_parts(ends[2:3] + ends[3:4], 2)
-            for number, vector in enumerate(vectors):
-                table = table + jnp.where(out_row == number, vector, 0.0)
-            out_ref[head, 0:rows, :] = part[0:rows, :].astype(BF16)
-            out_ref[head, rows : rows + EXTRA, :] = table.astype(BF16)
+    @pl.when(layer == (1 if layered else 0))
+    def _():
+        vectors = jnp.where(core == 0, even_ref[...], odd_ref[...])
+        gain, bias = vectors[0:1, :], vectors[1:2, :]
+        row16 = lax.broadcasted_iota(jnp.int32, (EXTRA, columns), 0)
+        tail = jnp.zeros((EXTRA, columns), F32)
+        for number, vector in enumerate(split_parts(gain, 2) + split_parts(bias, 2)):
+            tail = tail + jnp.where(row16 == number, vector, 0.0)
+        lhs[rows : rows + EXTRA, :] = tail.astype(BF16)
+
+        source = base_ref if layered else x_ref
+        firsts, seconds = [], []
+        for start, size in segments_of(rows):
+            value = source[start : start + size, :].astype(F32)
+            first = jnp.sum(value, axis=1, keepdims=True)
+            second = jnp.sum(value * value, axis=1, keepdims=True)
+            lhs[start : start + size, :] = ((value - first * (1.0 / columns)) * gain).astype(BF16)
+            lane = lax.broadcasted_iota(jnp.int32, (size, 128), 1)
+            turned = jnp.where(lane == 0, first, jnp.where(lane == 1, second, 0.0)).T
+            firsts.append(turned[0:1, :])
+            seconds.append(turned[1:2, :])
+        blank = jnp.zeros((1, width), F32)
+        joined = lambda lines: jnp.concatenate(lines, axis=1) if len(lines) > 1 else lines[0]
+        lines = ending(blank, blank, joined(firsts), joined(seconds), width)
+        out_row = lax.broadcasted_iota(jnp.int32, (EXTRA, width), 0)
+
+        for pair in range(TP // 2):
+            weights = jnp.concatenate([w_ref[2 * pair], w_ref[2 * pair + 1]], axis=1)
+            result = jnp.dot(lhs[...], weights, preferred_element_type=F32)
+            for side in range(2):
+                head = 2 * pair + side
+                part = result[:, side * width : (side + 1) * width]
+                ends = part[rows : rows + EXTRA, :]
+                table = lines
+                vectors = split_parts(ends[0:1] + ends[1:2], 2) + split_parts(ends[2:3] + ends[3:4], 2)
+                for number, vector in enumerate(vectors):
+                    table = table + jnp.where(out_row == number, vector, 0.0)
+                out_ref[head, 0:rows, :] = part[0:rows, :].astype(BF16)
+                out_ref[head, rows : rows + EXTRA, :] = table.astype(BF16)
 
 
 def qkv(place, x, pieces, even, odd, w):
@@ -214,37 +218,40 @@
     return out if pieces else (None, out[0])
 
 
-def attention_kernel(features, pieces_ref, out_ref):
+def attention_kernel(features, phase, place, pieces_ref, out_ref):
     rows, head_dim = out_ref.shape
-    total, scale, offset = combine([pieces_ref.at[t] for t in range(TP)], features // TP)
-    joined = (total * scale + offset).astype(BF16)
-    query = joined[:, :head_dim]
-    key = joined[:, head_dim : 2 * head_dim]
-    value = joined[:, 2 * head_dim :]
-    scores = lax.dot_general(
-        query, key, (((1,), (1,)), ((), ())), preferred_element_type=F32
-    ) * (1.0 / head_dim**0.5)
-    at_query = lax.broadcasted_iota(jnp.int32, (rows, rows), 0)
-    at_key = lax.broadcasted_iota(jnp.int32, (rows, rows), 1)
-    scores = jnp.where(at_key <= at_query, scores, -1e30)
-    highest = jnp.max(scores, axis=1, keepdims=True)
-    lifted = jnp.exp(scores - highest)
-    weights = (lifted * (1.0 / jnp.sum(lifted, axis=1, keepdims=True))).astype(BF16)
-    out_ref[...] = jnp.dot(weights, value, preferred_element_type=F32).astype(BF16)
-
-
-def attention(pieces, features):
+
+    @pl.when(place[3] == phase)
+    def _():
+        total, scale, offset = combine([pieces_ref.at[t] for t in range(TP)], features // TP)
+        joined = (total * scale + offset).astype(BF16)
+        query = joined[:, :head_dim]
+        key = joined[:, head_dim : 2 * head_dim]
+        value = joined[:, 2 * head_dim :]
+        scores = lax.dot_general(
+            query, key, (((1,), (1,)), ((), ())), preferred_element_type=F32
+        ) * (1.0 / head_dim**0.5)
+        at_query = lax.broadcasted_iota(jnp.int32, (rows, rows), 0)
+        at_key = lax.broadcasted_iota(jnp.int32, (rows, rows), 1)
+        scores = jnp.where(at_key <= at_query, scores, -1e30)
+        highest = jnp.max(scores, axis=1, keepdims=True)
+        lifted = jnp.exp(scores - highest)
+        weights = (lifted * (1.0 / jnp.sum(lifted, axis=1, keepdims=True))).astype(BF16)
+        out_ref[...] = jnp.dot(weights, value, preferred_element_type=F32).astype(BF16)
+
+
+def attention(place, pieces, features, phase):
     rows = pieces.shape[1] - EXTRA
     head_dim = pieces.shape[2] // 3
     return pl.pallas_call(
-        functools.partial(attention_kernel, features),
+        functools.partial(attention_kernel, features, phase),
         out_shape=jax.ShapeDtypeStruct((rows, head_dim), BF16),
-        in_specs=[VMEM],
+        in_specs=[SMEM, VMEM],
         out_specs=VMEM,
         compiler_params=params(24),
         cost_estimate=cheap(),
         name="attention",
-    )(pieces)
+    )(place, pieces)
 
 
 def project_kernel(passing, place, *refs):
@@ -315,55 +322,38 @@
     )(place, keep, got)
 
 
-def arrange_kernel(place, *refs):
-    chip = place[2]
-    out_ref = refs[CHIPS]
-    size = out_ref.shape[0] // CHIPS
-    for d in range(CHIPS):
-        rows = pl.ds(pl.multiple_of(jnp.bitwise_xor(chip, d) * size, size), size)
-        out_ref[rows, :] = refs[d][...]
-
-
-def arrange(place, pieces):
-    rows, columns = pieces[0].shape
-    return pl.pallas_call(
-        arrange_kernel,
-        out_shape=jax.ShapeDtypeStruct((rows * CHIPS, columns), BF16),
-        in_specs=[SMEM] + [VMEM] * CHIPS,
-        out_specs=VMEM,
-        compiler_params=params(16),
-        cost_estimate=cheap(),
-        name="arrange",
-    )(place, *pieces)
-
-
-def finish_kernel(place, base_ref, keep_ref, got_ref, send_ref, other_keep_ref, own_ref, other_ref, out_ref):
-    core = place[1]
+def finish_kernel(place, base_ref, keep_ref, got_ref, send_ref, other_keep_ref, *refs):
+    own, others, out_ref = refs[:CHIPS], refs[CHIPS : 2 * CHIPS], refs[2 * CHIPS]
+    core, chip = place[1], place[2]
     half_rows = keep_ref.shape[0]
+    size = half_rows // CHIPS
     second = core.astype(F32)
     for half, sums, mine, theirs in (
-        (core, own_ref, keep_ref, got_ref),
-        (1 - core, other_ref, send_ref, other_keep_ref),
+        (core, own, keep_ref, got_ref),
+        (1 - core, others, send_ref, other_keep_ref),
     ):
-        rows = pl.ds(pl.multiple_of(half * half_rows, half_rows), half_rows)
-        out_ref[rows, :] = (
-            base_ref[rows, :].astype(F32)
-            + sums[...].astype(F32)
-            + mine[...].astype(F32)
-            + second * theirs[...].astype(F32)
-        ).astype(BF16)
-
-
-def finish(place, base, *values):
+        for d in range(CHIPS):
+            start = pl.multiple_of(jnp.bitwise_xor(chip, d) * size, size)
+            inside = pl.ds(start, size)
+            whole = pl.ds(pl.multiple_of(half * half_rows + start, size), size)
+            out_ref[whole, :] = (
+                base_ref[whole, :].astype(F32)
+                + sums[d][...].astype(F32)
+                + mine[inside, :].astype(F32)
+                + second * theirs[inside, :].astype(F32)
+            ).astype(BF16)
+
+
+def finish(place, base, keep, got, send, other_keep, own, others):
     return pl.pallas_call(
         finish_kernel,
         out_shape=jax.ShapeDtypeStruct(base.shape, BF16),
-        in_specs=[SMEM] + [VMEM] * (1 + len(values)),
+        in_specs=[SMEM] + [VMEM] * (5 + 2 * CHIPS),
         out_specs=VMEM,
         compiler_params=params(24),
         cost_estimate=cheap(),
         name="finish",
-    )(place, base, *values)
+    )(place, base, keep, got, send, other_keep, *own, *others)
 
 
 def over_tp(value):
@@ -407,15 +397,16 @@
     odd = over_cores(even)
 
     _, part = qkv(place, tokens, [], even, odd, weight_in)
-    out = attention(over_tp(part), features)
+    out = attention(place, over_tp(part), features, 0)
     kept = project(place, spread(out), weight_back, None)
     keep, send = kept
-    quarter = quarters(place, keep, over_cores(send))
-    total = sum(value.astype(F32) for value in over_layer(quarter)).astype(BF16)
-    half = arrange(place, over_layer([over_chips(total, CHIPS)] * CHIPS))
-
-    base, part = qkv(place, tokens, [half, over_cores(half)], even, odd, weight_in)
-    out = attention(over_tp(part), features)
+    arrived = over_layer(quarters(place, keep, over_cores(send)))
+    total = sum(value.astype(F32) for value in arrived).astype(BF16)
+    own = over_layer([over_chips(total, CHIPS)] * CHIPS)
+    others = [over_cores(value) for value in own]
+
+    base, part = qkv(place, tokens, own + others, even, odd, weight_in)
+    out = attention(place, over_tp(part), features, 1)
     keep, send = project(place, spread(out), weight_back, kept)
     got = over_cores(send)
     other_keep = over_cores(keep)
@@ -429,8 +420,9 @@
                 for e in range(CHIPS)
             ).astype(BF16)
         )
-    own = arrange(place, over_layer(before))
-    return finish(place, base, keep, got, send, other_keep, own, over_cores(own))[None]
+    own = over_layer(before)
+    others = [over_cores(value) for value in own]
+    return finish(place, base, keep, got, send, other_keep, own, others)[None]
 
 
 def solution(mesh):

time: 238 us -> 232 us (0.975)
  waiting for transfers between devices: 55.9 us -> 45.6 us
  starting transfers between devices: 69.2 us -> 78 us
  Pallas kernels: 22 us -> 16.2 us
    ppermute x6 -> x12, starting transfers between devices: 20.4 us -> 34.6 us  [over_cores(): return lax.ppermute(value, 'section', [(s, s ^ 1) for s in range(2 * SPAN)])]
    ppermute x16, waiting for transfers between devices: 34.5 us -> 24.4 us  [over_chips(): lax.ppermute(value, 'section', [(s, s ^ 2 * d) for s in range(2 * SPAN)])]
    ppermute x16, starting transfers between devices: 30.5 us -> 25 us  [over_chips(): lax.ppermute(value, 'section', [(s, s ^ 2 * d) for s in range(2 * SPAN)])]
    pallas_call x2, Pallas kernels: 9.63 us -> 5.31 us  [qkv(): pl.pallas_call(functools.partial(qkv_kernel, bool(pieces)), out_shape=sha...]
    pallas_call x4 -> x2, Pallas kernels: 5.16 us -> 3.13 us  [attention(): pl.pallas_call(functools.partial(attention_kernel, features, phase), out_...]
    ppermute x6 -> x12, waiting for transfers between devices: 6.98 us -> 6.56 us  [over_cores(): return lax.ppermute(value, 'section', [(s, s ^ 1) for s in range(2 * SPAN)])]
  transfers between devices with their start and end apart: 36 -> 42, of which waited for: 20 -> 17; matrix products, arithmetic and copies ran while one was open for 0% -> 1% of each run, Pallas kernels for 0% -> 0%
where the time goes in v2:
time: 232 us; the launch traced here: 231 us
  blocking collectives  85.1 us (37%)
  starting transfers between devices  78 us (34%)
  waiting for transfers between devices  45.6 us (20%)
  Pallas kernels  16.2 us (7%)
  local copies, waits for them, and re-layouts  4.01 us (2%)
    all_to_all x2, blocking collectives, over_tp(): return lax.all_to_all(value, 'tp', 0, 0, tiled=True)  85.1 us
    ppermute x12, starting transfers between devices, over_cores(): return lax.ppermute(value, 'section', [(s, s ^ 1) for s in range(2 * SPAN)])  34.6 us
    ppermute x16, starting transfers between devices, over_chips(): lax.ppermute(value, 'section', [(s, s ^ 2 * d) for s in range(2 * SPAN)])  25 us
    ppermute x16, waiting for transfers between devices, over_chips(): lax.ppermute(value, 'section', [(s, s ^ 2 * d) for s in range(2 * SPAN)])  24.4 us
    ppermute x14, starting transfers between devices, spread(): got[d] = lax.ppermute(value, 'tp', [(t, t ^ d) for t in range(TP)])  18.4 us
    ppermute x14, waiting for transfers between devices, spread(): got[d] = lax.ppermute(value, 'tp', [(t, t ^ d) for t in range(TP)])  14.7 us
    ppermute x12, waiting for transfers between devices, over_cores(): return lax.ppermute(value, 'section', [(s, s ^ 1) for s in range(2 * SPAN)])  6.56 us
    pallas_call x2, Pallas kernels, qkv(): pl.pallas_call(functools.partial(qkv_kernel, bool(pieces)), out_shape=sha...  5.31 us
  transfers between devices with their start and end apart: 42, of which 17 were waited for; matrix products, arithmetic and copies ran while one was open for 1% of the time, Pallas kernels for 0%

profile of v2, /device:TPU:1, one launch (start us, length us, event | category | flops | bytes accessed | tf_op | source)
XLA Modules:
  0.0 231.3 jit_solution(16327439622586735368)
XLA Ops:
  0.0 0.7 pad_maximum_fusion.own_ref
  0.7 2.6 %collective-permute-start = (f32[2,1024]{1,0:T(2,128)S(1)}, f32[2,1024]{1,0:T(2,128)S(1)}, u32[]{:S(2)}, u32[]{:S(2)}) collective-permute-start(f32[2,1024]{1,0:T(2,128)S(1)} %pad_maximum_fusion.own_ref), channel_id=1, source_target_pairs={{0,32},{16,48},{32,0},{48,16},{64,96},{80,112},{96,64},{112,80},{1... | collective-permute-start | bytes 24584 | tf_op jit(solution)/shard_map/ppermute | solution.py:368
  3.3 3.0 %collective-permute-start.1 = (f32[2,1024]{1,0:T(2,128)S(1)}, f32[2,1024]{1,0:T(2,128)S(1)}, u32[]{:S(2)}, u32[]{:S(2)}) collective-permute-start(f32[2,1024]{1,0:T(2,128)S(1)} %pad_maximum_fusion.own_ref), channel_id=1, source_target_pairs={{0,64},{16,80},{32,96},{48,112},{64,0},{80,16},{96,32},{112,48},{1... | collective-permute-start | bytes 24584 | tf_op jit(solution)/shard_map/ppermute | solution.py:368
  6.3 2.8 %copy-done.1 = bf16[1,8,1024,384]{3,2,1,0:T(8,128)(2,1)S(1)} copy-done((bf16[1,8,1024,384]{3,2,1,0:T(8,128)(2,1)S(1)}, bf16[1,8,1024,384]{3,2,1,0:T(8,128)(2,1)}, u32[]{:S(2)}) %copy-start.1) | copy-done | bytes 6291480
  9.1 1.2 copy-done.2
  10.4 0.5 stage.1
  10.9 0.6 pick.1.refs_2_.refs_10_
  11.5 2.3 collective-permute-start.3
  13.7 0.8 collective-permute-done.3.refs_3_.refs_11_
  14.5 4.5 %qkv.2 = bf16[8,528,384]{2,1,0:T(8,128)(2,1)S(1)} custom-call(s32[4]{0:T(128)S(1)} %pad_add_fusion.place.refs_0_, bf16[512,1024]{1,0:T(8,128)(2,1)S(1)} %get-tuple-element.21.refs_1_, f32[2,1024]{1,0:T(2,128)S(1)} %pick.1.refs_2_.refs_10_, f32[2,1024]{1,0:T(2,128)S(1)} %collective-permute-done.3.refs_3_.refs_11_, ...), custom_call_target="tpu_custom_call" | custom-call | flops 1 | bytes 1 | tf_op jit(solution)/shard_map/qkv/pallas_call | solution.py:208
  19.0 43.5 %all_to_all.10.pieces_ref = bf16[8,528,384]{2,1,0:T(8,128)(2,1)S(1)} all-to-all(bf16[8,528,384]{2,1,0:T(8,128)(2,1)S(1)} %qkv.2), channel_id=1, replica_groups=mesh['section'=16,'tp'=8,'dp'=2] {'tp'}, dimensions={0} | all-to-all | bytes 6488064 | tf_op jit(solution)/shard_map/all_to_all | solution.py:360
  62.5 2.6 %attention.2.refs_0_ = bf16[512,128]{1,0:T(8,128)(2,1)S(1)} custom-call(s32[4]{0:T(128)S(1)} %pad_add_fusion.place.refs_0_, bf16[8,528,384]{2,1,0:T(8,128)(2,1)S(1)} %all_to_all.10.pieces_ref), custom_call_target="tpu_custom_call" | custom-call | flops 1 | bytes 1 | tf_op jit(solution)/shard_map/attention/pallas_call | solution.py:246
  65.1 1.7 collective-permute-start.10
  67.0 2.4 %collective-permute-start.6 = (bf16[512,128]{1,0:T(8,128)(2,1)S(1)}, bf16[512,128]{1,0:T(8,128)(2,1)S(1)}, u32[]{:S(2)}, u32[]{:S(2)}) collective-permute-start(bf16[512,128]{1,0:T(8,128)(2,1)S(1)} %attention.2.refs_0_), channel_id=1, source_target_pairs={{0,6},{2,4},{4,2},{6,0},{8,14},{10,12},{12,10},{14,8},{1,7},{3,5},... | collective-permute-start | bytes 393224 | tf_op jit(solution)/shard_map/ppermute | solution.py:374
  69.4 1.4 collective-permute-start.7
  71.1 1.3 collective-permute-start.8
  72.3 2.0 collective-permute-start.9
  74.4 5.2 %collective-permute-done.7.refs_4_ = bf16[512,128]{1,0:T(8,128)(2,1)S(1)} collective-permute-done((bf16[512,128]{1,0:T(8,128)(2,1)S(1)}, bf16[512,128]{1,0:T(8,128)(2,1)S(1)}, u32[]{:S(2)}, u32[]{:S(2)}) %collective-permute-start.7) | collective-permute-done | bytes 131104 | tf_op jit(solution)/shard_map/ppermute | solution.py:374
  79.6 2.1 project.2
  81.7 5.4 %collective-permute-start.11 = (bf16[256,1024]{1,0:T(8,128)(2,1)S(1)}, bf16[256,1024]{1,0:T(8,128)(2,1)S(1)}, u32[]{:S(2)}, u32[]{:S(2)}) collective-permute-start(bf16[256,1024]{1,0:T(8,128)(2,1)S(1)} %get-tuple-element.24.refs_10_), channel_id=1, source_target_pairs={{0,16},{16,0},{32,48},{48,32},{64,80},{80,64},{96,112},{112,96},{1... | collective-permute-start | bytes 1572872 | tf_op jit(solution)/shard_map/ppermute | solution.py:364
  87.1 1.5 collective-permute-done.11.got_ref
  88.6 0.7 quarters.2
  89.4 3.0 %collective-permute-start.13 = (bf16[64,1024]{1,0:T(8,128)(2,1)S(1)}, bf16[64,1024]{1,0:T(8,128)(2,1)S(1)}, u32[]{:S(2)}, u32[]{:S(2)}) collective-permute-start(bf16[64,1024]{1,0:T(8,128)(2,1)S(1)} %get-tuple-element.27), channel_id=1, source_target_pairs={{0,64},{16,80},{32,96},{48,112},{64,0},{80,16},{96,32},{112,48},{1... | collective-permute-start | bytes 393224 | tf_op jit(solution)/shard_map/ppermute | solution.py:368
  92.4 0.5 collective-permute-start.14
  92.9 3.3 %collective-permute-done.12 = bf16[64,1024]{1,0:T(8,128)(2,1)S(1)} collective-permute-done((bf16[64,1024]{1,0:T(8,128)(2,1)S(1)}, bf16[64,1024]{1,0:T(8,128)(2,1)S(1)}, u32[]{:S(2)}, u32[]{:S(2)}) %collective-permute-start.12) | collective-permute-done | bytes 131104 | tf_op jit(solution)/shard_map/ppermute | solution.py:368
  96.2 5.1 %collective-permute-done.14 = bf16[64,1024]{1,0:T(8,128)(2,1)S(1)} collective-permute-done((bf16[64,1024]{1,0:T(8,128)(2,1)S(1)}, bf16[64,1024]{1,0:T(8,128)(2,1)S(1)}, u32[]{:S(2)}, u32[]{:S(2)}) %collective-permute-start.14) | collective-permute-done | bytes 131104 | tf_op jit(solution)/shard_map/ppermute | solution.py:368
  101.5 7.7 %collective-permute-done.15.refs_2_ = bf16[64,1024]{1,0:T(8,128)(2,1)S(1)} collective-permute-done((bf16[64,1024]{1,0:T(8,128)(2,1)S(1)}, bf16[64,1024]{1,0:T(8,128)(2,1)S(1)}, u32[]{:S(2)}, u32[]{:S(2)}) %collective-permute-start.15) | collective-permute-done | bytes 131104 | tf_op jit(solution)/shard_map/ppermute | solution.py:368
  109.2 4.6 %collective-permute-start.16 = (bf16[64,1024]{1,0:T(8,128)(2,1)S(1)}, bf16[64,1024]{1,0:T(8,128)(2,1)S(1)}, u32[]{:S(2)}, u32[]{:S(2)}) collective-permute-start(bf16[64,1024]{1,0:T(8,128)(2,1)S(1)} %collective-permute-done.15.refs_2_), channel_id=1, source_target_pairs={{0,32},{16,48},{32,0},{48,16},{64,96},{80,112},{96,64},{112,80},{1... | collective-permute-start | bytes 393224 | tf_op jit(solution)/shard_map/ppermute | solution.py:368
  113.9 1.0 collective-permute-start.17
  114.8 1.2 collective-permute-start.18
  116.0 5.8 %collective-permute-start.19 = (bf16[64,1024]{1,0:T(8,128)(2,1)S(1)}, bf16[64,1024]{1,0:T(8,128)(2,1)S(1)}, u32[]{:S(2)}, u32[]{:S(2)}) collective-permute-start(bf16[64,1024]{1,0:T(8,128)(2,1)S(1)} %collective-permute-done.15.refs_2_), channel_id=1, source_target_pairs={{0,16},{16,0},{32,48},{48,32},{64,80},{80,64},{96,112},{112,96},{1... | collective-permute-start | bytes 393224 | tf_op jit(solution)/shard_map/ppermute | solution.py:364
  121.8 0.4 collective-permute-start.20
  122.3 5.5 %collective-permute-start.21 = (bf16[64,1024]{1,0:T(8,128)(2,1)S(1)}, bf16[64,1024]{1,0:T(8,128)(2,1)S(1)}, u32[]{:S(2)}, u32[]{:S(2)}) collective-permute-start(bf16[64,1024]{1,0:T(8,128)(2,1)S(1)} %collective-permute-done.17.refs_4_), channel_id=1, source_target_pairs={{0,16},{16,0},{32,48},{48,32},{64,80},{80,64},{96,112},{112,96},{1... | collective-permute-start | bytes 393224 | tf_op jit(solution)/shard_map/ppermute | solution.py:364
  127.8 1.0 collective-permute-done.21.refs_8_
  129.1 0.8 qkv.3
  129.9 41.6 %all_to_all.11.pieces_ref = bf16[8,528,384]{2,1,0:T(8,128)(2,1)S(1)} all-to-all(bf16[8,528,384]{2,1,0:T(8,128)(2,1)S(1)} %get-tuple-element.30), channel_id=1, replica_groups=mesh['section'=16,'tp'=8,'dp'=2] {'tp'}, dimensions={0} | all-to-all | bytes 6488064 | tf_op jit(solution)/shard_map/all_to_all | solution.py:360
  171.5 0.5 attention.3.refs_0_
  172.1 1.2 collective-permute-start.23
  173.7 1.2 collective-permute-start.25
  174.8 1.2 collective-permute-start.26
  176.1 2.6 %collective-permute-start.27 = (bf16[512,128]{1,0:T(8,128)(2,1)S(1)}, bf16[512,128]{1,0:T(8,128)(2,1)S(1)}, u32[]{:S(2)}, u32[]{:S(2)}) collective-permute-start(bf16[512,128]{1,0:T(8,128)(2,1)S(1)} %attention.3.refs_0_), channel_id=1, source_target_pairs={{0,10},{2,8},{4,14},{6,12},{8,2},{10,0},{12,6},{14,4},{1,11},{3,9}... | collective-permute-start | bytes 393224 | tf_op jit(solution)/shard_map/ppermute | solution.py:374
  178.6 1.0 collective-permute-start.28
  179.6 1.8 collective-permute-start.29
  181.4 6.1 %collective-permute-done.26.refs_4_ = bf16[512,128]{1,0:T(8,128)(2,1)S(1)} collective-permute-done((bf16[512,128]{1,0:T(8,128)(2,1)S(1)}, bf16[512,128]{1,0:T(8,128)(2,1)S(1)}, u32[]{:S(2)}, u32[]{:S(2)}) %collective-permute-start.26) | collective-permute-done | bytes 131104 | tf_op jit(solution)/shard_map/ppermute | solution.py:374
  187.5 3.1 %collective-permute-done.28.refs_6_ = bf16[512,128]{1,0:T(8,128)(2,1)S(1)} collective-permute-done((bf16[512,128]{1,0:T(8,128)(2,1)S(1)}, bf16[512,128]{1,0:T(8,128)(2,1)S(1)}, u32[]{:S(2)}, u32[]{:S(2)}) %collective-permute-start.28) | collective-permute-done | bytes 131104 | tf_op jit(solution)/shard_map/ppermute | solution.py:374
  190.6 0.6 project.3
  191.3 2.8 %collective-permute-start.30 = (bf16[256,1024]{1,0:T(8,128)(2,1)S(1)}, bf16[256,1024]{1,0:T(8,128)(2,1)S(1)}, u32[]{:S(2)}, u32[]{:S(2)}) collective-permute-start(bf16[256,1024]{1,0:T(8,128)(2,1)S(1)} %get-tuple-element.32.send_ref), channel_id=1, source_target_pairs={{0,16},{16,0},{32,48},{48,32},{64,80},{80,64},{96,112},{112,96},{1... | collective-permute-start | bytes 1572872 | tf_op jit(solution)/shard_map/ppermute | solution.py:364
  194.1 1.5 collective-permute-done.30.got_ref
  195.7 1.2 quarters.3
  196.9 1.3 collective-permute-start.32
  198.2 1.5 collective-permute-start.33
  199.7 1.0 collective-permute-start.34
  200.7 1.0 collective-permute-start.31
  201.9 1.8 collective-permute-done.33
  203.8 6.1 %collective-permute-done.34 = bf16[64,1024]{1,0:T(8,128)(2,1)} collective-permute-done((bf16[64,1024]{1,0:T(8,128)(2,1)S(1)}, bf16[64,1024]{1,0:T(8,128)(2,1)}, u32[]{:S(2)}, u32[]{:S(2)}) %collective-permute-start.34) | collective-permute-done | bytes 131104 | tf_op jit(solution)/shard_map/ppermute | solution.py:368
  209.9 1.3 fusion.8
  211.2 2.6 %collective-permute-start.35 = (bf16[64,1024]{1,0:T(8,128)(2,1)S(1)}, bf16[64,1024]{1,0:T(8,128)(2,1)S(1)}, u32[]{:S(2)}, u32[]{:S(2)}) collective-permute-start(bf16[64,1024]{1,0:T(8,128)(2,1)S(1)} %get-tuple-element.38), channel_id=1, source_target_pairs={{0,32},{16,48},{32,0},{48,16},{64,96},{80,112},{96,64},{112,80},{1... | collective-permute-start | bytes 393224 | tf_op jit(solution)/shard_map/ppermute | solution.py:368
  213.7 1.6 collective-permute-start.36
  215.3 1.1 collective-permute-start.37
  216.4 1.8 collective-permute-start.38
  218.2 1.6 collective-permute-start.39
  219.9 8.0 %collective-permute-start.40 = (bf16[64,1024]{1,0:T(8,128)(2,1)S(1)}, bf16[64,1024]{1,0:T(8,128)(2,1)S(1)}, u32[]{:S(2)}, u32[]{:S(2)}) collective-permute-start(bf16[64,1024]{1,0:T(8,128)(2,1)S(1)} %collective-permute-done.36.refs_2_), channel_id=1, source_target_pairs={{0,16},{16,0},{32,48},{48,32},{64,80},{80,64},{96,112},{112,96},{1... | collective-permute-start | bytes 393224 | tf_op jit(solution)/shard_map/ppermute | solution.py:364
  227.9 1.0 collective-permute-done.40.refs_6_
  229.2 2.1 finish.1
  (43 shorter events, 2.2 us)
Async XLA Ops:
  0.7 10.2 %collective-permute-start = (f32[2,1024]{1,0:T(2,128)S(1)}, f32[2,1024]{1,0:T(2,128)S(1)}, u32[]{:S(2)}, u32[]{:S(2)}) collective-permute-start(f32[2,1024]{1,0:T(2,128)S(1)} %pad_maximum_fusion.own_ref), channel_id=1, source_target_pairs={{0,32},{16,48},{32,0},{48,16},{64,96},{80,112},{96,64},{112,80},{1... | collective-permute-start | bytes 24584 | tf_op jit(solution)/shard_map/ppermute | solution.py:368
  3.3 7.6 %collective-permute-start.1 = (f32[2,1024]{1,0:T(2,128)S(1)}, f32[2,1024]{1,0:T(2,128)S(1)}, u32[]{:S(2)}, u32[]{:S(2)}) collective-permute-start(f32[2,1024]{1,0:T(2,128)S(1)} %pad_maximum_fusion.own_ref), channel_id=1, source_target_pairs={{0,64},{16,80},{32,96},{48,112},{64,0},{80,16},{96,32},{112,48},{1... | collective-permute-start | bytes 24584 | tf_op jit(solution)/shard_map/ppermute | solution.py:368
  6.3 4.6 %collective-permute-start.2 = (f32[2,1024]{1,0:T(2,128)S(1)}, f32[2,1024]{1,0:T(2,128)S(1)}, u32[]{:S(2)}, u32[]{:S(2)}) collective-permute-start(f32[2,1024]{1,0:T(2,128)S(1)} %pad_maximum_fusion.own_ref), channel_id=1, source_target_pairs={{0,96},{16,112},{32,64},{48,80},{64,32},{80,48},{96,0},{112,16},{1... | collective-permute-start | bytes 24584 | tf_op jit(solution)/shard_map/ppermute | solution.py:368
  6.3 2.8 %copy-start.1 = (bf16[1,8,1024,384]{3,2,1,0:T(8,128)(2,1)S(1)}, bf16[1,8,1024,384]{3,2,1,0:T(8,128)(2,1)}, u32[]{:S(2)}) copy-start(bf16[1,8,1024,384]{3,2,1,0:T(8,128)(2,1)} %param.8) | copy-start | bytes 18874372
  9.1 1.2 copy-start.2
  11.5 3.1 %collective-permute-start.3 = (f32[2,1024]{1,0:T(2,128)S(1)}, f32[2,1024]{1,0:T(2,128)S(1)}, u32[]{:S(2)}, u32[]{:S(2)}) collective-permute-start(f32[2,1024]{1,0:T(2,128)S(1)} %pick.1.refs_2_.refs_10_), channel_id=1, source_target_pairs={{0,16},{16,0},{32,48},{48,32},{64,80},{80,64},{96,112},{112,96},{1... | collective-permute-start | bytes 24584 | tf_op jit(solution)/shard_map/ppermute | solution.py:364
  62.5 17.1 %copy-start = (bf16[1,1024,1024]{2,1,0:T(8,128)(2,1)S(1)}, bf16[1,1024,1024]{2,1,0:T(8,128)(2,1)}, u32[]{:S(2)}) copy-start(bf16[1,1024,1024]{2,1,0:T(8,128)(2,1)} %param.9) | copy-start | bytes 6291460
  65.1 6.0 %collective-permute-start.10 = (bf16[512,128]{1,0:T(8,128)(2,1)S(1)}, bf16[512,128]{1,0:T(8,128)(2,1)S(1)}, u32[]{:S(2)}, u32[]{:S(2)}) collective-permute-start(bf16[512,128]{1,0:T(8,128)(2,1)S(1)} %attention.2.refs_0_), channel_id=1, source_target_pairs={{0,14},{2,12},{4,10},{6,8},{8,6},{10,4},{12,2},{14,0},{1,15},{3,13... | collective-permute-start | bytes 393224 | tf_op jit(solution)/shard_map/ppermute | solution.py:374
  66.8 5.6 %collective-permute-start.4 = (bf16[512,128]{1,0:T(8,128)(2,1)S(1)}, bf16[512,128]{1,0:T(8,128)(2,1)S(1)}, u32[]{:S(2)}, u32[]{:S(2)}) collective-permute-start(bf16[512,128]{1,0:T(8,128)(2,1)S(1)} %attention.2.refs_0_), channel_id=1, source_target_pairs={{0,2},{2,0},{4,6},{6,4},{8,10},{10,8},{12,14},{14,12},{1,3},{3,1},... | collective-permute-start | bytes 393224 | tf_op jit(solution)/shard_map/ppermute | solution.py:374
  67.0 7.4 %collective-permute-start.5 = (bf16[512,128]{1,0:T(8,128)(2,1)S(1)}, bf16[512,128]{1,0:T(8,128)(2,1)S(1)}, u32[]{:S(2)}, u32[]{:S(2)}) collective-permute-start(bf16[512,128]{1,0:T(8,128)(2,1)S(1)} %attention.2.refs_0_), channel_id=1, source_target_pairs={{0,4},{2,6},{4,0},{6,2},{8,12},{10,14},{12,8},{14,10},{1,5},{3,7},... | collective-permute-start | bytes 393224 | tf_op jit(solution)/shard_map/ppermute | solution.py:374
  67.0 7.4 %collective-permute-start.6 = (bf16[512,128]{1,0:T(8,128)(2,1)S(1)}, bf16[512,128]{1,0:T(8,128)(2,1)S(1)}, u32[]{:S(2)}, u32[]{:S(2)}) collective-permute-start(bf16[512,128]{1,0:T(8,128)(2,1)S(1)} %attention.2.refs_0_), channel_id=1, source_target_pairs={{0,6},{2,4},{4,2},{6,0},{8,14},{10,12},{12,10},{14,8},{1,7},{3,5},... | collective-permute-start | bytes 393224 | tf_op jit(solution)/shard_map/ppermute | solution.py:374
  69.4 10.1 %collective-permute-start.7 = (bf16[512,128]{1,0:T(8,128)(2,1)S(1)}, bf16[512,128]{1,0:T(8,128)(2,1)S(1)}, u32[]{:S(2)}, u32[]{:S(2)}) collective-permute-start(bf16[512,128]{1,0:T(8,128)(2,1)S(1)} %attention.2.refs_0_), channel_id=1, source_target_pairs={{0,8},{2,10},{4,12},{6,14},{8,0},{10,2},{12,4},{14,6},{1,9},{3,11}... | collective-permute-start | bytes 393224 | tf_op jit(solution)/shard_map/ppermute | solution.py:374
  71.1 8.5 %collective-permute-start.8 = (bf16[512,128]{1,0:T(8,128)(2,1)S(1)}, bf16[512,128]{1,0:T(8,128)(2,1)S(1)}, u32[]{:S(2)}, u32[]{:S(2)}) collective-permute-start(bf16[512,128]{1,0:T(8,128)(2,1)S(1)} %attention.2.refs_0_), channel_id=1, source_target_pairs={{0,10},{2,8},{4,14},{6,12},{8,2},{10,0},{12,6},{14,4},{1,11},{3,9}... | collective-permute-start | bytes 393224 | tf_op jit(solution)/shard_map/ppermute | solution.py:374
  72.3 7.2 %collective-permute-start.9 = (bf16[512,128]{1,0:T(8,128)(2,1)S(1)}, bf16[512,128]{1,0:T(8,128)(2,1)S(1)}, u32[]{:S(2)}, u32[]{:S(2)}) collective-permute-start(bf16[512,128]{1,0:T(8,128)(2,1)S(1)} %attention.2.refs_0_), channel_id=1, source_target_pairs={{0,12},{2,14},{4,8},{6,10},{8,4},{10,6},{12,0},{14,2},{1,13},{3,15... | collective-permute-start | bytes 393224 | tf_op jit(solution)/shard_map/ppermute | solution.py:374
  81.7 6.9 %collective-permute-start.11 = (bf16[256,1024]{1,0:T(8,128)(2,1)S(1)}, bf16[256,1024]{1,0:T(8,128)(2,1)S(1)}, u32[]{:S(2)}, u32[]{:S(2)}) collective-permute-start(bf16[256,1024]{1,0:T(8,128)(2,1)S(1)} %get-tuple-element.24.refs_10_), channel_id=1, source_target_pairs={{0,16},{16,0},{32,48},{48,32},{64,80},{80,64},{96,112},{112,96},{1... | collective-permute-start | bytes 1572872 | tf_op jit(solution)/shard_map/ppermute | solution.py:364
  89.3 6.9 %collective-permute-start.12 = (bf16[64,1024]{1,0:T(8,128)(2,1)S(1)}, bf16[64,1024]{1,0:T(8,128)(2,1)S(1)}, u32[]{:S(2)}, u32[]{:S(2)}) collective-permute-start(bf16[64,1024]{1,0:T(8,128)(2,1)S(1)} %get-tuple-element.26), channel_id=1, source_target_pairs={{0,32},{16,48},{32,0},{48,16},{64,96},{80,112},{96,64},{112,80},{1... | collective-permute-start | bytes 393224 | tf_op jit(solution)/shard_map/ppermute | solution.py:368
  89.4 6.8 %collective-permute-start.13 = (bf16[64,1024]{1,0:T(8,128)(2,1)S(1)}, bf16[64,1024]{1,0:T(8,128)(2,1)S(1)}, u32[]{:S(2)}, u32[]{:S(2)}) collective-permute-start(bf16[64,1024]{1,0:T(8,128)(2,1)S(1)} %get-tuple-element.27), channel_id=1, source_target_pairs={{0,64},{16,80},{32,96},{48,112},{64,0},{80,16},{96,32},{112,48},{1... | collective-permute-start | bytes 393224 | tf_op jit(solution)/shard_map/ppermute | solution.py:368
  92.4 8.9 %collective-permute-start.14 = (bf16[64,1024]{1,0:T(8,128)(2,1)S(1)}, bf16[64,1024]{1,0:T(8,128)(2,1)S(1)}, u32[]{:S(2)}, u32[]{:S(2)}) collective-permute-start(bf16[64,1024]{1,0:T(8,128)(2,1)S(1)} %get-tuple-element.28), channel_id=1, source_target_pairs={{0,96},{16,112},{32,64},{48,80},{64,32},{80,48},{96,0},{112,16},{1... | collective-permute-start | bytes 393224 | tf_op jit(solution)/shard_map/ppermute | solution.py:368
  101.4 7.8 %collective-permute-start.15 = (bf16[64,1024]{1,0:T(8,128)(2,1)S(1)}, bf16[64,1024]{1,0:T(8,128)(2,1)S(1)}, u32[]{:S(2)}, u32[]{:S(2)}) collective-permute-start(bf16[64,1024]{1,0:T(8,128)(2,1)S(1)} %add_convert_fusion), channel_id=1, source_target_pairs={{0,128},{16,144},{32,160},{48,176},{64,192},{80,208},{96,224},{112... | collective-permute-start | bytes 393224 | tf_op jit(solution)/shard_map/ppermute | solution.py:368
  109.2 12.6 %collective-permute-start.16 = (bf16[64,1024]{1,0:T(8,128)(2,1)S(1)}, bf16[64,1024]{1,0:T(8,128)(2,1)S(1)}, u32[]{:S(2)}, u32[]{:S(2)}) collective-permute-start(bf16[64,1024]{1,0:T(8,128)(2,1)S(1)} %collective-permute-done.15.refs_2_), channel_id=1, source_target_pairs={{0,32},{16,48},{32,0},{48,16},{64,96},{80,112},{96,64},{112,80},{1... | collective-permute-start | bytes 393224 | tf_op jit(solution)/shard_map/ppermute | solution.py:368
  113.9 8.4 %collective-permute-start.17 = (bf16[64,1024]{1,0:T(8,128)(2,1)S(1)}, bf16[64,1024]{1,0:T(8,128)(2,1)S(1)}, u32[]{:S(2)}, u32[]{:S(2)}) collective-permute-start(bf16[64,1024]{1,0:T(8,128)(2,1)S(1)} %collective-permute-done.15.refs_2_), channel_id=1, source_target_pairs={{0,64},{16,80},{32,96},{48,112},{64,0},{80,16},{96,32},{112,48},{1... | collective-permute-start | bytes 393224 | tf_op jit(solution)/shard_map/ppermute | solution.py:368
  114.8 12.9 %collective-permute-start.18 = (bf16[64,1024]{1,0:T(8,128)(2,1)S(1)}, bf16[64,1024]{1,0:T(8,128)(2,1)S(1)}, u32[]{:S(2)}, u32[]{:S(2)}) collective-permute-start(bf16[64,1024]{1,0:T(8,128)(2,1)S(1)} %collective-permute-done.15.refs_2_), channel_id=1, source_target_pairs={{0,96},{16,112},{32,64},{48,80},{64,32},{80,48},{96,0},{112,16},{1... | collective-permute-start | bytes 393224 | tf_op jit(solution)/shard_map/ppermute | solution.py:368
  116.0 11.7 %collective-permute-start.19 = (bf16[64,1024]{1,0:T(8,128)(2,1)S(1)}, bf16[64,1024]{1,0:T(8,128)(2,1)S(1)}, u32[]{:S(2)}, u32[]{:S(2)}) collective-permute-start(bf16[64,1024]{1,0:T(8,128)(2,1)S(1)} %collective-permute-done.15.refs_2_), channel_id=1, source_target_pairs={{0,16},{16,0},{32,48},{48,32},{64,80},{80,64},{96,112},{112,96},{1... | collective-permute-start | bytes 393224 | tf_op jit(solution)/shard_map/ppermute | solution.py:364
  121.8 5.9 %collective-permute-start.20 = (bf16[64,1024]{1,0:T(8,128)(2,1)S(1)}, bf16[64,1024]{1,0:T(8,128)(2,1)S(1)}, u32[]{:S(2)}, u32[]{:S(2)}) collective-permute-start(bf16[64,1024]{1,0:T(8,128)(2,1)S(1)} %collective-permute-done.16.refs_3_), channel_id=1, source_target_pairs={{0,16},{16,0},{32,48},{48,32},{64,80},{80,64},{96,112},{112,96},{1... | collective-permute-start | bytes 393224 | tf_op jit(solution)/shard_map/ppermute | solution.py:364
  122.3 6.4 %collective-permute-start.21 = (bf16[64,1024]{1,0:T(8,128)(2,1)S(1)}, bf16[64,1024]{1,0:T(8,128)(2,1)S(1)}, u32[]{:S(2)}, u32[]{:S(2)}) collective-permute-start(bf16[64,1024]{1,0:T(8,128)(2,1)S(1)} %collective-permute-done.17.refs_4_), channel_id=1, source_target_pairs={{0,16},{16,0},{32,48},{48,32},{64,80},{80,64},{96,112},{112,96},{1... | collective-permute-start | bytes 393224 | tf_op jit(solution)/shard_map/ppermute | solution.py:364
  127.7 1.3 collective-permute-start.22
  172.1 6.5 %collective-permute-start.23 = (bf16[512,128]{1,0:T(8,128)(2,1)S(1)}, bf16[512,128]{1,0:T(8,128)(2,1)S(1)}, u32[]{:S(2)}, u32[]{:S(2)}) collective-permute-start(bf16[512,128]{1,0:T(8,128)(2,1)S(1)} %attention.3.refs_0_), channel_id=1, source_target_pairs={{0,2},{2,0},{4,6},{6,4},{8,10},{10,8},{12,14},{14,12},{1,3},{3,1},... | collective-permute-start | bytes 393224 | tf_op jit(solution)/shard_map/ppermute | solution.py:374
  173.3 6.3 %collective-permute-start.24 = (bf16[512,128]{1,0:T(8,128)(2,1)S(1)}, bf16[512,128]{1,0:T(8,128)(2,1)S(1)}, u32[]{:S(2)}, u32[]{:S(2)}) collective-permute-start(bf16[512,128]{1,0:T(8,128)(2,1)S(1)} %attention.3.refs_0_), channel_id=1, source_target_pairs={{0,4},{2,6},{4,0},{6,2},{8,12},{10,14},{12,8},{14,10},{1,5},{3,7},... | collective-permute-start | bytes 393224 | tf_op jit(solution)/shard_map/ppermute | solution.py:374
  173.7 7.7 %collective-permute-start.25 = (bf16[512,128]{1,0:T(8,128)(2,1)S(1)}, bf16[512,128]{1,0:T(8,128)(2,1)S(1)}, u32[]{:S(2)}, u32[]{:S(2)}) collective-permute-start(bf16[512,128]{1,0:T(8,128)(2,1)S(1)} %attention.3.refs_0_), channel_id=1, source_target_pairs={{0,6},{2,4},{4,2},{6,0},{8,14},{10,12},{12,10},{14,8},{1,7},{3,5},... | collective-permute-start | bytes 393224 | tf_op jit(solution)/shard_map/ppermute | solution.py:374
  174.8 12.7 %collective-permute-start.26 = (bf16[512,128]{1,0:T(8,128)(2,1)S(1)}, bf16[512,128]{1,0:T(8,128)(2,1)S(1)}, u32[]{:S(2)}, u32[]{:S(2)}) collective-permute-start(bf16[512,128]{1,0:T(8,128)(2,1)S(1)} %attention.3.refs_0_), channel_id=1, source_target_pairs={{0,8},{2,10},{4,12},{6,14},{8,0},{10,2},{12,4},{14,6},{1,9},{3,11}... | collective-permute-start | bytes 393224 | tf_op jit(solution)/shard_map/ppermute | solution.py:374
  176.1 11.5 %collective-permute-start.27 = (bf16[512,128]{1,0:T(8,128)(2,1)S(1)}, bf16[512,128]{1,0:T(8,128)(2,1)S(1)}, u32[]{:S(2)}, u32[]{:S(2)}) collective-permute-start(bf16[512,128]{1,0:T(8,128)(2,1)S(1)} %attention.3.refs_0_), channel_id=1, source_target_pairs={{0,10},{2,8},{4,14},{6,12},{8,2},{10,0},{12,6},{14,4},{1,11},{3,9}... | collective-permute-start | bytes 393224 | tf_op jit(solution)/shard_map/ppermute | solution.py:374
  178.6 12.0 %collective-permute-start.28 = (bf16[512,128]{1,0:T(8,128)(2,1)S(1)}, bf16[512,128]{1,0:T(8,128)(2,1)S(1)}, u32[]{:S(2)}, u32[]{:S(2)}) collective-permute-start(bf16[512,128]{1,0:T(8,128)(2,1)S(1)} %attention.3.refs_0_), channel_id=1, source_target_pairs={{0,12},{2,14},{4,8},{6,10},{8,4},{10,6},{12,0},{14,2},{1,13},{3,15... | collective-permute-start | bytes 393224 | tf_op jit(solution)/shard_map/ppermute | solution.py:374
  179.6 11.0 %collective-permute-start.29 = (bf16[512,128]{1,0:T(8,128)(2,1)S(1)}, bf16[512,128]{1,0:T(8,128)(2,1)S(1)}, u32[]{:S(2)}, u32[]{:S(2)}) collective-permute-start(bf16[512,128]{1,0:T(8,128)(2,1)S(1)} %attention.3.refs_0_), channel_id=1, source_target_pairs={{0,14},{2,12},{4,10},{6,8},{8,6},{10,4},{12,2},{14,0},{1,15},{3,13... | collective-permute-start | bytes 393224 | tf_op jit(solution)/shard_map/ppermute | solution.py:374
  191.3 4.4 %collective-permute-start.30 = (bf16[256,1024]{1,0:T(8,128)(2,1)S(1)}, bf16[256,1024]{1,0:T(8,128)(2,1)S(1)}, u32[]{:S(2)}, u32[]{:S(2)}) collective-permute-start(bf16[256,1024]{1,0:T(8,128)(2,1)S(1)} %get-tuple-element.32.send_ref), channel_id=1, source_target_pairs={{0,16},{16,0},{32,48},{48,32},{64,80},{80,64},{96,112},{112,96},{1... | collective-permute-start | bytes 1572872 | tf_op jit(solution)/shard_map/ppermute | solution.py:364
  196.9 5.0 %collective-permute-start.32 = (bf16[64,1024]{1,0:T(8,128)(2,1)}, bf16[64,1024]{1,0:T(8,128)(2,1)}, u32[]{:S(2)}, u32[]{:S(2)}) collective-permute-start(bf16[64,1024]{1,0:T(8,128)(2,1)} %get-tuple-element.33), channel_id=1, source_target_pairs={{0,32},{16,48},{32,0},{48,16},{64,96},{80,112},{96,64},{112,80},{1... | collective-permute-start | bytes 393224 | tf_op jit(solution)/shard_map/ppermute | solution.py:368
  198.2 5.6 %collective-permute-start.33 = (bf16[64,1024]{1,0:T(8,128)(2,1)S(1)}, bf16[64,1024]{1,0:T(8,128)(2,1)}, u32[]{:S(2)}, u32[]{:S(2)}) collective-permute-start(bf16[64,1024]{1,0:T(8,128)(2,1)S(1)} %get-tuple-element.34), channel_id=1, source_target_pairs={{0,64},{16,80},{32,96},{48,112},{64,0},{80,16},{96,32},{112,48},{1... | collective-permute-start | bytes 393224 | tf_op jit(solution)/shard_map/ppermute | solution.py:368
  199.7 10.2 %collective-permute-start.34 = (bf16[64,1024]{1,0:T(8,128)(2,1)S(1)}, bf16[64,1024]{1,0:T(8,128)(2,1)}, u32[]{:S(2)}, u32[]{:S(2)}) collective-permute-start(bf16[64,1024]{1,0:T(8,128)(2,1)S(1)} %get-tuple-element.35), channel_id=1, source_target_pairs={{0,96},{16,112},{32,64},{48,80},{64,32},{80,48},{96,0},{112,16},{1... | collective-permute-start | bytes 393224 | tf_op jit(solution)/shard_map/ppermute | solution.py:368
  200.7 27.2 %collective-permute-start.31 = (bf16[256,1024]{1,0:T(8,128)(2,1)S(1)}, bf16[256,1024]{1,0:T(8,128)(2,1)S(1)}, u32[]{:S(2)}, u32[]{:S(2)}) collective-permute-start(bf16[256,1024]{1,0:T(8,128)(2,1)S(1)} %get-tuple-element.31.keep_ref), channel_id=1, source_target_pairs={{0,16},{16,0},{32,48},{48,32},{64,80},{80,64},{96,112},{112,96},{1... | collective-permute-start | bytes 1572872 | tf_op jit(solution)/shard_map/ppermute | solution.py:364
  211.2 7.1 %collective-permute-start.35 = (bf16[64,1024]{1,0:T(8,128)(2,1)S(1)}, bf16[64,1024]{1,0:T(8,128)(2,1)S(1)}, u32[]{:S(2)}, u32[]{:S(2)}) collective-permute-start(bf16[64,1024]{1,0:T(8,128)(2,1)S(1)} %get-tuple-element.38), channel_id=1, source_target_pairs={{0,32},{16,48},{32,0},{48,16},{64,96},{80,112},{96,64},{112,80},{1... | collective-permute-start | bytes 393224 | tf_op jit(solution)/shard_map/ppermute | solution.py:368
  213.7 6.1 %collective-permute-start.36 = (bf16[64,1024]{1,0:T(8,128)(2,1)S(1)}, bf16[64,1024]{1,0:T(8,128)(2,1)S(1)}, u32[]{:S(2)}, u32[]{:S(2)}) collective-permute-start(bf16[64,1024]{1,0:T(8,128)(2,1)S(1)} %get-tuple-element.39), channel_id=1, source_target_pairs={{0,64},{16,80},{32,96},{48,112},{64,0},{80,16},{96,32},{112,48},{1... | collective-permute-start | bytes 393224 | tf_op jit(solution)/shard_map/ppermute | solution.py:368
  215.3 12.6 %collective-permute-start.37 = (bf16[64,1024]{1,0:T(8,128)(2,1)S(1)}, bf16[64,1024]{1,0:T(8,128)(2,1)S(1)}, u32[]{:S(2)}, u32[]{:S(2)}) collective-permute-start(bf16[64,1024]{1,0:T(8,128)(2,1)S(1)} %get-tuple-element.37), channel_id=1, source_target_pairs={{0,96},{16,112},{32,64},{48,80},{64,32},{80,48},{96,0},{112,16},{1... | collective-permute-start | bytes 393224 | tf_op jit(solution)/shard_map/ppermute | solution.py:368
  216.4 11.5 %collective-permute-start.38 = (bf16[64,1024]{1,0:T(8,128)(2,1)S(1)}, bf16[64,1024]{1,0:T(8,128)(2,1)S(1)}, u32[]{:S(2)}, u32[]{:S(2)}) collective-permute-start(bf16[64,1024]{1,0:T(8,128)(2,1)S(1)} %get-tuple-element.40.refs_0_), channel_id=1, source_target_pairs={{0,16},{16,0},{32,48},{48,32},{64,80},{80,64},{96,112},{112,96},{1... | collective-permute-start | bytes 393224 | tf_op jit(solution)/shard_map/ppermute | solution.py:364
  218.2 9.6 %collective-permute-start.39 = (bf16[64,1024]{1,0:T(8,128)(2,1)S(1)}, bf16[64,1024]{1,0:T(8,128)(2,1)S(1)}, u32[]{:S(2)}, u32[]{:S(2)}) collective-permute-start(bf16[64,1024]{1,0:T(8,128)(2,1)S(1)} %collective-permute-done.35.refs_1_), channel_id=1, source_target_pairs={{0,16},{16,0},{32,48},{48,32},{64,80},{80,64},{96,112},{112,96},{1... | collective-permute-start | bytes 393224 | tf_op jit(solution)/shard_map/ppermute | solution.py:364
  219.9 9.0 %collective-permute-start.40 = (bf16[64,1024]{1,0:T(8,128)(2,1)S(1)}, bf16[64,1024]{1,0:T(8,128)(2,1)S(1)}, u32[]{:S(2)}, u32[]{:S(2)}) collective-permute-start(bf16[64,1024]{1,0:T(8,128)(2,1)S(1)} %collective-permute-done.36.refs_2_), channel_id=1, source_target_pairs={{0,16},{16,0},{32,48},{48,32},{64,80},{80,64},{96,112},{112,96},{1... | collective-permute-start | bytes 393224 | tf_op jit(solution)/shard_map/ppermute | solution.py:364
  227.8 1.3 collective-permute-start.41

commit v3 on v2

--- a/solution.py
+++ b/solution.py
@@ -12,6 +12,8 @@
 CHIPS = 4
 EXTRA = 16
 EPS = 1e-05
+ROUND = (0, 2, 3, 1)
+AWAY = (0, 5, 7, 3, 1, 4, 6, 2)
 SEGMENT = 256
 BF16 = jnp.bfloat16
 F32 = jnp.float32
@@ -153,7 +155,8 @@
         size = rows // (2 * CHIPS)
         for number, piece in enumerate(pieces):
             half = core if number < CHIPS else 1 - core
-            start = (half * CHIPS + jnp.bitwise_xor(chip, number % CHIPS)) * size
+            quarter = jnp.bitwise_xor(chip, ROUND[number % CHIPS] ^ (CHIPS - 1))
+            start = (half * CHIPS + quarter) * size
             place_rows = pl.ds(pl.multiple_of(start, size), size)
             tokens = x_ref[place_rows, :].astype(F32)
             added = tokens + piece[...].astype(F32)
@@ -254,48 +257,41 @@
     )(place, pieces)
 
 
-def project_kernel(passing, place, *refs):
+def project_kernel(keeping, passing, place, *refs):
     refs = list(refs)
     pieces = [refs.pop(0) for _ in range(TP)]
     w_ref = refs.pop(0)
-    old = [refs.pop(0) for _ in range(2)] if passing else None
-    keep_ref, send_ref, side = refs
+    old_ref = refs.pop(0) if passing else None
+    out_ref, side = refs
     me, core, layer = place[0], place[1], place[3]
-    rows, head_dim = pieces[0].shape
-
-    def work():
-        for d in range(TP):
+    rows, head_dim = out_ref.shape[0], pieces[0].shape[1]
+
+    @pl.when(layer == (1 if passing else 0))
+    def _():
+        half = core if keeping else 1 - core
+        inside = pl.ds(pl.multiple_of(half * rows, rows), rows)
+        for d, piece in zip(AWAY, pieces):
             start = pl.multiple_of(jnp.bitwise_xor(me, d) * head_dim, head_dim)
-            side[:, pl.ds(start, head_dim)] = pieces[d][...]
-        for half, target in ((1 - core, send_ref), (core, keep_ref)):
-            place_rows = pl.ds(pl.multiple_of(half * (rows // 2), rows // 2), rows // 2)
-            target[...] = jnp.dot(
-                side[place_rows, :], w_ref[...], preferred_element_type=F32
-            ).astype(BF16)
+            side[:, pl.ds(start, head_dim)] = piece[inside, :]
+        out_ref[...] = jnp.dot(side[...], w_ref[...], preferred_element_type=F32).astype(BF16)
 
     if passing:
-        pl.when(layer == 1)(work)
 
         @pl.when(layer == 0)
         def _():
-            keep_ref[...] = old[0][...]
-            send_ref[...] = old[1][...]
-    else:
-        work()
-
-
-def project(place, pieces, w, old):
+            out_ref[...] = old_ref[...]
+
+
+def project(keeping, place, pieces, w, old):
     rows, head_dim = pieces[0].shape
     columns = w.shape[1]
-    shape = jax.ShapeDtypeStruct((rows // 2, columns), BF16)
-    old = list(old) if old else []
-    return pl.pallas_call(
-        functools.partial(project_kernel, bool(old)),
-        out_shape=[shape] * 2,
+    return pl.pallas_call(
+        functools.partial(project_kernel, keeping, bool(old)),
+        out_shape=jax.ShapeDtypeStruct((rows // 2, columns), BF16),
         in_specs=[SMEM] + [VMEM] * (TP + 1 + len(old)),
-        out_specs=[VMEM] * 2,
-        scratch_shapes=[pltpu.VMEM((rows, TP * head_dim), BF16)],
-        compiler_params=params(24),
+        out_specs=VMEM,
+        scratch_shapes=[pltpu.VMEM((rows // 2, TP * head_dim), BF16)],
+        compiler_params=params(16),
         cost_estimate=cheap(),
         name="project",
     )(place, *pieces, w, *old)
@@ -304,9 +300,9 @@
 def quarters_kernel(place, keep_ref, got_ref, *outs):
     chip = place[2]
     size = outs[0].shape[0]
-    for d in range(CHIPS):
+    for d, out_ref in zip(ROUND, outs):
         rows = pl.ds(pl.multiple_of(jnp.bitwise_xor(chip, d) * size, size), size)
-        outs[d][...] = (keep_ref[rows, :].astype(F32) + got_ref[rows, :].astype(F32)).astype(BF16)
+        out_ref[...] = (keep_ref[rows, :].astype(F32) + got_ref[rows, :].astype(F32)).astype(BF16)
 
 
 def quarters(place, keep, got):
@@ -332,13 +328,13 @@
         (core, own, keep_ref, got_ref),
         (1 - core, others, send_ref, other_keep_ref),
     ):
-        for d in range(CHIPS):
+        for slot, d in enumerate(ROUND):
             start = pl.multiple_of(jnp.bitwise_xor(chip, d) * size, size)
             inside = pl.ds(start, size)
             whole = pl.ds(pl.multiple_of(half * half_rows + start, size), size)
             out_ref[whole, :] = (
                 base_ref[whole, :].astype(F32)
-                + sums[d][...].astype(F32)
+                + sums[slot][...].astype(F32)
                 + mine[inside, :].astype(F32)
                 + second * theirs[inside, :].astype(F32)
             ).astype(BF16)
@@ -369,14 +365,13 @@
 
 
 def spread(value):
-    got = {0: value}
-    for d in (5, 7, 3, 1, 4, 6, 2):
-        got[d] = lax.ppermute(value, "tp", [(t, t ^ d) for t in range(TP)])
-    return [got[d] for d in range(TP)]
+    return [
+        lax.ppermute(value, "tp", [(t, t ^ d) for t in range(TP)]) if d else value for d in AWAY
+    ]
 
 
 def over_layer(values):
-    return [values[0]] + [over_chips(values[d], d) for d in range(1, CHIPS)]
+    return [over_chips(value, d) if d else value for d, value in zip(ROUND, values)]
 
 
 def on_device(tokens, ln_gain, ln_bias, w_qkv, w_out):
@@ -398,26 +393,30 @@
 
     _, part = qkv(place, tokens, [], even, odd, weight_in)
     out = attention(place, over_tp(part), features, 0)
-    kept = project(place, spread(out), weight_back, None)
-    keep, send = kept
-    arrived = over_layer(quarters(place, keep, over_cores(send)))
+    heads = spread(out)
+    send = project(False, place, heads, weight_back, [])
+    got = over_cores(send)
+    keep = project(True, place, heads, weight_back, [])
+    arrived = over_layer(quarters(place, keep, got))
     total = sum(value.astype(F32) for value in arrived).astype(BF16)
-    own = over_layer([over_chips(total, CHIPS)] * CHIPS)
+    own = over_layer([over_chips(total, 2 * CHIPS - 1)] * CHIPS)
     others = [over_cores(value) for value in own]
 
     base, part = qkv(place, tokens, own + others, even, odd, weight_in)
     out = attention(place, over_tp(part), features, 1)
-    keep, send = project(place, spread(out), weight_back, kept)
+    heads = spread(out)
+    send = project(False, place, heads, weight_back, [send])
     got = over_cores(send)
+    keep = project(True, place, heads, weight_back, [keep])
     other_keep = over_cores(keep)
     arrived = over_layer(quarters(place, keep, got))
     before = []
-    for d in range(CHIPS):
+    for d in ROUND:
         target = jnp.bitwise_xor(chip, d)
         before.append(
             sum(
-                jnp.where(jnp.bitwise_xor(chip, e) < target, arrived[e].astype(F32), 0.0)
-                for e in range(CHIPS)
+                jnp.where(jnp.bitwise_xor(chip, e) < target, value.astype(F32), 0.0)
+                for e, value in zip(ROUND, arrived)
             ).astype(BF16)
         )
     own = over_layer(before)

time: 232 us -> 220 us (0.948)
  starting transfers between devices: 78 us -> 70.2 us
  waiting for transfers between devices: 45.6 us -> 40.3 us
    ppermute x12, starting transfers between devices: 34.6 us -> 27.8 us  [over_cores(): return lax.ppermute(value, 'section', [(s, s ^ 1) for s in range(2 * SPAN)])]
    ppermute x12, waiting for transfers between devices: 6.56 us -> 3.82 us  [over_cores(): return lax.ppermute(value, 'section', [(s, s ^ 1) for s in range(2 * SPAN)])]
  transfers between devices with their start and end apart: 42 -> 42, of which waited for: 17 -> 20; matrix products, arithmetic and copies ran while one was open for 1% -> 1% of each run, Pallas kernels for 0% -> 1%
where the time goes in v3:
time: 220 us; the launch traced here: 219 us
  blocking collectives  84.8 us (39%)
  starting transfers between devices  70.2 us (32%)
  waiting for transfers between devices  40.3 us (18%)
  Pallas kernels  17.6 us (8%)
  local copies, waits for them, and re-layouts  4.01 us (2%)
    all_to_all x2, blocking collectives, over_tp(): return lax.all_to_all(value, 'tp', 0, 0, tiled=True)  84.8 us
    ppermute x12, starting transfers between devices, over_cores(): return lax.ppermute(value, 'section', [(s, s ^ 1) for s in range(2 * SPAN)])  27.8 us
    ppermute x16, starting transfers between devices, over_chips(): lax.ppermute(value, 'section', [(s, s ^ 2 * d) for s in range(2 * SPAN)])  24.1 us
    ppermute x16, waiting for transfers between devices, over_chips(): lax.ppermute(value, 'section', [(s, s ^ 2 * d) for s in range(2 * SPAN)])  22.1 us
    ppermute x14, starting transfers between devices, spread(): lax.ppermute(value, 'tp', [(t, t ^ d) for t in range(TP)])  18.4 us
    ppermute x14, waiting for transfers between devices, spread(): lax.ppermute(value, 'tp', [(t, t ^ d) for t in range(TP)])  14.4 us
    pallas_call x2, Pallas kernels, qkv(): pl.pallas_call(functools.partial(qkv_kernel, bool(pieces)), out_shape=sha...  5.31 us
  transfers between devices with their start and end apart: 42, of which 20 were waited for; matrix products, arithmetic and copies ran while one was open for 1% of the time, Pallas kernels for 1%

profile of v3, /device:TPU:1, one launch (start us, length us, event | category | flops | bytes accessed | tf_op | source)
XLA Modules:
  0.0 219.3 jit_solution(7722644389489682355)
XLA Ops:
  0.0 0.7 pad_maximum_fusion.own_ref
  0.7 2.6 %collective-permute-start = (f32[2,1024]{1,0:T(2,128)S(1)}, f32[2,1024]{1,0:T(2,128)S(1)}, u32[]{:S(2)}, u32[]{:S(2)}) collective-permute-start(f32[2,1024]{1,0:T(2,128)S(1)} %pad_maximum_fusion.own_ref), channel_id=1, source_target_pairs={{0,32},{16,48},{32,0},{48,16},{64,96},{80,112},{96,64},{112,80},{1... | collective-permute-start | bytes 24584 | tf_op jit(solution)/shard_map/ppermute | solution.py:364
  3.3 3.0 %collective-permute-start.1 = (f32[2,1024]{1,0:T(2,128)S(1)}, f32[2,1024]{1,0:T(2,128)S(1)}, u32[]{:S(2)}, u32[]{:S(2)}) collective-permute-start(f32[2,1024]{1,0:T(2,128)S(1)} %pad_maximum_fusion.own_ref), channel_id=1, source_target_pairs={{0,64},{16,80},{32,96},{48,112},{64,0},{80,16},{96,32},{112,48},{1... | collective-permute-start | bytes 24584 | tf_op jit(solution)/shard_map/ppermute | solution.py:364
  6.3 2.8 %copy-done.1 = bf16[1,8,1024,384]{3,2,1,0:T(8,128)(2,1)S(1)} copy-done((bf16[1,8,1024,384]{3,2,1,0:T(8,128)(2,1)S(1)}, bf16[1,8,1024,384]{3,2,1,0:T(8,128)(2,1)}, u32[]{:S(2)}) %copy-start.1) | copy-done | bytes 6291480
  9.1 1.2 copy-done.2
  10.4 0.5 stage.1
  10.9 0.6 pick.1.refs_2_.refs_10_
  11.5 2.3 %collective-permute-start.3 = (f32[2,1024]{1,0:T(2,128)S(1)}, f32[2,1024]{1,0:T(2,128)S(1)}, u32[]{:S(2)}, u32[]{:S(2)}) collective-permute-start(f32[2,1024]{1,0:T(2,128)S(1)} %pick.1.refs_2_.refs_10_), channel_id=1, source_target_pairs={{0,16},{16,0},{32,48},{48,32},{64,80},{80,64},{96,112},{112,96},{1... | collective-permute-start | bytes 24584 | tf_op jit(solution)/shard_map/ppermute | solution.py:360
  13.7 0.8 collective-permute-done.3.refs_3_.refs_11_
  14.5 4.5 %qkv.2 = bf16[8,528,384]{2,1,0:T(8,128)(2,1)S(1)} custom-call(s32[4]{0:T(128)S(1)} %pad_add_fusion.place.refs_0_, bf16[512,1024]{1,0:T(8,128)(2,1)S(1)} %get-tuple-element.17.refs_1_, f32[2,1024]{1,0:T(2,128)S(1)} %pick.1.refs_2_.refs_10_, f32[2,1024]{1,0:T(2,128)S(1)} %collective-permute-done.3.refs_3_.refs_11_, ...), custom_call_target="tpu_custom_call" | custom-call | flops 1 | bytes 1 | tf_op jit(solution)/shard_map/qkv/pallas_call | solution.py:211
  19.0 43.5 %all_to_all.10.pieces_ref = bf16[8,528,384]{2,1,0:T(8,128)(2,1)S(1)} all-to-all(bf16[8,528,384]{2,1,0:T(8,128)(2,1)S(1)} %qkv.2), channel_id=1, replica_groups=mesh['section'=16,'tp'=8,'dp'=2] {'tp'}, dimensions={0} | all-to-all | bytes 6488064 | tf_op jit(solution)/shard_map/all_to_all | solution.py:356
  62.5 2.6 %attention.2.refs_0_ = bf16[512,128]{1,0:T(8,128)(2,1)S(1)} custom-call(s32[4]{0:T(128)S(1)} %pad_add_fusion.place.refs_0_, bf16[8,528,384]{2,1,0:T(8,128)(2,1)S(1)} %all_to_all.10.pieces_ref), custom_call_target="tpu_custom_call" | custom-call | flops 1 | bytes 1 | tf_op jit(solution)/shard_map/attention/pallas_call | solution.py:249
  65.2 2.7 %collective-permute-start.4 = (bf16[512,128]{1,0:T(8,128)(2,1)S(1)}, bf16[512,128]{1,0:T(8,128)(2,1)S(1)}, u32[]{:S(2)}, u32[]{:S(2)}) collective-permute-start(bf16[512,128]{1,0:T(8,128)(2,1)S(1)} %attention.2.refs_0_), channel_id=1, source_target_pairs={{0,10},{2,8},{4,14},{6,12},{8,2},{10,0},{12,6},{14,4},{1,11},{3,9}... | collective-permute-start | bytes 393224 | tf_op jit(solution)/shard_map/ppermute | solution.py:369
  68.0 2.0 collective-permute-start.5
  69.9 1.0 collective-permute-start.7
  70.9 2.1 collective-permute-start.8
  73.0 2.0 collective-permute-start.9
  75.1 1.3 collective-permute-done.6.refs_3_
  76.4 4.1 %collective-permute-done.7.refs_4_ = bf16[512,128]{1,0:T(8,128)(2,1)S(1)} collective-permute-done((bf16[512,128]{1,0:T(8,128)(2,1)S(1)}, bf16[512,128]{1,0:T(8,128)(2,1)S(1)}, u32[]{:S(2)}, u32[]{:S(2)}) %collective-permute-start.7) | collective-permute-done | bytes 131104 | tf_op jit(solution)/shard_map/ppermute | solution.py:369
  80.6 1.4 collective-permute-done.9.refs_6_
  82.0 1.4 project.5.refs_9_
  83.4 1.3 collective-permute-start.11
  84.7 1.6 project.4.keep_ref.refs_9_
  86.3 0.7 quarters.2
  87.0 0.6 collective-permute-start.12
  87.5 2.3 %collective-permute-start.13 = (bf16[64,1024]{1,0:T(8,128)(2,1)S(1)}, bf16[64,1024]{1,0:T(8,128)(2,1)S(1)}, u32[]{:S(2)}, u32[]{:S(2)}) collective-permute-start(bf16[64,1024]{1,0:T(8,128)(2,1)S(1)} %get-tuple-element.21), channel_id=1, source_target_pairs={{0,96},{16,112},{32,64},{48,80},{64,32},{80,48},{96,0},{112,16},{1... | collective-permute-start | bytes 393224 | tf_op jit(solution)/shard_map/ppermute | solution.py:364
  90.1 8.6 %collective-permute-done.12 = bf16[64,1024]{1,0:T(8,128)(2,1)S(1)} collective-permute-done((bf16[64,1024]{1,0:T(8,128)(2,1)S(1)}, bf16[64,1024]{1,0:T(8,128)(2,1)S(1)}, u32[]{:S(2)}, u32[]{:S(2)}) %collective-permute-start.12) | collective-permute-done | bytes 131104 | tf_op jit(solution)/shard_map/ppermute | solution.py:364
  98.7 0.8 collective-permute-done.14
  99.7 5.0 %collective-permute-done.15.refs_2_ = bf16[64,1024]{1,0:T(8,128)(2,1)S(1)} collective-permute-done((bf16[64,1024]{1,0:T(8,128)(2,1)S(1)}, bf16[64,1024]{1,0:T(8,128)(2,1)S(1)}, u32[]{:S(2)}, u32[]{:S(2)}) %collective-permute-start.15) | collective-permute-done | bytes 131104 | tf_op jit(solution)/shard_map/ppermute | solution.py:364
  104.7 5.5 %collective-permute-start.16 = (bf16[64,1024]{1,0:T(8,128)(2,1)S(1)}, bf16[64,1024]{1,0:T(8,128)(2,1)S(1)}, u32[]{:S(2)}, u32[]{:S(2)}) collective-permute-start(bf16[64,1024]{1,0:T(8,128)(2,1)S(1)} %collective-permute-done.15.refs_2_), channel_id=1, source_target_pairs={{0,64},{16,80},{32,96},{48,112},{64,0},{80,16},{96,32},{112,48},{1... | collective-permute-start | bytes 393224 | tf_op jit(solution)/shard_map/ppermute | solution.py:364
  110.2 1.1 collective-permute-start.17
  111.3 2.3 %collective-permute-start.19 = (bf16[64,1024]{1,0:T(8,128)(2,1)S(1)}, bf16[64,1024]{1,0:T(8,128)(2,1)S(1)}, u32[]{:S(2)}, u32[]{:S(2)}) collective-permute-start(bf16[64,1024]{1,0:T(8,128)(2,1)S(1)} %collective-permute-done.15.refs_2_), channel_id=1, source_target_pairs={{0,16},{16,0},{32,48},{48,32},{64,80},{80,64},{96,112},{112,96},{1... | collective-permute-start | bytes 393224 | tf_op jit(solution)/shard_map/ppermute | solution.py:360
  114.0 7.6 %collective-permute-start.20 = (bf16[64,1024]{1,0:T(8,128)(2,1)S(1)}, bf16[64,1024]{1,0:T(8,128)(2,1)S(1)}, u32[]{:S(2)}, u32[]{:S(2)}) collective-permute-start(bf16[64,1024]{1,0:T(8,128)(2,1)S(1)} %collective-permute-done.16.refs_3_), channel_id=1, source_target_pairs={{0,16},{16,0},{32,48},{48,32},{64,80},{80,64},{96,112},{112,96},{1... | collective-permute-start | bytes 393224 | tf_op jit(solution)/shard_map/ppermute | solution.py:360
  121.6 0.5 collective-permute-start.22
  122.1 0.5 collective-permute-done.20.refs_7_
  123.2 0.8 qkv.3
  124.0 41.3 %all_to_all.11.pieces_ref = bf16[8,528,384]{2,1,0:T(8,128)(2,1)S(1)} all-to-all(bf16[8,528,384]{2,1,0:T(8,128)(2,1)S(1)} %get-tuple-element.24), channel_id=1, replica_groups=mesh['section'=16,'tp'=8,'dp'=2] {'tp'}, dimensions={0} | all-to-all | bytes 6488064 | tf_op jit(solution)/shard_map/all_to_all | solution.py:356
  165.4 0.5 attention.3.refs_0_
  165.9 1.2 collective-permute-start.23
  167.2 2.2 %collective-permute-start.24 = (bf16[512,128]{1,0:T(8,128)(2,1)S(1)}, bf16[512,128]{1,0:T(8,128)(2,1)S(1)}, u32[]{:S(2)}, u32[]{:S(2)}) collective-permute-start(bf16[512,128]{1,0:T(8,128)(2,1)S(1)} %attention.3.refs_0_), channel_id=1, source_target_pairs={{0,14},{2,12},{4,10},{6,8},{8,6},{10,4},{12,2},{14,0},{1,15},{3,13... | collective-permute-start | bytes 393224 | tf_op jit(solution)/shard_map/ppermute | solution.py:369
  169.4 0.9 collective-permute-start.25
  170.2 0.5 collective-permute-start.26
  170.7 2.1 collective-permute-start.27
  172.9 1.5 collective-permute-start.28
  174.4 2.5 %collective-permute-done.25.refs_3_ = bf16[512,128]{1,0:T(8,128)(2,1)S(1)} collective-permute-done((bf16[512,128]{1,0:T(8,128)(2,1)S(1)}, bf16[512,128]{1,0:T(8,128)(2,1)S(1)}, u32[]{:S(2)}, u32[]{:S(2)}) %collective-permute-start.25) | collective-permute-done | bytes 131104 | tf_op jit(solution)/shard_map/ppermute | solution.py:369
  177.0 3.3 %collective-permute-done.26.refs_4_ = bf16[512,128]{1,0:T(8,128)(2,1)S(1)} collective-permute-done((bf16[512,128]{1,0:T(8,128)(2,1)S(1)}, bf16[512,128]{1,0:T(8,128)(2,1)S(1)}, u32[]{:S(2)}, u32[]{:S(2)}) %collective-permute-start.26) | collective-permute-done | bytes 131104 | tf_op jit(solution)/shard_map/ppermute | solution.py:369
  180.3 1.5 collective-permute-done.28.refs_6_
  181.8 0.6 project.7.send_ref
  182.4 2.7 %collective-permute-start.30 = (bf16[256,1024]{1,0:T(8,128)(2,1)S(1)}, bf16[256,1024]{1,0:T(8,128)(2,1)S(1)}, u32[]{:S(2)}, u32[]{:S(2)}) collective-permute-start(bf16[256,1024]{1,0:T(8,128)(2,1)S(1)} %project.7.send_ref), channel_id=1, source_target_pairs={{0,16},{16,0},{32,48},{48,32},{64,80},{80,64},{96,112},{112,96},{1... | collective-permute-start | bytes 1572872 | tf_op jit(solution)/shard_map/ppermute | solution.py:360
  185.1 0.6 project.6.keep_ref
  185.7 0.9 collective-permute-done.30.got_ref
  186.7 1.2 quarters.3
  187.9 1.3 collective-permute-start.32
  189.2 2.1 collective-permute-start.33
  191.3 0.9 collective-permute-start.31
  192.3 7.2 %collective-permute-done.32 = bf16[64,1024]{1,0:T(8,128)(2,1)} collective-permute-done((bf16[64,1024]{1,0:T(8,128)(2,1)}, bf16[64,1024]{1,0:T(8,128)(2,1)}, u32[]{:S(2)}, u32[]{:S(2)}) %collective-permute-start.32) | collective-permute-done | bytes 131104 | tf_op jit(solution)/shard_map/ppermute | solution.py:364
  199.5 1.3 fusion.8
  200.8 3.4 %collective-permute-start.35 = (bf16[64,1024]{1,0:T(8,128)(2,1)S(1)}, bf16[64,1024]{1,0:T(8,128)(2,1)S(1)}, u32[]{:S(2)}, u32[]{:S(2)}) collective-permute-start(bf16[64,1024]{1,0:T(8,128)(2,1)S(1)} %get-tuple-element.30), channel_id=1, source_target_pairs={{0,64},{16,80},{32,96},{48,112},{64,0},{80,16},{96,32},{112,48},{1... | collective-permute-start | bytes 393224 | tf_op jit(solution)/shard_map/ppermute | solution.py:364
  204.1 1.9 collective-permute-start.36
  206.0 1.8 collective-permute-start.38
  207.8 7.9 %collective-permute-start.39 = (bf16[64,1024]{1,0:T(8,128)(2,1)S(1)}, bf16[64,1024]{1,0:T(8,128)(2,1)S(1)}, u32[]{:S(2)}, u32[]{:S(2)}) collective-permute-start(bf16[64,1024]{1,0:T(8,128)(2,1)S(1)} %collective-permute-done.35.refs_1_), channel_id=1, source_target_pairs={{0,16},{16,0},{32,48},{48,32},{64,80},{80,64},{96,112},{112,96},{1... | collective-permute-start | bytes 393224 | tf_op jit(solution)/shard_map/ppermute | solution.py:360
  215.7 0.5 collective-permute-start.41
  216.2 0.5 collective-permute-done.39.refs_5_
  217.2 2.1 finish.1
  (45 shorter events, 2.3 us)
Async XLA Ops:
  0.7 10.2 %collective-permute-start = (f32[2,1024]{1,0:T(2,128)S(1)}, f32[2,1024]{1,0:T(2,128)S(1)}, u32[]{:S(2)}, u32[]{:S(2)}) collective-permute-start(f32[2,1024]{1,0:T(2,128)S(1)} %pad_maximum_fusion.own_ref), channel_id=1, source_target_pairs={{0,32},{16,48},{32,0},{48,16},{64,96},{80,112},{96,64},{112,80},{1... | collective-permute-start | bytes 24584 | tf_op jit(solution)/shard_map/ppermute | solution.py:364
  3.3 7.6 %collective-permute-start.1 = (f32[2,1024]{1,0:T(2,128)S(1)}, f32[2,1024]{1,0:T(2,128)S(1)}, u32[]{:S(2)}, u32[]{:S(2)}) collective-permute-start(f32[2,1024]{1,0:T(2,128)S(1)} %pad_maximum_fusion.own_ref), channel_id=1, source_target_pairs={{0,64},{16,80},{32,96},{48,112},{64,0},{80,16},{96,32},{112,48},{1... | collective-permute-start | bytes 24584 | tf_op jit(solution)/shard_map/ppermute | solution.py:364
  6.3 4.6 %collective-permute-start.2 = (f32[2,1024]{1,0:T(2,128)S(1)}, f32[2,1024]{1,0:T(2,128)S(1)}, u32[]{:S(2)}, u32[]{:S(2)}) collective-permute-start(f32[2,1024]{1,0:T(2,128)S(1)} %pad_maximum_fusion.own_ref), channel_id=1, source_target_pairs={{0,96},{16,112},{32,64},{48,80},{64,32},{80,48},{96,0},{112,16},{1... | collective-permute-start | bytes 24584 | tf_op jit(solution)/shard_map/ppermute | solution.py:364
  6.3 2.8 %copy-start.1 = (bf16[1,8,1024,384]{3,2,1,0:T(8,128)(2,1)S(1)}, bf16[1,8,1024,384]{3,2,1,0:T(8,128)(2,1)}, u32[]{:S(2)}) copy-start(bf16[1,8,1024,384]{3,2,1,0:T(8,128)(2,1)} %param.8) | copy-start | bytes 18874372
  9.1 1.2 copy-start.2
  11.5 3.1 %collective-permute-start.3 = (f32[2,1024]{1,0:T(2,128)S(1)}, f32[2,1024]{1,0:T(2,128)S(1)}, u32[]{:S(2)}, u32[]{:S(2)}) collective-permute-start(f32[2,1024]{1,0:T(2,128)S(1)} %pick.1.refs_2_.refs_10_), channel_id=1, source_target_pairs={{0,16},{16,0},{32,48},{48,32},{64,80},{80,64},{96,112},{112,96},{1... | collective-permute-start | bytes 24584 | tf_op jit(solution)/shard_map/ppermute | solution.py:360
  62.5 19.5 %copy-start = (bf16[1,1024,1024]{2,1,0:T(8,128)(2,1)S(1)}, bf16[1,1024,1024]{2,1,0:T(8,128)(2,1)}, u32[]{:S(2)}) copy-start(bf16[1,1024,1024]{2,1,0:T(8,128)(2,1)} %param.9) | copy-start | bytes 6291460
  65.1 5.8 %collective-permute-start.10 = (bf16[512,128]{1,0:T(8,128)(2,1)S(1)}, bf16[512,128]{1,0:T(8,128)(2,1)S(1)}, u32[]{:S(2)}, u32[]{:S(2)}) collective-permute-start(bf16[512,128]{1,0:T(8,128)(2,1)S(1)} %attention.2.refs_0_), channel_id=1, source_target_pairs={{0,4},{2,6},{4,0},{6,2},{8,12},{10,14},{12,8},{14,10},{1,5},{3,7},... | collective-permute-start | bytes 393224 | tf_op jit(solution)/shard_map/ppermute | solution.py:369
  65.2 7.7 %collective-permute-start.4 = (bf16[512,128]{1,0:T(8,128)(2,1)S(1)}, bf16[512,128]{1,0:T(8,128)(2,1)S(1)}, u32[]{:S(2)}, u32[]{:S(2)}) collective-permute-start(bf16[512,128]{1,0:T(8,128)(2,1)S(1)} %attention.2.refs_0_), channel_id=1, source_target_pairs={{0,10},{2,8},{4,14},{6,12},{8,2},{10,0},{12,6},{14,4},{1,11},{3,9}... | collective-permute-start | bytes 393224 | tf_op jit(solution)/shard_map/ppermute | solution.py:369
  68.0 7.1 %collective-permute-start.5 = (bf16[512,128]{1,0:T(8,128)(2,1)S(1)}, bf16[512,128]{1,0:T(8,128)(2,1)S(1)}, u32[]{:S(2)}, u32[]{:S(2)}) collective-permute-start(bf16[512,128]{1,0:T(8,128)(2,1)S(1)} %attention.2.refs_0_), channel_id=1, source_target_pairs={{0,14},{2,12},{4,10},{6,8},{8,6},{10,4},{12,2},{14,0},{1,15},{3,13... | collective-permute-start | bytes 393224 | tf_op jit(solution)/shard_map/ppermute | solution.py:369
  69.9 6.5 %collective-permute-start.6 = (bf16[512,128]{1,0:T(8,128)(2,1)S(1)}, bf16[512,128]{1,0:T(8,128)(2,1)S(1)}, u32[]{:S(2)}, u32[]{:S(2)}) collective-permute-start(bf16[512,128]{1,0:T(8,128)(2,1)S(1)} %attention.2.refs_0_), channel_id=1, source_target_pairs={{0,6},{2,4},{4,2},{6,0},{8,14},{10,12},{12,10},{14,8},{1,7},{3,5},... | collective-permute-start | bytes 393224 | tf_op jit(solution)/shard_map/ppermute | solution.py:369
  69.9 10.6 %collective-permute-start.7 = (bf16[512,128]{1,0:T(8,128)(2,1)S(1)}, bf16[512,128]{1,0:T(8,128)(2,1)S(1)}, u32[]{:S(2)}, u32[]{:S(2)}) collective-permute-start(bf16[512,128]{1,0:T(8,128)(2,1)S(1)} %attention.2.refs_0_), channel_id=1, source_target_pairs={{0,2},{2,0},{4,6},{6,4},{8,10},{10,8},{12,14},{14,12},{1,3},{3,1},... | collective-permute-start | bytes 393224 | tf_op jit(solution)/shard_map/ppermute | solution.py:369
  70.9 9.7 %collective-permute-start.8 = (bf16[512,128]{1,0:T(8,128)(2,1)S(1)}, bf16[512,128]{1,0:T(8,128)(2,1)S(1)}, u32[]{:S(2)}, u32[]{:S(2)}) collective-permute-start(bf16[512,128]{1,0:T(8,128)(2,1)S(1)} %attention.2.refs_0_), channel_id=1, source_target_pairs={{0,8},{2,10},{4,12},{6,14},{8,0},{10,2},{12,4},{14,6},{1,9},{3,11}... | collective-permute-start | bytes 393224 | tf_op jit(solution)/shard_map/ppermute | solution.py:369
  73.0 9.0 %collective-permute-start.9 = (bf16[512,128]{1,0:T(8,128)(2,1)S(1)}, bf16[512,128]{1,0:T(8,128)(2,1)S(1)}, u32[]{:S(2)}, u32[]{:S(2)}) collective-permute-start(bf16[512,128]{1,0:T(8,128)(2,1)S(1)} %attention.2.refs_0_), channel_id=1, source_target_pairs={{0,12},{2,14},{4,8},{6,10},{8,4},{10,6},{12,0},{14,2},{1,13},{3,15... | collective-permute-start | bytes 393224 | tf_op jit(solution)/shard_map/ppermute | solution.py:369
  83.4 2.9 %collective-permute-start.11 = (bf16[256,1024]{1,0:T(8,128)(2,1)S(1)}, bf16[256,1024]{1,0:T(8,128)(2,1)S(1)}, u32[]{:S(2)}, u32[]{:S(2)}) collective-permute-start(bf16[256,1024]{1,0:T(8,128)(2,1)S(1)} %project.5.refs_9_), channel_id=1, source_target_pairs={{0,16},{16,0},{32,48},{48,32},{64,80},{80,64},{96,112},{112,96},{1... | collective-permute-start | bytes 1572872 | tf_op jit(solution)/shard_map/ppermute | solution.py:360
  87.0 11.7 %collective-permute-start.12 = (bf16[64,1024]{1,0:T(8,128)(2,1)S(1)}, bf16[64,1024]{1,0:T(8,128)(2,1)S(1)}, u32[]{:S(2)}, u32[]{:S(2)}) collective-permute-start(bf16[64,1024]{1,0:T(8,128)(2,1)S(1)} %get-tuple-element.20), channel_id=1, source_target_pairs={{0,64},{16,80},{32,96},{48,112},{64,0},{80,16},{96,32},{112,48},{1... | collective-permute-start | bytes 393224 | tf_op jit(solution)/shard_map/ppermute | solution.py:364
  87.5 11.2 %collective-permute-start.13 = (bf16[64,1024]{1,0:T(8,128)(2,1)S(1)}, bf16[64,1024]{1,0:T(8,128)(2,1)S(1)}, u32[]{:S(2)}, u32[]{:S(2)}) collective-permute-start(bf16[64,1024]{1,0:T(8,128)(2,1)S(1)} %get-tuple-element.21), channel_id=1, source_target_pairs={{0,96},{16,112},{32,64},{48,80},{64,32},{80,48},{96,0},{112,16},{1... | collective-permute-start | bytes 393224 | tf_op jit(solution)/shard_map/ppermute | solution.py:364
  89.9 9.6 %collective-permute-start.14 = (bf16[64,1024]{1,0:T(8,128)(2,1)S(1)}, bf16[64,1024]{1,0:T(8,128)(2,1)S(1)}, u32[]{:S(2)}, u32[]{:S(2)}) collective-permute-start(bf16[64,1024]{1,0:T(8,128)(2,1)S(1)} %get-tuple-element.22), channel_id=1, source_target_pairs={{0,32},{16,48},{32,0},{48,16},{64,96},{80,112},{96,64},{112,80},{1... | collective-permute-start | bytes 393224 | tf_op jit(solution)/shard_map/ppermute | solution.py:364
  99.6 5.1 %collective-permute-start.15 = (bf16[64,1024]{1,0:T(8,128)(2,1)S(1)}, bf16[64,1024]{1,0:T(8,128)(2,1)S(1)}, u32[]{:S(2)}, u32[]{:S(2)}) collective-permute-start(bf16[64,1024]{1,0:T(8,128)(2,1)S(1)} %add_convert_fusion), channel_id=1, source_target_pairs={{0,224},{16,240},{32,192},{48,208},{64,160},{80,176},{96,128},{112... | collective-permute-start | bytes 393224 | tf_op jit(solution)/shard_map/ppermute | solution.py:364
  104.7 9.3 %collective-permute-start.16 = (bf16[64,1024]{1,0:T(8,128)(2,1)S(1)}, bf16[64,1024]{1,0:T(8,128)(2,1)S(1)}, u32[]{:S(2)}, u32[]{:S(2)}) collective-permute-start(bf16[64,1024]{1,0:T(8,128)(2,1)S(1)} %collective-permute-done.15.refs_2_), channel_id=1, source_target_pairs={{0,64},{16,80},{32,96},{48,112},{64,0},{80,16},{96,32},{112,48},{1... | collective-permute-start | bytes 393224 | tf_op jit(solution)/shard_map/ppermute | solution.py:364
  110.2 11.5 %collective-permute-start.17 = (bf16[64,1024]{1,0:T(8,128)(2,1)S(1)}, bf16[64,1024]{1,0:T(8,128)(2,1)S(1)}, u32[]{:S(2)}, u32[]{:S(2)}) collective-permute-start(bf16[64,1024]{1,0:T(8,128)(2,1)S(1)} %collective-permute-done.15.refs_2_), channel_id=1, source_target_pairs={{0,96},{16,112},{32,64},{48,80},{64,32},{80,48},{96,0},{112,16},{1... | collective-permute-start | bytes 393224 | tf_op jit(solution)/shard_map/ppermute | solution.py:364
  111.3 10.3 %collective-permute-start.18 = (bf16[64,1024]{1,0:T(8,128)(2,1)S(1)}, bf16[64,1024]{1,0:T(8,128)(2,1)S(1)}, u32[]{:S(2)}, u32[]{:S(2)}) collective-permute-start(bf16[64,1024]{1,0:T(8,128)(2,1)S(1)} %collective-permute-done.15.refs_2_), channel_id=1, source_target_pairs={{0,32},{16,48},{32,0},{48,16},{64,96},{80,112},{96,64},{112,80},{1... | collective-permute-start | bytes 393224 | tf_op jit(solution)/shard_map/ppermute | solution.py:364
  111.3 10.8 %collective-permute-start.19 = (bf16[64,1024]{1,0:T(8,128)(2,1)S(1)}, bf16[64,1024]{1,0:T(8,128)(2,1)S(1)}, u32[]{:S(2)}, u32[]{:S(2)}) collective-permute-start(bf16[64,1024]{1,0:T(8,128)(2,1)S(1)} %collective-permute-done.15.refs_2_), channel_id=1, source_target_pairs={{0,16},{16,0},{32,48},{48,32},{64,80},{80,64},{96,112},{112,96},{1... | collective-permute-start | bytes 393224 | tf_op jit(solution)/shard_map/ppermute | solution.py:360
  114.0 8.6 %collective-permute-start.20 = (bf16[64,1024]{1,0:T(8,128)(2,1)S(1)}, bf16[64,1024]{1,0:T(8,128)(2,1)S(1)}, u32[]{:S(2)}, u32[]{:S(2)}) collective-permute-start(bf16[64,1024]{1,0:T(8,128)(2,1)S(1)} %collective-permute-done.16.refs_3_), channel_id=1, source_target_pairs={{0,16},{16,0},{32,48},{48,32},{64,80},{80,64},{96,112},{112,96},{1... | collective-permute-start | bytes 393224 | tf_op jit(solution)/shard_map/ppermute | solution.py:360
  121.6 1.3 collective-permute-start.21
  121.6 1.5 collective-permute-start.22
  165.9 7.0 %collective-permute-start.23 = (bf16[512,128]{1,0:T(8,128)(2,1)S(1)}, bf16[512,128]{1,0:T(8,128)(2,1)S(1)}, u32[]{:S(2)}, u32[]{:S(2)}) collective-permute-start(bf16[512,128]{1,0:T(8,128)(2,1)S(1)} %attention.3.refs_0_), channel_id=1, source_target_pairs={{0,10},{2,8},{4,14},{6,12},{8,2},{10,0},{12,6},{14,4},{1,11},{3,9}... | collective-permute-start | bytes 393224 | tf_op jit(solution)/shard_map/ppermute | solution.py:369
  167.2 7.3 %collective-permute-start.24 = (bf16[512,128]{1,0:T(8,128)(2,1)S(1)}, bf16[512,128]{1,0:T(8,128)(2,1)S(1)}, u32[]{:S(2)}, u32[]{:S(2)}) collective-permute-start(bf16[512,128]{1,0:T(8,128)(2,1)S(1)} %attention.3.refs_0_), channel_id=1, source_target_pairs={{0,14},{2,12},{4,10},{6,8},{8,6},{10,4},{12,2},{14,0},{1,15},{3,13... | collective-permute-start | bytes 393224 | tf_op jit(solution)/shard_map/ppermute | solution.py:369
  169.4 7.6 %collective-permute-start.25 = (bf16[512,128]{1,0:T(8,128)(2,1)S(1)}, bf16[512,128]{1,0:T(8,128)(2,1)S(1)}, u32[]{:S(2)}, u32[]{:S(2)}) collective-permute-start(bf16[512,128]{1,0:T(8,128)(2,1)S(1)} %attention.3.refs_0_), channel_id=1, source_target_pairs={{0,6},{2,4},{4,2},{6,0},{8,14},{10,12},{12,10},{14,8},{1,7},{3,5},... | collective-permute-start | bytes 393224 | tf_op jit(solution)/shard_map/ppermute | solution.py:369
  170.2 10.0 %collective-permute-start.26 = (bf16[512,128]{1,0:T(8,128)(2,1)S(1)}, bf16[512,128]{1,0:T(8,128)(2,1)S(1)}, u32[]{:S(2)}, u32[]{:S(2)}) collective-permute-start(bf16[512,128]{1,0:T(8,128)(2,1)S(1)} %attention.3.refs_0_), channel_id=1, source_target_pairs={{0,2},{2,0},{4,6},{6,4},{8,10},{10,8},{12,14},{14,12},{1,3},{3,1},... | collective-permute-start | bytes 393224 | tf_op jit(solution)/shard_map/ppermute | solution.py:369
  170.7 9.5 %collective-permute-start.27 = (bf16[512,128]{1,0:T(8,128)(2,1)S(1)}, bf16[512,128]{1,0:T(8,128)(2,1)S(1)}, u32[]{:S(2)}, u32[]{:S(2)}) collective-permute-start(bf16[512,128]{1,0:T(8,128)(2,1)S(1)} %attention.3.refs_0_), channel_id=1, source_target_pairs={{0,8},{2,10},{4,12},{6,14},{8,0},{10,2},{12,4},{14,6},{1,9},{3,11}... | collective-permute-start | bytes 393224 | tf_op jit(solution)/shard_map/ppermute | solution.py:369
  172.9 8.9 %collective-permute-start.28 = (bf16[512,128]{1,0:T(8,128)(2,1)S(1)}, bf16[512,128]{1,0:T(8,128)(2,1)S(1)}, u32[]{:S(2)}, u32[]{:S(2)}) collective-permute-start(bf16[512,128]{1,0:T(8,128)(2,1)S(1)} %attention.3.refs_0_), channel_id=1, source_target_pairs={{0,12},{2,14},{4,8},{6,10},{8,4},{10,6},{12,0},{14,2},{1,13},{3,15... | collective-permute-start | bytes 393224 | tf_op jit(solution)/shard_map/ppermute | solution.py:369
  174.4 7.4 %collective-permute-start.29 = (bf16[512,128]{1,0:T(8,128)(2,1)S(1)}, bf16[512,128]{1,0:T(8,128)(2,1)S(1)}, u32[]{:S(2)}, u32[]{:S(2)}) collective-permute-start(bf16[512,128]{1,0:T(8,128)(2,1)S(1)} %attention.3.refs_0_), channel_id=1, source_target_pairs={{0,4},{2,6},{4,0},{6,2},{8,12},{10,14},{12,8},{14,10},{1,5},{3,7},... | collective-permute-start | bytes 393224 | tf_op jit(solution)/shard_map/ppermute | solution.py:369
  182.4 4.3 %collective-permute-start.30 = (bf16[256,1024]{1,0:T(8,128)(2,1)S(1)}, bf16[256,1024]{1,0:T(8,128)(2,1)S(1)}, u32[]{:S(2)}, u32[]{:S(2)}) collective-permute-start(bf16[256,1024]{1,0:T(8,128)(2,1)S(1)} %project.7.send_ref), channel_id=1, source_target_pairs={{0,16},{16,0},{32,48},{48,32},{64,80},{80,64},{96,112},{112,96},{1... | collective-permute-start | bytes 1572872 | tf_op jit(solution)/shard_map/ppermute | solution.py:360
  187.9 11.6 %collective-permute-start.32 = (bf16[64,1024]{1,0:T(8,128)(2,1)}, bf16[64,1024]{1,0:T(8,128)(2,1)}, u32[]{:S(2)}, u32[]{:S(2)}) collective-permute-start(bf16[64,1024]{1,0:T(8,128)(2,1)} %get-tuple-element.25), channel_id=1, source_target_pairs={{0,64},{16,80},{32,96},{48,112},{64,0},{80,16},{96,32},{112,48},{1... | collective-permute-start | bytes 393224 | tf_op jit(solution)/shard_map/ppermute | solution.py:364
  189.2 10.3 %collective-permute-start.33 = (bf16[64,1024]{1,0:T(8,128)(2,1)S(1)}, bf16[64,1024]{1,0:T(8,128)(2,1)}, u32[]{:S(2)}, u32[]{:S(2)}) collective-permute-start(bf16[64,1024]{1,0:T(8,128)(2,1)S(1)} %get-tuple-element.26), channel_id=1, source_target_pairs={{0,96},{16,112},{32,64},{48,80},{64,32},{80,48},{96,0},{112,16},{1... | collective-permute-start | bytes 393224 | tf_op jit(solution)/shard_map/ppermute | solution.py:364
  191.3 8.2 %collective-permute-start.34 = (bf16[64,1024]{1,0:T(8,128)(2,1)S(1)}, bf16[64,1024]{1,0:T(8,128)(2,1)}, u32[]{:S(2)}, u32[]{:S(2)}) collective-permute-start(bf16[64,1024]{1,0:T(8,128)(2,1)S(1)} %get-tuple-element.27), channel_id=1, source_target_pairs={{0,32},{16,48},{32,0},{48,16},{64,96},{80,112},{96,64},{112,80},{1... | collective-permute-start | bytes 393224 | tf_op jit(solution)/shard_map/ppermute | solution.py:364
  191.3 24.8 %collective-permute-start.31 = (bf16[256,1024]{1,0:T(8,128)(2,1)S(1)}, bf16[256,1024]{1,0:T(8,128)(2,1)S(1)}, u32[]{:S(2)}, u32[]{:S(2)}) collective-permute-start(bf16[256,1024]{1,0:T(8,128)(2,1)S(1)} %project.6.keep_ref), channel_id=1, source_target_pairs={{0,16},{16,0},{32,48},{48,32},{64,80},{80,64},{96,112},{112,96},{1... | collective-permute-start | bytes 1572872 | tf_op jit(solution)/shard_map/ppermute | solution.py:360
  200.8 7.0 %collective-permute-start.35 = (bf16[64,1024]{1,0:T(8,128)(2,1)S(1)}, bf16[64,1024]{1,0:T(8,128)(2,1)S(1)}, u32[]{:S(2)}, u32[]{:S(2)}) collective-permute-start(bf16[64,1024]{1,0:T(8,128)(2,1)S(1)} %get-tuple-element.30), channel_id=1, source_target_pairs={{0,64},{16,80},{32,96},{48,112},{64,0},{80,16},{96,32},{112,48},{1... | collective-permute-start | bytes 393224 | tf_op jit(solution)/shard_map/ppermute | solution.py:364
  204.1 11.5 %collective-permute-start.36 = (bf16[64,1024]{1,0:T(8,128)(2,1)S(1)}, bf16[64,1024]{1,0:T(8,128)(2,1)S(1)}, u32[]{:S(2)}, u32[]{:S(2)}) collective-permute-start(bf16[64,1024]{1,0:T(8,128)(2,1)S(1)} %get-tuple-element.31), channel_id=1, source_target_pairs={{0,96},{16,112},{32,64},{48,80},{64,32},{80,48},{96,0},{112,16},{1... | collective-permute-start | bytes 393224 | tf_op jit(solution)/shard_map/ppermute | solution.py:364
  206.0 9.6 %collective-permute-start.37 = (bf16[64,1024]{1,0:T(8,128)(2,1)S(1)}, bf16[64,1024]{1,0:T(8,128)(2,1)S(1)}, u32[]{:S(2)}, u32[]{:S(2)}) collective-permute-start(bf16[64,1024]{1,0:T(8,128)(2,1)S(1)} %get-tuple-element.29), channel_id=1, source_target_pairs={{0,32},{16,48},{32,0},{48,16},{64,96},{80,112},{96,64},{112,80},{1... | collective-permute-start | bytes 393224 | tf_op jit(solution)/shard_map/ppermute | solution.py:364
  206.0 10.2 %collective-permute-start.38 = (bf16[64,1024]{1,0:T(8,128)(2,1)S(1)}, bf16[64,1024]{1,0:T(8,128)(2,1)S(1)}, u32[]{:S(2)}, u32[]{:S(2)}) collective-permute-start(bf16[64,1024]{1,0:T(8,128)(2,1)S(1)} %get-tuple-element.32.refs_0_), channel_id=1, source_target_pairs={{0,16},{16,0},{32,48},{48,32},{64,80},{80,64},{96,112},{112,96},{1... | collective-permute-start | bytes 393224 | tf_op jit(solution)/shard_map/ppermute | solution.py:360
  207.8 8.9 %collective-permute-start.39 = (bf16[64,1024]{1,0:T(8,128)(2,1)S(1)}, bf16[64,1024]{1,0:T(8,128)(2,1)S(1)}, u32[]{:S(2)}, u32[]{:S(2)}) collective-permute-start(bf16[64,1024]{1,0:T(8,128)(2,1)S(1)} %collective-permute-done.35.refs_1_), channel_id=1, source_target_pairs={{0,16},{16,0},{32,48},{48,32},{64,80},{80,64},{96,112},{112,96},{1... | collective-permute-start | bytes 393224 | tf_op jit(solution)/shard_map/ppermute | solution.py:360
  215.7 1.3 collective-permute-start.40
  215.7 1.5 collective-permute-start.41

commit v4 on v3

--- a/solution.py
+++ b/solution.py
@@ -123,8 +123,8 @@
     chip = place[2]
     out_ref = refs[-1]
     value = own_ref[...]
-    for d in range(1, CHIPS):
-        value = jnp.where(chip == d, refs[d - 1][...], value)
+    for d, value_ref in zip(ROUND[1:], refs):
+        value = jnp.where(chip == d, value_ref[...], value)
     out_ref[...] = value
 
 
@@ -387,7 +387,7 @@
 
     vectors = jnp.concatenate([ln_gain, ln_bias], axis=0)
     weight_in, tokens = stage(weight_in, tokens)
-    received = [over_chips(vectors, d) for d in range(1, CHIPS)]
+    received = [over_chips(vectors, d) for d in ROUND[1:]]
     even = pick(place, vectors, received, [weight_in])
     odd = over_cores(even)
 

time: 220 us -> 220 us (level)
  starting transfers between devices: 70.2 us -> 65.7 us
  waiting for transfers between devices: 40.3 us -> 44.6 us
    ppermute x12, starting transfers between devices: 27.8 us -> 22.9 us  [over_cores(): return lax.ppermute(value, 'section', [(s, s ^ 1) for s in range(2 * SPAN)])]
    ppermute x16, waiting for transfers between devices: 22.1 us -> 26.5 us  [over_chips(): lax.ppermute(value, 'section', [(s, s ^ 2 * d) for s in range(2 * SPAN)])]
where the time goes in v4:
time: 220 us; the launch traced here: 219 us
  blocking collectives  84.9 us (39%)
  starting transfers between devices  65.7 us (30%)
  waiting for transfers between devices  44.6 us (20%)
  Pallas kernels  17.6 us (8%)
  local copies, waits for them, and re-layouts  4.01 us (2%)
    all_to_all x2, blocking collectives, over_tp(): return lax.all_to_all(value, 'tp', 0, 0, tiled=True)  84.9 us
    ppermute x16, waiting for transfers between devices, over_chips(): lax.ppermute(value, 'section', [(s, s ^ 2 * d) for s in range(2 * SPAN)])  26.5 us
    ppermute x16, starting transfers between devices, over_chips(): lax.ppermute(value, 'section', [(s, s ^ 2 * d) for s in range(2 * SPAN)])  24.5 us
    ppermute x12, starting transfers between devices, over_cores(): return lax.ppermute(value, 'section', [(s, s ^ 1) for s in range(2 * SPAN)])  22.9 us
    ppermute x14, starting transfers between devices, spread(): lax.ppermute(value, 'tp', [(t, t ^ d) for t in range(TP)])  18.4 us
    ppermute x14, waiting for transfers between devices, spread(): lax.ppermute(value, 'tp', [(t, t ^ d) for t in range(TP)])  14.4 us
    pallas_call x2, Pallas kernels, qkv(): pl.pallas_call(functools.partial(qkv_kernel, bool(pieces)), out_shape=sha...  5.31 us
  transfers between devices with their start and end apart: 42, of which 20 were waited for; matrix products, arithmetic and copies ran while one was open for 1% of the time, Pallas kernels for 1%

profile of v4, /device:TPU:1, one launch (start us, length us, event | category | flops | bytes accessed | tf_op | source)
XLA Modules:
  0.0 219.2 jit_solution(11528560231821230290)
XLA Ops:
  0.0 0.7 pad_maximum_fusion.own_ref
  0.7 3.9 %collective-permute-start = (f32[2,1024]{1,0:T(2,128)S(1)}, f32[2,1024]{1,0:T(2,128)S(1)}, u32[]{:S(2)}, u32[]{:S(2)}) collective-permute-start(f32[2,1024]{1,0:T(2,128)S(1)} %pad_maximum_fusion.own_ref), channel_id=1, source_target_pairs={{0,64},{16,80},{32,96},{48,112},{64,0},{80,16},{96,32},{112,48},{1... | collective-permute-start | bytes 24584 | tf_op jit(solution)/shard_map/ppermute | solution.py:364
  4.6 1.5 collective-permute-start.1
  6.3 2.8 %copy-done.1 = bf16[1,8,1024,384]{3,2,1,0:T(8,128)(2,1)S(1)} copy-done((bf16[1,8,1024,384]{3,2,1,0:T(8,128)(2,1)S(1)}, bf16[1,8,1024,384]{3,2,1,0:T(8,128)(2,1)}, u32[]{:S(2)}) %copy-start.1) | copy-done | bytes 6291480
  9.1 1.2 copy-done.2
  10.4 0.5 stage.1
  10.9 0.6 pick.1.refs_2_.refs_10_
  11.5 1.4 collective-permute-start.3
  12.8 0.8 collective-permute-done.3.refs_3_.refs_11_
  13.6 4.5 %qkv.2 = bf16[8,528,384]{2,1,0:T(8,128)(2,1)S(1)} custom-call(s32[4]{0:T(128)S(1)} %pad_add_fusion.place.refs_0_, bf16[512,1024]{1,0:T(8,128)(2,1)S(1)} %get-tuple-element.17.refs_1_, f32[2,1024]{1,0:T(2,128)S(1)} %pick.1.refs_2_.refs_10_, f32[2,1024]{1,0:T(2,128)S(1)} %collective-permute-done.3.refs_3_.refs_11_, ...), custom_call_target="tpu_custom_call" | custom-call | flops 1 | bytes 1 | tf_op jit(solution)/shard_map/qkv/pallas_call | solution.py:211
  18.1 43.6 %all_to_all.10.pieces_ref = bf16[8,528,384]{2,1,0:T(8,128)(2,1)S(1)} all-to-all(bf16[8,528,384]{2,1,0:T(8,128)(2,1)S(1)} %qkv.2), channel_id=1, replica_groups=mesh['section'=16,'tp'=8,'dp'=2] {'tp'}, dimensions={0} | all-to-all | bytes 6488064 | tf_op jit(solution)/shard_map/all_to_all | solution.py:356
  61.7 2.6 %attention.2.refs_0_ = bf16[512,128]{1,0:T(8,128)(2,1)S(1)} custom-call(s32[4]{0:T(128)S(1)} %pad_add_fusion.place.refs_0_, bf16[8,528,384]{2,1,0:T(8,128)(2,1)S(1)} %all_to_all.10.pieces_ref), custom_call_target="tpu_custom_call" | custom-call | flops 1 | bytes 1 | tf_op jit(solution)/shard_map/attention/pallas_call | solution.py:249
  64.4 2.7 %collective-permute-start.4 = (bf16[512,128]{1,0:T(8,128)(2,1)S(1)}, bf16[512,128]{1,0:T(8,128)(2,1)S(1)}, u32[]{:S(2)}, u32[]{:S(2)}) collective-permute-start(bf16[512,128]{1,0:T(8,128)(2,1)S(1)} %attention.2.refs_0_), channel_id=1, source_target_pairs={{0,10},{2,8},{4,14},{6,12},{8,2},{10,0},{12,6},{14,4},{1,11},{3,9}... | collective-permute-start | bytes 393224 | tf_op jit(solution)/shard_map/ppermute | solution.py:369
  67.2 2.0 collective-permute-start.5
  69.1 1.0 collective-permute-start.7
  70.1 2.1 collective-permute-start.8
  72.1 2.0 collective-permute-start.9
  74.3 1.3 collective-permute-done.6.refs_3_
  75.6 4.1 %collective-permute-done.7.refs_4_ = bf16[512,128]{1,0:T(8,128)(2,1)S(1)} collective-permute-done((bf16[512,128]{1,0:T(8,128)(2,1)S(1)}, bf16[512,128]{1,0:T(8,128)(2,1)S(1)}, u32[]{:S(2)}, u32[]{:S(2)}) %collective-permute-start.7) | collective-permute-done | bytes 131104 | tf_op jit(solution)/shard_map/ppermute | solution.py:369
  79.7 1.4 collective-permute-done.9.refs_6_
  81.2 1.4 project.5.refs_9_
  82.6 1.3 collective-permute-start.11
  83.9 1.6 project.4.keep_ref.refs_9_
  85.5 0.7 quarters.2
  86.2 2.3 %collective-permute-start.12 = (bf16[64,1024]{1,0:T(8,128)(2,1)S(1)}, bf16[64,1024]{1,0:T(8,128)(2,1)S(1)}, u32[]{:S(2)}, u32[]{:S(2)}) collective-permute-start(bf16[64,1024]{1,0:T(8,128)(2,1)S(1)} %get-tuple-element.20), channel_id=1, source_target_pairs={{0,64},{16,80},{32,96},{48,112},{64,0},{80,16},{96,32},{112,48},{1... | collective-permute-start | bytes 393224 | tf_op jit(solution)/shard_map/ppermute | solution.py:364
  88.4 1.2 collective-permute-start.13
  89.6 8.0 %collective-permute-done.12 = bf16[64,1024]{1,0:T(8,128)(2,1)S(1)} collective-permute-done((bf16[64,1024]{1,0:T(8,128)(2,1)S(1)}, bf16[64,1024]{1,0:T(8,128)(2,1)S(1)}, u32[]{:S(2)}, u32[]{:S(2)}) %collective-permute-start.12) | collective-permute-done | bytes 131104 | tf_op jit(solution)/shard_map/ppermute | solution.py:364
  97.6 0.5 collective-permute-done.14
  98.3 5.0 %collective-permute-done.15.refs_2_ = bf16[64,1024]{1,0:T(8,128)(2,1)S(1)} collective-permute-done((bf16[64,1024]{1,0:T(8,128)(2,1)S(1)}, bf16[64,1024]{1,0:T(8,128)(2,1)S(1)}, u32[]{:S(2)}, u32[]{:S(2)}) %collective-permute-start.15) | collective-permute-done | bytes 131104 | tf_op jit(solution)/shard_map/ppermute | solution.py:364
  103.3 6.4 %collective-permute-start.16 = (bf16[64,1024]{1,0:T(8,128)(2,1)S(1)}, bf16[64,1024]{1,0:T(8,128)(2,1)S(1)}, u32[]{:S(2)}, u32[]{:S(2)}) collective-permute-start(bf16[64,1024]{1,0:T(8,128)(2,1)S(1)} %collective-permute-done.15.refs_2_), channel_id=1, source_target_pairs={{0,64},{16,80},{32,96},{48,112},{64,0},{80,16},{96,32},{112,48},{1... | collective-permute-start | bytes 393224 | tf_op jit(solution)/shard_map/ppermute | solution.py:364
  110.0 3.8 %collective-permute-start.19 = (bf16[64,1024]{1,0:T(8,128)(2,1)S(1)}, bf16[64,1024]{1,0:T(8,128)(2,1)S(1)}, u32[]{:S(2)}, u32[]{:S(2)}) collective-permute-start(bf16[64,1024]{1,0:T(8,128)(2,1)S(1)} %collective-permute-done.15.refs_2_), channel_id=1, source_target_pairs={{0,16},{16,0},{32,48},{48,32},{64,80},{80,64},{96,112},{112,96},{1... | collective-permute-start | bytes 393224 | tf_op jit(solution)/shard_map/ppermute | solution.py:360
  113.8 7.4 %collective-permute-start.20 = (bf16[64,1024]{1,0:T(8,128)(2,1)S(1)}, bf16[64,1024]{1,0:T(8,128)(2,1)S(1)}, u32[]{:S(2)}, u32[]{:S(2)}) collective-permute-start(bf16[64,1024]{1,0:T(8,128)(2,1)S(1)} %collective-permute-done.16.refs_3_), channel_id=1, source_target_pairs={{0,16},{16,0},{32,48},{48,32},{64,80},{80,64},{96,112},{112,96},{1... | collective-permute-start | bytes 393224 | tf_op jit(solution)/shard_map/ppermute | solution.py:360
  121.2 0.5 collective-permute-start.22
  121.7 0.5 collective-permute-done.20.refs_7_
  122.7 0.8 qkv.3
  123.6 41.4 %all_to_all.11.pieces_ref = bf16[8,528,384]{2,1,0:T(8,128)(2,1)S(1)} all-to-all(bf16[8,528,384]{2,1,0:T(8,128)(2,1)S(1)} %get-tuple-element.24), channel_id=1, replica_groups=mesh['section'=16,'tp'=8,'dp'=2] {'tp'}, dimensions={0} | all-to-all | bytes 6488064 | tf_op jit(solution)/shard_map/all_to_all | solution.py:356
  165.0 0.5 attention.3.refs_0_
  165.5 1.2 collective-permute-start.23
  166.8 2.2 %collective-permute-start.24 = (bf16[512,128]{1,0:T(8,128)(2,1)S(1)}, bf16[512,128]{1,0:T(8,128)(2,1)S(1)}, u32[]{:S(2)}, u32[]{:S(2)}) collective-permute-start(bf16[512,128]{1,0:T(8,128)(2,1)S(1)} %attention.3.refs_0_), channel_id=1, source_target_pairs={{0,14},{2,12},{4,10},{6,8},{8,6},{10,4},{12,2},{14,0},{1,15},{3,13... | collective-permute-start | bytes 393224 | tf_op jit(solution)/shard_map/ppermute | solution.py:369
  169.0 0.9 collective-permute-start.25
  169.8 0.5 collective-permute-start.26
  170.3 2.1 collective-permute-start.27
  172.5 1.5 collective-permute-start.28
  174.0 2.5 %collective-permute-done.25.refs_3_ = bf16[512,128]{1,0:T(8,128)(2,1)S(1)} collective-permute-done((bf16[512,128]{1,0:T(8,128)(2,1)S(1)}, bf16[512,128]{1,0:T(8,128)(2,1)S(1)}, u32[]{:S(2)}, u32[]{:S(2)}) %collective-permute-start.25) | collective-permute-done | bytes 131104 | tf_op jit(solution)/shard_map/ppermute | solution.py:369
  176.5 3.3 %collective-permute-done.26.refs_4_ = bf16[512,128]{1,0:T(8,128)(2,1)S(1)} collective-permute-done((bf16[512,128]{1,0:T(8,128)(2,1)S(1)}, bf16[512,128]{1,0:T(8,128)(2,1)S(1)}, u32[]{:S(2)}, u32[]{:S(2)}) %collective-permute-start.26) | collective-permute-done | bytes 131104 | tf_op jit(solution)/shard_map/ppermute | solution.py:369
  179.9 1.5 collective-permute-done.28.refs_6_
  181.4 0.6 project.7.send_ref
  182.0 2.7 %collective-permute-start.30 = (bf16[256,1024]{1,0:T(8,128)(2,1)S(1)}, bf16[256,1024]{1,0:T(8,128)(2,1)S(1)}, u32[]{:S(2)}, u32[]{:S(2)}) collective-permute-start(bf16[256,1024]{1,0:T(8,128)(2,1)S(1)} %project.7.send_ref), channel_id=1, source_target_pairs={{0,16},{16,0},{32,48},{48,32},{64,80},{80,64},{96,112},{112,96},{1... | collective-permute-start | bytes 1572872 | tf_op jit(solution)/shard_map/ppermute | solution.py:360
  184.7 0.6 project.6.keep_ref
  185.3 0.9 collective-permute-done.30.got_ref
  186.2 1.2 quarters.3
  187.5 1.2 collective-permute-start.32
  188.7 2.3 %collective-permute-start.33 = (bf16[64,1024]{1,0:T(8,128)(2,1)S(1)}, bf16[64,1024]{1,0:T(8,128)(2,1)}, u32[]{:S(2)}, u32[]{:S(2)}) collective-permute-start(bf16[64,1024]{1,0:T(8,128)(2,1)S(1)} %get-tuple-element.26), channel_id=1, source_target_pairs={{0,96},{16,112},{32,64},{48,80},{64,32},{80,48},{96,0},{112,16},{1... | collective-permute-start | bytes 393224 | tf_op jit(solution)/shard_map/ppermute | solution.py:364
  190.9 0.9 collective-permute-start.31
  191.8 7.2 %collective-permute-done.32 = bf16[64,1024]{1,0:T(8,128)(2,1)} collective-permute-done((bf16[64,1024]{1,0:T(8,128)(2,1)}, bf16[64,1024]{1,0:T(8,128)(2,1)}, u32[]{:S(2)}, u32[]{:S(2)}) %collective-permute-start.32) | collective-permute-done | bytes 131104 | tf_op jit(solution)/shard_map/ppermute | solution.py:364
  199.1 1.3 fusion.8
  200.3 4.3 %collective-permute-start.35 = (bf16[64,1024]{1,0:T(8,128)(2,1)S(1)}, bf16[64,1024]{1,0:T(8,128)(2,1)S(1)}, u32[]{:S(2)}, u32[]{:S(2)}) collective-permute-start(bf16[64,1024]{1,0:T(8,128)(2,1)S(1)} %get-tuple-element.30), channel_id=1, source_target_pairs={{0,64},{16,80},{32,96},{48,112},{64,0},{80,16},{96,32},{112,48},{1... | collective-permute-start | bytes 393224 | tf_op jit(solution)/shard_map/ppermute | solution.py:364
  204.6 1.0 collective-permute-start.36
  205.6 1.8 collective-permute-start.38
  207.4 5.7 %collective-permute-done.35.refs_1_ = bf16[64,1024]{1,0:T(8,128)(2,1)S(1)} collective-permute-done((bf16[64,1024]{1,0:T(8,128)(2,1)S(1)}, bf16[64,1024]{1,0:T(8,128)(2,1)S(1)}, u32[]{:S(2)}, u32[]{:S(2)}) %collective-permute-start.35) | collective-permute-done | bytes 131104 | tf_op jit(solution)/shard_map/ppermute | solution.py:364
  213.1 2.6 %collective-permute-start.39 = (bf16[64,1024]{1,0:T(8,128)(2,1)S(1)}, bf16[64,1024]{1,0:T(8,128)(2,1)S(1)}, u32[]{:S(2)}, u32[]{:S(2)}) collective-permute-start(bf16[64,1024]{1,0:T(8,128)(2,1)S(1)} %collective-permute-done.35.refs_1_), channel_id=1, source_target_pairs={{0,16},{16,0},{32,48},{48,32},{64,80},{80,64},{96,112},{112,96},{1... | collective-permute-start | bytes 393224 | tf_op jit(solution)/shard_map/ppermute | solution.py:360
  215.6 0.5 collective-permute-start.41
  216.1 0.5 collective-permute-done.39.refs_5_
  217.2 2.1 finish.1
  (45 shorter events, 2.2 us)
Async XLA Ops:
  0.7 10.2 %collective-permute-start = (f32[2,1024]{1,0:T(2,128)S(1)}, f32[2,1024]{1,0:T(2,128)S(1)}, u32[]{:S(2)}, u32[]{:S(2)}) collective-permute-start(f32[2,1024]{1,0:T(2,128)S(1)} %pad_maximum_fusion.own_ref), channel_id=1, source_target_pairs={{0,64},{16,80},{32,96},{48,112},{64,0},{80,16},{96,32},{112,48},{1... | collective-permute-start | bytes 24584 | tf_op jit(solution)/shard_map/ppermute | solution.py:364
  4.6 6.3 %collective-permute-start.1 = (f32[2,1024]{1,0:T(2,128)S(1)}, f32[2,1024]{1,0:T(2,128)S(1)}, u32[]{:S(2)}, u32[]{:S(2)}) collective-permute-start(f32[2,1024]{1,0:T(2,128)S(1)} %pad_maximum_fusion.own_ref), channel_id=1, source_target_pairs={{0,96},{16,112},{32,64},{48,80},{64,32},{80,48},{96,0},{112,16},{1... | collective-permute-start | bytes 24584 | tf_op jit(solution)/shard_map/ppermute | solution.py:364
  6.1 4.8 %collective-permute-start.2 = (f32[2,1024]{1,0:T(2,128)S(1)}, f32[2,1024]{1,0:T(2,128)S(1)}, u32[]{:S(2)}, u32[]{:S(2)}) collective-permute-start(f32[2,1024]{1,0:T(2,128)S(1)} %pad_maximum_fusion.own_ref), channel_id=1, source_target_pairs={{0,32},{16,48},{32,0},{48,16},{64,96},{80,112},{96,64},{112,80},{1... | collective-permute-start | bytes 24584 | tf_op jit(solution)/shard_map/ppermute | solution.py:364
  6.3 2.8 %copy-start.1 = (bf16[1,8,1024,384]{3,2,1,0:T(8,128)(2,1)S(1)}, bf16[1,8,1024,384]{3,2,1,0:T(8,128)(2,1)}, u32[]{:S(2)}) copy-start(bf16[1,8,1024,384]{3,2,1,0:T(8,128)(2,1)} %param.8) | copy-start | bytes 18874372
  9.1 1.2 copy-start.2
  11.5 2.2 collective-permute-start.3
  61.7 19.5 %copy-start = (bf16[1,1024,1024]{2,1,0:T(8,128)(2,1)S(1)}, bf16[1,1024,1024]{2,1,0:T(8,128)(2,1)}, u32[]{:S(2)}) copy-start(bf16[1,1024,1024]{2,1,0:T(8,128)(2,1)} %param.9) | copy-start | bytes 6291460
  64.3 5.8 %collective-permute-start.10 = (bf16[512,128]{1,0:T(8,128)(2,1)S(1)}, bf16[512,128]{1,0:T(8,128)(2,1)S(1)}, u32[]{:S(2)}, u32[]{:S(2)}) collective-permute-start(bf16[512,128]{1,0:T(8,128)(2,1)S(1)} %attention.2.refs_0_), channel_id=1, source_target_pairs={{0,4},{2,6},{4,0},{6,2},{8,12},{10,14},{12,8},{14,10},{1,5},{3,7},... | collective-permute-start | bytes 393224 | tf_op jit(solution)/shard_map/ppermute | solution.py:369
  64.4 7.7 %collective-permute-start.4 = (bf16[512,128]{1,0:T(8,128)(2,1)S(1)}, bf16[512,128]{1,0:T(8,128)(2,1)S(1)}, u32[]{:S(2)}, u32[]{:S(2)}) collective-permute-start(bf16[512,128]{1,0:T(8,128)(2,1)S(1)} %attention.2.refs_0_), channel_id=1, source_target_pairs={{0,10},{2,8},{4,14},{6,12},{8,2},{10,0},{12,6},{14,4},{1,11},{3,9}... | collective-permute-start | bytes 393224 | tf_op jit(solution)/shard_map/ppermute | solution.py:369
  67.2 7.1 %collective-permute-start.5 = (bf16[512,128]{1,0:T(8,128)(2,1)S(1)}, bf16[512,128]{1,0:T(8,128)(2,1)S(1)}, u32[]{:S(2)}, u32[]{:S(2)}) collective-permute-start(bf16[512,128]{1,0:T(8,128)(2,1)S(1)} %attention.2.refs_0_), channel_id=1, source_target_pairs={{0,14},{2,12},{4,10},{6,8},{8,6},{10,4},{12,2},{14,0},{1,15},{3,13... | collective-permute-start | bytes 393224 | tf_op jit(solution)/shard_map/ppermute | solution.py:369
  69.1 6.5 %collective-permute-start.6 = (bf16[512,128]{1,0:T(8,128)(2,1)S(1)}, bf16[512,128]{1,0:T(8,128)(2,1)S(1)}, u32[]{:S(2)}, u32[]{:S(2)}) collective-permute-start(bf16[512,128]{1,0:T(8,128)(2,1)S(1)} %attention.2.refs_0_), channel_id=1, source_target_pairs={{0,6},{2,4},{4,2},{6,0},{8,14},{10,12},{12,10},{14,8},{1,7},{3,5},... | collective-permute-start | bytes 393224 | tf_op jit(solution)/shard_map/ppermute | solution.py:369
  69.1 10.6 %collective-permute-start.7 = (bf16[512,128]{1,0:T(8,128)(2,1)S(1)}, bf16[512,128]{1,0:T(8,128)(2,1)S(1)}, u32[]{:S(2)}, u32[]{:S(2)}) collective-permute-start(bf16[512,128]{1,0:T(8,128)(2,1)S(1)} %attention.2.refs_0_), channel_id=1, source_target_pairs={{0,2},{2,0},{4,6},{6,4},{8,10},{10,8},{12,14},{14,12},{1,3},{3,1},... | collective-permute-start | bytes 393224 | tf_op jit(solution)/shard_map/ppermute | solution.py:369
  70.1 9.7 %collective-permute-start.8 = (bf16[512,128]{1,0:T(8,128)(2,1)S(1)}, bf16[512,128]{1,0:T(8,128)(2,1)S(1)}, u32[]{:S(2)}, u32[]{:S(2)}) collective-permute-start(bf16[512,128]{1,0:T(8,128)(2,1)S(1)} %attention.2.refs_0_), channel_id=1, source_target_pairs={{0,8},{2,10},{4,12},{6,14},{8,0},{10,2},{12,4},{14,6},{1,9},{3,11}... | collective-permute-start | bytes 393224 | tf_op jit(solution)/shard_map/ppermute | solution.py:369
  72.1 9.0 %collective-permute-start.9 = (bf16[512,128]{1,0:T(8,128)(2,1)S(1)}, bf16[512,128]{1,0:T(8,128)(2,1)S(1)}, u32[]{:S(2)}, u32[]{:S(2)}) collective-permute-start(bf16[512,128]{1,0:T(8,128)(2,1)S(1)} %attention.2.refs_0_), channel_id=1, source_target_pairs={{0,12},{2,14},{4,8},{6,10},{8,4},{10,6},{12,0},{14,2},{1,13},{3,15... | collective-permute-start | bytes 393224 | tf_op jit(solution)/shard_map/ppermute | solution.py:369
  82.6 2.9 %collective-permute-start.11 = (bf16[256,1024]{1,0:T(8,128)(2,1)S(1)}, bf16[256,1024]{1,0:T(8,128)(2,1)S(1)}, u32[]{:S(2)}, u32[]{:S(2)}) collective-permute-start(bf16[256,1024]{1,0:T(8,128)(2,1)S(1)} %project.5.refs_9_), channel_id=1, source_target_pairs={{0,16},{16,0},{32,48},{48,32},{64,80},{80,64},{96,112},{112,96},{1... | collective-permute-start | bytes 1572872 | tf_op jit(solution)/shard_map/ppermute | solution.py:360
  86.2 11.4 %collective-permute-start.12 = (bf16[64,1024]{1,0:T(8,128)(2,1)S(1)}, bf16[64,1024]{1,0:T(8,128)(2,1)S(1)}, u32[]{:S(2)}, u32[]{:S(2)}) collective-permute-start(bf16[64,1024]{1,0:T(8,128)(2,1)S(1)} %get-tuple-element.20), channel_id=1, source_target_pairs={{0,64},{16,80},{32,96},{48,112},{64,0},{80,16},{96,32},{112,48},{1... | collective-permute-start | bytes 393224 | tf_op jit(solution)/shard_map/ppermute | solution.py:364
  88.4 9.2 %collective-permute-start.13 = (bf16[64,1024]{1,0:T(8,128)(2,1)S(1)}, bf16[64,1024]{1,0:T(8,128)(2,1)S(1)}, u32[]{:S(2)}, u32[]{:S(2)}) collective-permute-start(bf16[64,1024]{1,0:T(8,128)(2,1)S(1)} %get-tuple-element.21), channel_id=1, source_target_pairs={{0,96},{16,112},{32,64},{48,80},{64,32},{80,48},{96,0},{112,16},{1... | collective-permute-start | bytes 393224 | tf_op jit(solution)/shard_map/ppermute | solution.py:364
  89.6 8.5 %collective-permute-start.14 = (bf16[64,1024]{1,0:T(8,128)(2,1)S(1)}, bf16[64,1024]{1,0:T(8,128)(2,1)S(1)}, u32[]{:S(2)}, u32[]{:S(2)}) collective-permute-start(bf16[64,1024]{1,0:T(8,128)(2,1)S(1)} %get-tuple-element.22), channel_id=1, source_target_pairs={{0,32},{16,48},{32,0},{48,16},{64,96},{80,112},{96,64},{112,80},{1... | collective-permute-start | bytes 393224 | tf_op jit(solution)/shard_map/ppermute | solution.py:364
  98.2 5.1 %collective-permute-start.15 = (bf16[64,1024]{1,0:T(8,128)(2,1)S(1)}, bf16[64,1024]{1,0:T(8,128)(2,1)S(1)}, u32[]{:S(2)}, u32[]{:S(2)}) collective-permute-start(bf16[64,1024]{1,0:T(8,128)(2,1)S(1)} %add_convert_fusion), channel_id=1, source_target_pairs={{0,224},{16,240},{32,192},{48,208},{64,160},{80,176},{96,128},{112... | collective-permute-start | bytes 393224 | tf_op jit(solution)/shard_map/ppermute | solution.py:364
  103.3 10.6 %collective-permute-start.16 = (bf16[64,1024]{1,0:T(8,128)(2,1)S(1)}, bf16[64,1024]{1,0:T(8,128)(2,1)S(1)}, u32[]{:S(2)}, u32[]{:S(2)}) collective-permute-start(bf16[64,1024]{1,0:T(8,128)(2,1)S(1)} %collective-permute-done.15.refs_2_), channel_id=1, source_target_pairs={{0,64},{16,80},{32,96},{48,112},{64,0},{80,16},{96,32},{112,48},{1... | collective-permute-start | bytes 393224 | tf_op jit(solution)/shard_map/ppermute | solution.py:364
  109.7 11.5 %collective-permute-start.17 = (bf16[64,1024]{1,0:T(8,128)(2,1)S(1)}, bf16[64,1024]{1,0:T(8,128)(2,1)S(1)}, u32[]{:S(2)}, u32[]{:S(2)}) collective-permute-start(bf16[64,1024]{1,0:T(8,128)(2,1)S(1)} %collective-permute-done.15.refs_2_), channel_id=1, source_target_pairs={{0,96},{16,112},{32,64},{48,80},{64,32},{80,48},{96,0},{112,16},{1... | collective-permute-start | bytes 393224 | tf_op jit(solution)/shard_map/ppermute | solution.py:364
  109.9 11.4 %collective-permute-start.18 = (bf16[64,1024]{1,0:T(8,128)(2,1)S(1)}, bf16[64,1024]{1,0:T(8,128)(2,1)S(1)}, u32[]{:S(2)}, u32[]{:S(2)}) collective-permute-start(bf16[64,1024]{1,0:T(8,128)(2,1)S(1)} %collective-permute-done.15.refs_2_), channel_id=1, source_target_pairs={{0,32},{16,48},{32,0},{48,16},{64,96},{80,112},{96,64},{112,80},{1... | collective-permute-start | bytes 393224 | tf_op jit(solution)/shard_map/ppermute | solution.py:364
  110.0 11.7 %collective-permute-start.19 = (bf16[64,1024]{1,0:T(8,128)(2,1)S(1)}, bf16[64,1024]{1,0:T(8,128)(2,1)S(1)}, u32[]{:S(2)}, u32[]{:S(2)}) collective-permute-start(bf16[64,1024]{1,0:T(8,128)(2,1)S(1)} %collective-permute-done.15.refs_2_), channel_id=1, source_target_pairs={{0,16},{16,0},{32,48},{48,32},{64,80},{80,64},{96,112},{112,96},{1... | collective-permute-start | bytes 393224 | tf_op jit(solution)/shard_map/ppermute | solution.py:360
  113.8 8.3 %collective-permute-start.20 = (bf16[64,1024]{1,0:T(8,128)(2,1)S(1)}, bf16[64,1024]{1,0:T(8,128)(2,1)S(1)}, u32[]{:S(2)}, u32[]{:S(2)}) collective-permute-start(bf16[64,1024]{1,0:T(8,128)(2,1)S(1)} %collective-permute-done.16.refs_3_), channel_id=1, source_target_pairs={{0,16},{16,0},{32,48},{48,32},{64,80},{80,64},{96,112},{112,96},{1... | collective-permute-start | bytes 393224 | tf_op jit(solution)/shard_map/ppermute | solution.py:360
  121.2 1.3 collective-permute-start.21
  121.2 1.5 collective-permute-start.22
  165.5 7.0 %collective-permute-start.23 = (bf16[512,128]{1,0:T(8,128)(2,1)S(1)}, bf16[512,128]{1,0:T(8,128)(2,1)S(1)}, u32[]{:S(2)}, u32[]{:S(2)}) collective-permute-start(bf16[512,128]{1,0:T(8,128)(2,1)S(1)} %attention.3.refs_0_), channel_id=1, source_target_pairs={{0,10},{2,8},{4,14},{6,12},{8,2},{10,0},{12,6},{14,4},{1,11},{3,9}... | collective-permute-start | bytes 393224 | tf_op jit(solution)/shard_map/ppermute | solution.py:369
  166.8 7.3 %collective-permute-start.24 = (bf16[512,128]{1,0:T(8,128)(2,1)S(1)}, bf16[512,128]{1,0:T(8,128)(2,1)S(1)}, u32[]{:S(2)}, u32[]{:S(2)}) collective-permute-start(bf16[512,128]{1,0:T(8,128)(2,1)S(1)} %attention.3.refs_0_), channel_id=1, source_target_pairs={{0,14},{2,12},{4,10},{6,8},{8,6},{10,4},{12,2},{14,0},{1,15},{3,13... | collective-permute-start | bytes 393224 | tf_op jit(solution)/shard_map/ppermute | solution.py:369
  169.0 7.6 %collective-permute-start.25 = (bf16[512,128]{1,0:T(8,128)(2,1)S(1)}, bf16[512,128]{1,0:T(8,128)(2,1)S(1)}, u32[]{:S(2)}, u32[]{:S(2)}) collective-permute-start(bf16[512,128]{1,0:T(8,128)(2,1)S(1)} %attention.3.refs_0_), channel_id=1, source_target_pairs={{0,6},{2,4},{4,2},{6,0},{8,14},{10,12},{12,10},{14,8},{1,7},{3,5},... | collective-permute-start | bytes 393224 | tf_op jit(solution)/shard_map/ppermute | solution.py:369
  169.8 10.0 %collective-permute-start.26 = (bf16[512,128]{1,0:T(8,128)(2,1)S(1)}, bf16[512,128]{1,0:T(8,128)(2,1)S(1)}, u32[]{:S(2)}, u32[]{:S(2)}) collective-permute-start(bf16[512,128]{1,0:T(8,128)(2,1)S(1)} %attention.3.refs_0_), channel_id=1, source_target_pairs={{0,2},{2,0},{4,6},{6,4},{8,10},{10,8},{12,14},{14,12},{1,3},{3,1},... | collective-permute-start | bytes 393224 | tf_op jit(solution)/shard_map/ppermute | solution.py:369
  170.3 9.5 %collective-permute-start.27 = (bf16[512,128]{1,0:T(8,128)(2,1)S(1)}, bf16[512,128]{1,0:T(8,128)(2,1)S(1)}, u32[]{:S(2)}, u32[]{:S(2)}) collective-permute-start(bf16[512,128]{1,0:T(8,128)(2,1)S(1)} %attention.3.refs_0_), channel_id=1, source_target_pairs={{0,8},{2,10},{4,12},{6,14},{8,0},{10,2},{12,4},{14,6},{1,9},{3,11}... | collective-permute-start | bytes 393224 | tf_op jit(solution)/shard_map/ppermute | solution.py:369
  172.5 8.9 %collective-permute-start.28 = (bf16[512,128]{1,0:T(8,128)(2,1)S(1)}, bf16[512,128]{1,0:T(8,128)(2,1)S(1)}, u32[]{:S(2)}, u32[]{:S(2)}) collective-permute-start(bf16[512,128]{1,0:T(8,128)(2,1)S(1)} %attention.3.refs_0_), channel_id=1, source_target_pairs={{0,12},{2,14},{4,8},{6,10},{8,4},{10,6},{12,0},{14,2},{1,13},{3,15... | collective-permute-start | bytes 393224 | tf_op jit(solution)/shard_map/ppermute | solution.py:369
  174.0 7.4 %collective-permute-start.29 = (bf16[512,128]{1,0:T(8,128)(2,1)S(1)}, bf16[512,128]{1,0:T(8,128)(2,1)S(1)}, u32[]{:S(2)}, u32[]{:S(2)}) collective-permute-start(bf16[512,128]{1,0:T(8,128)(2,1)S(1)} %attention.3.refs_0_), channel_id=1, source_target_pairs={{0,4},{2,6},{4,0},{6,2},{8,12},{10,14},{12,8},{14,10},{1,5},{3,7},... | collective-permute-start | bytes 393224 | tf_op jit(solution)/shard_map/ppermute | solution.py:369
  182.0 4.3 %collective-permute-start.30 = (bf16[256,1024]{1,0:T(8,128)(2,1)S(1)}, bf16[256,1024]{1,0:T(8,128)(2,1)S(1)}, u32[]{:S(2)}, u32[]{:S(2)}) collective-permute-start(bf16[256,1024]{1,0:T(8,128)(2,1)S(1)} %project.7.send_ref), channel_id=1, source_target_pairs={{0,16},{16,0},{32,48},{48,32},{64,80},{80,64},{96,112},{112,96},{1... | collective-permute-start | bytes 1572872 | tf_op jit(solution)/shard_map/ppermute | solution.py:360
  187.5 11.6 %collective-permute-start.32 = (bf16[64,1024]{1,0:T(8,128)(2,1)}, bf16[64,1024]{1,0:T(8,128)(2,1)}, u32[]{:S(2)}, u32[]{:S(2)}) collective-permute-start(bf16[64,1024]{1,0:T(8,128)(2,1)} %get-tuple-element.25), channel_id=1, source_target_pairs={{0,64},{16,80},{32,96},{48,112},{64,0},{80,16},{96,32},{112,48},{1... | collective-permute-start | bytes 393224 | tf_op jit(solution)/shard_map/ppermute | solution.py:364
  188.7 10.4 %collective-permute-start.33 = (bf16[64,1024]{1,0:T(8,128)(2,1)S(1)}, bf16[64,1024]{1,0:T(8,128)(2,1)}, u32[]{:S(2)}, u32[]{:S(2)}) collective-permute-start(bf16[64,1024]{1,0:T(8,128)(2,1)S(1)} %get-tuple-element.26), channel_id=1, source_target_pairs={{0,96},{16,112},{32,64},{48,80},{64,32},{80,48},{96,0},{112,16},{1... | collective-permute-start | bytes 393224 | tf_op jit(solution)/shard_map/ppermute | solution.py:364
  190.9 8.2 %collective-permute-start.34 = (bf16[64,1024]{1,0:T(8,128)(2,1)S(1)}, bf16[64,1024]{1,0:T(8,128)(2,1)}, u32[]{:S(2)}, u32[]{:S(2)}) collective-permute-start(bf16[64,1024]{1,0:T(8,128)(2,1)S(1)} %get-tuple-element.27), channel_id=1, source_target_pairs={{0,32},{16,48},{32,0},{48,16},{64,96},{80,112},{96,64},{112,80},{1... | collective-permute-start | bytes 393224 | tf_op jit(solution)/shard_map/ppermute | solution.py:364
  190.9 25.2 %collective-permute-start.31 = (bf16[256,1024]{1,0:T(8,128)(2,1)S(1)}, bf16[256,1024]{1,0:T(8,128)(2,1)S(1)}, u32[]{:S(2)}, u32[]{:S(2)}) collective-permute-start(bf16[256,1024]{1,0:T(8,128)(2,1)S(1)} %project.6.keep_ref), channel_id=1, source_target_pairs={{0,16},{16,0},{32,48},{48,32},{64,80},{80,64},{96,112},{112,96},{1... | collective-permute-start | bytes 1572872 | tf_op jit(solution)/shard_map/ppermute | solution.py:360
  200.3 12.7 %collective-permute-start.35 = (bf16[64,1024]{1,0:T(8,128)(2,1)S(1)}, bf16[64,1024]{1,0:T(8,128)(2,1)S(1)}, u32[]{:S(2)}, u32[]{:S(2)}) collective-permute-start(bf16[64,1024]{1,0:T(8,128)(2,1)S(1)} %get-tuple-element.30), channel_id=1, source_target_pairs={{0,64},{16,80},{32,96},{48,112},{64,0},{80,16},{96,32},{112,48},{1... | collective-permute-start | bytes 393224 | tf_op jit(solution)/shard_map/ppermute | solution.py:364
  204.6 11.0 %collective-permute-start.36 = (bf16[64,1024]{1,0:T(8,128)(2,1)S(1)}, bf16[64,1024]{1,0:T(8,128)(2,1)S(1)}, u32[]{:S(2)}, u32[]{:S(2)}) collective-permute-start(bf16[64,1024]{1,0:T(8,128)(2,1)S(1)} %get-tuple-element.31), channel_id=1, source_target_pairs={{0,96},{16,112},{32,64},{48,80},{64,32},{80,48},{96,0},{112,16},{1... | collective-permute-start | bytes 393224 | tf_op jit(solution)/shard_map/ppermute | solution.py:364
  205.6 10.0 %collective-permute-start.37 = (bf16[64,1024]{1,0:T(8,128)(2,1)S(1)}, bf16[64,1024]{1,0:T(8,128)(2,1)S(1)}, u32[]{:S(2)}, u32[]{:S(2)}) collective-permute-start(bf16[64,1024]{1,0:T(8,128)(2,1)S(1)} %get-tuple-element.29), channel_id=1, source_target_pairs={{0,32},{16,48},{32,0},{48,16},{64,96},{80,112},{96,64},{112,80},{1... | collective-permute-start | bytes 393224 | tf_op jit(solution)/shard_map/ppermute | solution.py:364
  205.6 10.5 %collective-permute-start.38 = (bf16[64,1024]{1,0:T(8,128)(2,1)S(1)}, bf16[64,1024]{1,0:T(8,128)(2,1)S(1)}, u32[]{:S(2)}, u32[]{:S(2)}) collective-permute-start(bf16[64,1024]{1,0:T(8,128)(2,1)S(1)} %get-tuple-element.32.refs_0_), channel_id=1, source_target_pairs={{0,16},{16,0},{32,48},{48,32},{64,80},{80,64},{96,112},{112,96},{1... | collective-permute-start | bytes 393224 | tf_op jit(solution)/shard_map/ppermute | solution.py:360
  213.1 3.5 %collective-permute-start.39 = (bf16[64,1024]{1,0:T(8,128)(2,1)S(1)}, bf16[64,1024]{1,0:T(8,128)(2,1)S(1)}, u32[]{:S(2)}, u32[]{:S(2)}) collective-permute-start(bf16[64,1024]{1,0:T(8,128)(2,1)S(1)} %collective-permute-done.35.refs_1_), channel_id=1, source_target_pairs={{0,16},{16,0},{32,48},{48,32},{64,80},{80,64},{96,112},{112,96},{1... | collective-permute-start | bytes 393224 | tf_op jit(solution)/shard_map/ppermute | solution.py:360
  215.6 1.3 collective-permute-start.40
  215.6 1.5 collective-permute-start.41

commit v5 on v4

--- a/solution.py
+++ b/solution.py
@@ -95,28 +95,24 @@
     return pl.CostEstimate(flops=1, bytes_accessed=1, transcendentals=0)
 
 
-def stage_kernel(w_ref, x_ref, w_out, x_out, sems):
-    copies = [
-        pltpu.make_async_copy(w_ref, w_out, sems.at[0]),
-        pltpu.make_async_copy(x_ref, x_out, sems.at[1]),
-    ]
-    for copy in copies:
-        copy.start()
-    for copy in copies:
-        copy.wait()
-
-
-def stage(w, x):
+def stage_kernel(value_ref, *refs):
+    out_ref, sem = refs[-2:]
+    copy = pltpu.make_async_copy(value_ref, out_ref, sem)
+    copy.start()
+    copy.wait()
+
+
+def stage(value, after):
     return pl.pallas_call(
         stage_kernel,
-        out_shape=[jax.ShapeDtypeStruct(w.shape, w.dtype), jax.ShapeDtypeStruct(x.shape, x.dtype)],
-        in_specs=[HBM, HBM],
-        out_specs=[HBM, HBM],
-        scratch_shapes=[pltpu.SemaphoreType.DMA((2,))],
+        out_shape=jax.ShapeDtypeStruct(value.shape, value.dtype),
+        in_specs=[HBM] * (1 + len(after)),
+        out_specs=HBM,
+        scratch_shapes=[pltpu.SemaphoreType.DMA],
         compiler_params=params(4),
         cost_estimate=cheap(),
         name="stage",
-    )(w, x)
+    )(value, *after)
 
 
 def pick_kernel(place, own_ref, *refs):
@@ -386,10 +382,11 @@
     features = tokens.shape[1] * TP
 
     vectors = jnp.concatenate([ln_gain, ln_bias], axis=0)
-    weight_in, tokens = stage(weight_in, tokens)
+    weight_in = stage(weight_in, [])
     received = [over_chips(vectors, d) for d in ROUND[1:]]
     even = pick(place, vectors, received, [weight_in])
     odd = over_cores(even)
+    tokens = stage(tokens, [even])
 
     _, part = qkv(place, tokens, [], even, odd, weight_in)
     out = attention(place, over_tp(part), features, 0)

time: 220 us -> 219 us (level)
  no operation moved by 1% of the time
where the time goes in v5:
time: 219 us; the launch traced here: 218 us
  blocking collectives  84.9 us (39%)
  starting transfers between devices  65.7 us (30%)
  waiting for transfers between devices  44.6 us (20%)
  Pallas kernels  17.6 us (8%)
  local copies, waits for them, and re-layouts  2.8 us (1%)
    all_to_all x2, blocking collectives, over_tp(): return lax.all_to_all(value, 'tp', 0, 0, tiled=True)  84.9 us
    ppermute x16, waiting for transfers between devices, over_chips(): lax.ppermute(value, 'section', [(s, s ^ 2 * d) for s in range(2 * SPAN)])  26.5 us
    ppermute x16, starting transfers between devices, over_chips(): lax.ppermute(value, 'section', [(s, s ^ 2 * d) for s in range(2 * SPAN)])  24.1 us
    ppermute x12, starting transfers between devices, over_cores(): return lax.ppermute(value, 'section', [(s, s ^ 1) for s in range(2 * SPAN)])  23.1 us
    ppermute x14, starting transfers between devices, spread(): lax.ppermute(value, 'tp', [(t, t ^ d) for t in range(TP)])  18.4 us
    ppermute x14, waiting for transfers between devices, spread(): lax.ppermute(value, 'tp', [(t, t ^ d) for t in range(TP)])  14.4 us
    pallas_call x2, Pallas kernels, qkv(): pl.pallas_call(functools.partial(qkv_kernel, bool(pieces)), out_shape=sha...  5.31 us
  transfers between devices with their start and end apart: 42, of which 20 were waited for; matrix products, arithmetic and copies ran while one was open for 1% of the time, Pallas kernels for 1%

profile of v5, /device:TPU:1, one launch (start us, length us, event | category | flops | bytes accessed | tf_op | source)
XLA Modules:
  0.0 218.0 jit_solution(17550684451969483678)
XLA Ops:
  0.0 0.7 pad_maximum_fusion.own_ref
  0.7 3.9 %collective-permute-start = (f32[2,1024]{1,0:T(2,128)S(1)}, f32[2,1024]{1,0:T(2,128)S(1)}, u32[]{:S(2)}, u32[]{:S(2)}) collective-permute-start(f32[2,1024]{1,0:T(2,128)S(1)} %pad_maximum_fusion.own_ref), channel_id=1, source_target_pairs={{0,64},{16,80},{32,96},{48,112},{64,0},{80,16},{96,32},{112,48},{1... | collective-permute-start | bytes 24584 | tf_op jit(solution)/shard_map/ppermute | solution.py:360
  4.6 1.5 collective-permute-start.1
  6.3 2.8 %copy-done.1 = bf16[1,8,1024,384]{3,2,1,0:T(8,128)(2,1)S(1)} copy-done((bf16[1,8,1024,384]{3,2,1,0:T(8,128)(2,1)S(1)}, bf16[1,8,1024,384]{3,2,1,0:T(8,128)(2,1)}, u32[]{:S(2)}) %copy-start.1) | copy-done | bytes 6291480
  9.1 0.4 stage.2.refs_3_.refs_4_.refs_12_
  9.6 0.6 pick.1.refs_0_.refs_2_.refs_10_
  10.2 1.5 collective-permute-start.3
  11.8 0.7 collective-permute-done.3.refs_3_.refs_11_
  12.5 4.5 %qkv.2 = bf16[8,528,384]{2,1,0:T(8,128)(2,1)S(1)} custom-call(s32[4]{0:T(128)S(1)} %pad_add_fusion.place.refs_0_, bf16[512,1024]{1,0:T(8,128)(2,1)S(1)} %stage.3.refs_1_, f32[2,1024]{1,0:T(2,128)S(1)} %pick.1.refs_0_.refs_2_.refs_10_, f32[2,1024]{1,0:T(2,128)S(1)} %collective-permute-done.3.refs_3_.refs_11_, ...), custom_call_target="tpu_custom_call" | custom-call | flops 1 | bytes 1 | tf_op jit(solution)/shard_map/qkv/pallas_call | solution.py:207
  17.0 43.6 %all_to_all.10.pieces_ref = bf16[8,528,384]{2,1,0:T(8,128)(2,1)S(1)} all-to-all(bf16[8,528,384]{2,1,0:T(8,128)(2,1)S(1)} %qkv.2), channel_id=1, replica_groups=mesh['section'=16,'tp'=8,'dp'=2] {'tp'}, dimensions={0} | all-to-all | bytes 6488064 | tf_op jit(solution)/shard_map/all_to_all | solution.py:352
  60.6 2.6 %attention.2.refs_0_ = bf16[512,128]{1,0:T(8,128)(2,1)S(1)} custom-call(s32[4]{0:T(128)S(1)} %pad_add_fusion.place.refs_0_, bf16[8,528,384]{2,1,0:T(8,128)(2,1)S(1)} %all_to_all.10.pieces_ref), custom_call_target="tpu_custom_call" | custom-call | flops 1 | bytes 1 | tf_op jit(solution)/shard_map/attention/pallas_call | solution.py:245
  63.3 2.8 %collective-permute-start.4 = (bf16[512,128]{1,0:T(8,128)(2,1)S(1)}, bf16[512,128]{1,0:T(8,128)(2,1)S(1)}, u32[]{:S(2)}, u32[]{:S(2)}) collective-permute-start(bf16[512,128]{1,0:T(8,128)(2,1)S(1)} %attention.2.refs_0_), channel_id=1, source_target_pairs={{0,10},{2,8},{4,14},{6,12},{8,2},{10,0},{12,6},{14,4},{1,11},{3,9}... | collective-permute-start | bytes 393224 | tf_op jit(solution)/shard_map/ppermute | solution.py:365
  66.1 2.0 collective-permute-start.5
  68.0 1.0 collective-permute-start.7
  69.0 2.1 collective-permute-start.8
  71.0 2.0 collective-permute-start.9
  73.2 1.3 collective-permute-done.6.refs_3_
  74.5 4.1 %collective-permute-done.7.refs_4_ = bf16[512,128]{1,0:T(8,128)(2,1)S(1)} collective-permute-done((bf16[512,128]{1,0:T(8,128)(2,1)S(1)}, bf16[512,128]{1,0:T(8,128)(2,1)S(1)}, u32[]{:S(2)}, u32[]{:S(2)}) %collective-permute-start.7) | collective-permute-done | bytes 131104 | tf_op jit(solution)/shard_map/ppermute | solution.py:365
  78.6 1.4 collective-permute-done.9.refs_6_
  80.1 1.4 project.5.refs_9_
  81.5 1.3 collective-permute-start.11
  82.8 1.6 project.4.keep_ref.refs_9_
  84.4 0.7 quarters.2
  85.1 2.1 collective-permute-start.12
  87.1 1.2 collective-permute-start.13
  88.3 8.2 %collective-permute-done.12 = bf16[64,1024]{1,0:T(8,128)(2,1)S(1)} collective-permute-done((bf16[64,1024]{1,0:T(8,128)(2,1)S(1)}, bf16[64,1024]{1,0:T(8,128)(2,1)S(1)}, u32[]{:S(2)}, u32[]{:S(2)}) %collective-permute-start.12) | collective-permute-done | bytes 131104 | tf_op jit(solution)/shard_map/ppermute | solution.py:360
  96.5 0.5 collective-permute-done.14
  97.2 5.0 %collective-permute-done.15.refs_2_ = bf16[64,1024]{1,0:T(8,128)(2,1)S(1)} collective-permute-done((bf16[64,1024]{1,0:T(8,128)(2,1)S(1)}, bf16[64,1024]{1,0:T(8,128)(2,1)S(1)}, u32[]{:S(2)}, u32[]{:S(2)}) %collective-permute-start.15) | collective-permute-done | bytes 131104 | tf_op jit(solution)/shard_map/ppermute | solution.py:360
  102.2 6.3 %collective-permute-start.16 = (bf16[64,1024]{1,0:T(8,128)(2,1)S(1)}, bf16[64,1024]{1,0:T(8,128)(2,1)S(1)}, u32[]{:S(2)}, u32[]{:S(2)}) collective-permute-start(bf16[64,1024]{1,0:T(8,128)(2,1)S(1)} %collective-permute-done.15.refs_2_), channel_id=1, source_target_pairs={{0,64},{16,80},{32,96},{48,112},{64,0},{80,16},{96,32},{112,48},{1... | collective-permute-start | bytes 393224 | tf_op jit(solution)/shard_map/ppermute | solution.py:360
  108.8 3.8 %collective-permute-start.19 = (bf16[64,1024]{1,0:T(8,128)(2,1)S(1)}, bf16[64,1024]{1,0:T(8,128)(2,1)S(1)}, u32[]{:S(2)}, u32[]{:S(2)}) collective-permute-start(bf16[64,1024]{1,0:T(8,128)(2,1)S(1)} %collective-permute-done.15.refs_2_), channel_id=1, source_target_pairs={{0,16},{16,0},{32,48},{48,32},{64,80},{80,64},{96,112},{112,96},{1... | collective-permute-start | bytes 393224 | tf_op jit(solution)/shard_map/ppermute | solution.py:356
  112.6 7.4 %collective-permute-start.20 = (bf16[64,1024]{1,0:T(8,128)(2,1)S(1)}, bf16[64,1024]{1,0:T(8,128)(2,1)S(1)}, u32[]{:S(2)}, u32[]{:S(2)}) collective-permute-start(bf16[64,1024]{1,0:T(8,128)(2,1)S(1)} %collective-permute-done.16.refs_3_), channel_id=1, source_target_pairs={{0,16},{16,0},{32,48},{48,32},{64,80},{80,64},{96,112},{112,96},{1... | collective-permute-start | bytes 393224 | tf_op jit(solution)/shard_map/ppermute | solution.py:356
  120.0 0.5 collective-permute-start.22
  120.5 0.5 collective-permute-done.20.refs_7_
  120.9 0.4 collective-permute-done.21.refs_8_
  121.5 0.8 qkv.3
  122.3 41.3 %all_to_all.11.pieces_ref = bf16[8,528,384]{2,1,0:T(8,128)(2,1)S(1)} all-to-all(bf16[8,528,384]{2,1,0:T(8,128)(2,1)S(1)} %get-tuple-element.20), channel_id=1, replica_groups=mesh['section'=16,'tp'=8,'dp'=2] {'tp'}, dimensions={0} | all-to-all | bytes 6488064 | tf_op jit(solution)/shard_map/all_to_all | solution.py:352
  163.7 0.5 attention.3.refs_0_
  164.2 1.2 collective-permute-start.23
  165.5 2.2 %collective-permute-start.24 = (bf16[512,128]{1,0:T(8,128)(2,1)S(1)}, bf16[512,128]{1,0:T(8,128)(2,1)S(1)}, u32[]{:S(2)}, u32[]{:S(2)}) collective-permute-start(bf16[512,128]{1,0:T(8,128)(2,1)S(1)} %attention.3.refs_0_), channel_id=1, source_target_pairs={{0,14},{2,12},{4,10},{6,8},{8,6},{10,4},{12,2},{14,0},{1,15},{3,13... | collective-permute-start | bytes 393224 | tf_op jit(solution)/shard_map/ppermute | solution.py:365
  167.7 0.9 collective-permute-start.25
  168.6 0.5 collective-permute-start.26
  169.1 2.1 collective-permute-start.27
  171.2 1.5 collective-permute-start.28
  172.8 2.5 %collective-permute-done.25.refs_3_ = bf16[512,128]{1,0:T(8,128)(2,1)S(1)} collective-permute-done((bf16[512,128]{1,0:T(8,128)(2,1)S(1)}, bf16[512,128]{1,0:T(8,128)(2,1)S(1)}, u32[]{:S(2)}, u32[]{:S(2)}) %collective-permute-start.25) | collective-permute-done | bytes 131104 | tf_op jit(solution)/shard_map/ppermute | solution.py:365
  175.3 3.3 %collective-permute-done.26.refs_4_ = bf16[512,128]{1,0:T(8,128)(2,1)S(1)} collective-permute-done((bf16[512,128]{1,0:T(8,128)(2,1)S(1)}, bf16[512,128]{1,0:T(8,128)(2,1)S(1)}, u32[]{:S(2)}, u32[]{:S(2)}) %collective-permute-start.26) | collective-permute-done | bytes 131104 | tf_op jit(solution)/shard_map/ppermute | solution.py:365
  178.6 1.5 collective-permute-done.28.refs_6_
  180.1 0.6 project.7.send_ref
  180.7 2.7 %collective-permute-start.30 = (bf16[256,1024]{1,0:T(8,128)(2,1)S(1)}, bf16[256,1024]{1,0:T(8,128)(2,1)S(1)}, u32[]{:S(2)}, u32[]{:S(2)}) collective-permute-start(bf16[256,1024]{1,0:T(8,128)(2,1)S(1)} %project.7.send_ref), channel_id=1, source_target_pairs={{0,16},{16,0},{32,48},{48,32},{64,80},{80,64},{96,112},{112,96},{1... | collective-permute-start | bytes 1572872 | tf_op jit(solution)/shard_map/ppermute | solution.py:356
  183.4 0.6 project.6.keep_ref
  184.0 0.9 collective-permute-done.30.got_ref
  185.0 1.2 quarters.3
  186.2 1.1 collective-permute-start.32
  187.4 2.3 %collective-permute-start.33 = (bf16[64,1024]{1,0:T(8,128)(2,1)S(1)}, bf16[64,1024]{1,0:T(8,128)(2,1)}, u32[]{:S(2)}, u32[]{:S(2)}) collective-permute-start(bf16[64,1024]{1,0:T(8,128)(2,1)S(1)} %get-tuple-element.22), channel_id=1, source_target_pairs={{0,96},{16,112},{32,64},{48,80},{64,32},{80,48},{96,0},{112,16},{1... | collective-permute-start | bytes 393224 | tf_op jit(solution)/shard_map/ppermute | solution.py:360
  189.6 0.9 collective-permute-start.31
  190.6 7.3 %collective-permute-done.32 = bf16[64,1024]{1,0:T(8,128)(2,1)} collective-permute-done((bf16[64,1024]{1,0:T(8,128)(2,1)}, bf16[64,1024]{1,0:T(8,128)(2,1)}, u32[]{:S(2)}, u32[]{:S(2)}) %collective-permute-start.32) | collective-permute-done | bytes 131104 | tf_op jit(solution)/shard_map/ppermute | solution.py:360
  197.8 1.3 fusion.8
  199.1 4.2 %collective-permute-start.35 = (bf16[64,1024]{1,0:T(8,128)(2,1)S(1)}, bf16[64,1024]{1,0:T(8,128)(2,1)S(1)}, u32[]{:S(2)}, u32[]{:S(2)}) collective-permute-start(bf16[64,1024]{1,0:T(8,128)(2,1)S(1)} %get-tuple-element.26), channel_id=1, source_target_pairs={{0,64},{16,80},{32,96},{48,112},{64,0},{80,16},{96,32},{112,48},{1... | collective-permute-start | bytes 393224 | tf_op jit(solution)/shard_map/ppermute | solution.py:360
  203.3 1.0 collective-permute-start.36
  204.3 1.8 collective-permute-start.38
  206.1 5.6 %collective-permute-done.35.refs_1_ = bf16[64,1024]{1,0:T(8,128)(2,1)S(1)} collective-permute-done((bf16[64,1024]{1,0:T(8,128)(2,1)S(1)}, bf16[64,1024]{1,0:T(8,128)(2,1)S(1)}, u32[]{:S(2)}, u32[]{:S(2)}) %collective-permute-start.35) | collective-permute-done | bytes 131104 | tf_op jit(solution)/shard_map/ppermute | solution.py:360
  211.7 2.7 %collective-permute-start.39 = (bf16[64,1024]{1,0:T(8,128)(2,1)S(1)}, bf16[64,1024]{1,0:T(8,128)(2,1)S(1)}, u32[]{:S(2)}, u32[]{:S(2)}) collective-permute-start(bf16[64,1024]{1,0:T(8,128)(2,1)S(1)} %collective-permute-done.35.refs_1_), channel_id=1, source_target_pairs={{0,16},{16,0},{32,48},{48,32},{64,80},{80,64},{96,112},{112,96},{1... | collective-permute-start | bytes 393224 | tf_op jit(solution)/shard_map/ppermute | solution.py:356
  214.4 0.5 collective-permute-start.41
  214.9 0.5 collective-permute-done.39.refs_5_
  215.9 2.1 finish.1
  (46 shorter events, 1.9 us)
Async XLA Ops:
  0.7 8.9 %collective-permute-start = (f32[2,1024]{1,0:T(2,128)S(1)}, f32[2,1024]{1,0:T(2,128)S(1)}, u32[]{:S(2)}, u32[]{:S(2)}) collective-permute-start(f32[2,1024]{1,0:T(2,128)S(1)} %pad_maximum_fusion.own_ref), channel_id=1, source_target_pairs={{0,64},{16,80},{32,96},{48,112},{64,0},{80,16},{96,32},{112,48},{1... | collective-permute-start | bytes 24584 | tf_op jit(solution)/shard_map/ppermute | solution.py:360
  4.6 5.0 %collective-permute-start.1 = (f32[2,1024]{1,0:T(2,128)S(1)}, f32[2,1024]{1,0:T(2,128)S(1)}, u32[]{:S(2)}, u32[]{:S(2)}) collective-permute-start(f32[2,1024]{1,0:T(2,128)S(1)} %pad_maximum_fusion.own_ref), channel_id=1, source_target_pairs={{0,96},{16,112},{32,64},{48,80},{64,32},{80,48},{96,0},{112,16},{1... | collective-permute-start | bytes 24584 | tf_op jit(solution)/shard_map/ppermute | solution.py:360
  6.1 3.5 %collective-permute-start.2 = (f32[2,1024]{1,0:T(2,128)S(1)}, f32[2,1024]{1,0:T(2,128)S(1)}, u32[]{:S(2)}, u32[]{:S(2)}) collective-permute-start(f32[2,1024]{1,0:T(2,128)S(1)} %pad_maximum_fusion.own_ref), channel_id=1, source_target_pairs={{0,32},{16,48},{32,0},{48,16},{64,96},{80,112},{96,64},{112,80},{1... | collective-permute-start | bytes 24584 | tf_op jit(solution)/shard_map/ppermute | solution.py:360
  6.3 2.8 %copy-start.1 = (bf16[1,8,1024,384]{3,2,1,0:T(8,128)(2,1)S(1)}, bf16[1,8,1024,384]{3,2,1,0:T(8,128)(2,1)}, u32[]{:S(2)}) copy-start(bf16[1,8,1024,384]{3,2,1,0:T(8,128)(2,1)} %param.8) | copy-start | bytes 18874372
  9.6 2.1 copy-start.2
  10.2 2.3 %collective-permute-start.3 = (f32[2,1024]{1,0:T(2,128)S(1)}, f32[2,1024]{1,0:T(2,128)S(1)}, u32[]{:S(2)}, u32[]{:S(2)}) collective-permute-start(f32[2,1024]{1,0:T(2,128)S(1)} %pick.1.refs_0_.refs_2_.refs_10_), channel_id=1, source_target_pairs={{0,16},{16,0},{32,48},{48,32},{64,80},{80,64},{96,112},{112,96},{1... | collective-permute-start | bytes 24584 | tf_op jit(solution)/shard_map/ppermute | solution.py:356
  60.6 19.5 %copy-start = (bf16[1,1024,1024]{2,1,0:T(8,128)(2,1)S(1)}, bf16[1,1024,1024]{2,1,0:T(8,128)(2,1)}, u32[]{:S(2)}) copy-start(bf16[1,1024,1024]{2,1,0:T(8,128)(2,1)} %param.9) | copy-start | bytes 6291460
  63.2 5.8 %collective-permute-start.10 = (bf16[512,128]{1,0:T(8,128)(2,1)S(1)}, bf16[512,128]{1,0:T(8,128)(2,1)S(1)}, u32[]{:S(2)}, u32[]{:S(2)}) collective-permute-start(bf16[512,128]{1,0:T(8,128)(2,1)S(1)} %attention.2.refs_0_), channel_id=1, source_target_pairs={{0,4},{2,6},{4,0},{6,2},{8,12},{10,14},{12,8},{14,10},{1,5},{3,7},... | collective-permute-start | bytes 393224 | tf_op jit(solution)/shard_map/ppermute | solution.py:365
  63.3 7.7 %collective-permute-start.4 = (bf16[512,128]{1,0:T(8,128)(2,1)S(1)}, bf16[512,128]{1,0:T(8,128)(2,1)S(1)}, u32[]{:S(2)}, u32[]{:S(2)}) collective-permute-start(bf16[512,128]{1,0:T(8,128)(2,1)S(1)} %attention.2.refs_0_), channel_id=1, source_target_pairs={{0,10},{2,8},{4,14},{6,12},{8,2},{10,0},{12,6},{14,4},{1,11},{3,9}... | collective-permute-start | bytes 393224 | tf_op jit(solution)/shard_map/ppermute | solution.py:365
  66.1 7.1 %collective-permute-start.5 = (bf16[512,128]{1,0:T(8,128)(2,1)S(1)}, bf16[512,128]{1,0:T(8,128)(2,1)S(1)}, u32[]{:S(2)}, u32[]{:S(2)}) collective-permute-start(bf16[512,128]{1,0:T(8,128)(2,1)S(1)} %attention.2.refs_0_), channel_id=1, source_target_pairs={{0,14},{2,12},{4,10},{6,8},{8,6},{10,4},{12,2},{14,0},{1,15},{3,13... | collective-permute-start | bytes 393224 | tf_op jit(solution)/shard_map/ppermute | solution.py:365
  68.0 6.5 %collective-permute-start.6 = (bf16[512,128]{1,0:T(8,128)(2,1)S(1)}, bf16[512,128]{1,0:T(8,128)(2,1)S(1)}, u32[]{:S(2)}, u32[]{:S(2)}) collective-permute-start(bf16[512,128]{1,0:T(8,128)(2,1)S(1)} %attention.2.refs_0_), channel_id=1, source_target_pairs={{0,6},{2,4},{4,2},{6,0},{8,14},{10,12},{12,10},{14,8},{1,7},{3,5},... | collective-permute-start | bytes 393224 | tf_op jit(solution)/shard_map/ppermute | solution.py:365
  68.0 10.6 %collective-permute-start.7 = (bf16[512,128]{1,0:T(8,128)(2,1)S(1)}, bf16[512,128]{1,0:T(8,128)(2,1)S(1)}, u32[]{:S(2)}, u32[]{:S(2)}) collective-permute-start(bf16[512,128]{1,0:T(8,128)(2,1)S(1)} %attention.2.refs_0_), channel_id=1, source_target_pairs={{0,2},{2,0},{4,6},{6,4},{8,10},{10,8},{12,14},{14,12},{1,3},{3,1},... | collective-permute-start | bytes 393224 | tf_op jit(solution)/shard_map/ppermute | solution.py:365
  69.0 9.7 %collective-permute-start.8 = (bf16[512,128]{1,0:T(8,128)(2,1)S(1)}, bf16[512,128]{1,0:T(8,128)(2,1)S(1)}, u32[]{:S(2)}, u32[]{:S(2)}) collective-permute-start(bf16[512,128]{1,0:T(8,128)(2,1)S(1)} %attention.2.refs_0_), channel_id=1, source_target_pairs={{0,8},{2,10},{4,12},{6,14},{8,0},{10,2},{12,4},{14,6},{1,9},{3,11}... | collective-permute-start | bytes 393224 | tf_op jit(solution)/shard_map/ppermute | solution.py:365
  71.0 9.0 %collective-permute-start.9 = (bf16[512,128]{1,0:T(8,128)(2,1)S(1)}, bf16[512,128]{1,0:T(8,128)(2,1)S(1)}, u32[]{:S(2)}, u32[]{:S(2)}) collective-permute-start(bf16[512,128]{1,0:T(8,128)(2,1)S(1)} %attention.2.refs_0_), channel_id=1, source_target_pairs={{0,12},{2,14},{4,8},{6,10},{8,4},{10,6},{12,0},{14,2},{1,13},{3,15... | collective-permute-start | bytes 393224 | tf_op jit(solution)/shard_map/ppermute | solution.py:365
  81.5 2.9 %collective-permute-start.11 = (bf16[256,1024]{1,0:T(8,128)(2,1)S(1)}, bf16[256,1024]{1,0:T(8,128)(2,1)S(1)}, u32[]{:S(2)}, u32[]{:S(2)}) collective-permute-start(bf16[256,1024]{1,0:T(8,128)(2,1)S(1)} %project.5.refs_9_), channel_id=1, source_target_pairs={{0,16},{16,0},{32,48},{48,32},{64,80},{80,64},{96,112},{112,96},{1... | collective-permute-start | bytes 1572872 | tf_op jit(solution)/shard_map/ppermute | solution.py:356
  85.1 11.4 %collective-permute-start.12 = (bf16[64,1024]{1,0:T(8,128)(2,1)S(1)}, bf16[64,1024]{1,0:T(8,128)(2,1)S(1)}, u32[]{:S(2)}, u32[]{:S(2)}) collective-permute-start(bf16[64,1024]{1,0:T(8,128)(2,1)S(1)} %get-tuple-element.16), channel_id=1, source_target_pairs={{0,64},{16,80},{32,96},{48,112},{64,0},{80,16},{96,32},{112,48},{1... | collective-permute-start | bytes 393224 | tf_op jit(solution)/shard_map/ppermute | solution.py:360
  87.1 9.3 %collective-permute-start.13 = (bf16[64,1024]{1,0:T(8,128)(2,1)S(1)}, bf16[64,1024]{1,0:T(8,128)(2,1)S(1)}, u32[]{:S(2)}, u32[]{:S(2)}) collective-permute-start(bf16[64,1024]{1,0:T(8,128)(2,1)S(1)} %get-tuple-element.17), channel_id=1, source_target_pairs={{0,96},{16,112},{32,64},{48,80},{64,32},{80,48},{96,0},{112,16},{1... | collective-permute-start | bytes 393224 | tf_op jit(solution)/shard_map/ppermute | solution.py:360
  88.3 8.7 %collective-permute-start.14 = (bf16[64,1024]{1,0:T(8,128)(2,1)S(1)}, bf16[64,1024]{1,0:T(8,128)(2,1)S(1)}, u32[]{:S(2)}, u32[]{:S(2)}) collective-permute-start(bf16[64,1024]{1,0:T(8,128)(2,1)S(1)} %get-tuple-element.18), channel_id=1, source_target_pairs={{0,32},{16,48},{32,0},{48,16},{64,96},{80,112},{96,64},{112,80},{1... | collective-permute-start | bytes 393224 | tf_op jit(solution)/shard_map/ppermute | solution.py:360
  97.1 5.1 %collective-permute-start.15 = (bf16[64,1024]{1,0:T(8,128)(2,1)S(1)}, bf16[64,1024]{1,0:T(8,128)(2,1)S(1)}, u32[]{:S(2)}, u32[]{:S(2)}) collective-permute-start(bf16[64,1024]{1,0:T(8,128)(2,1)S(1)} %add_convert_fusion), channel_id=1, source_target_pairs={{0,224},{16,240},{32,192},{48,208},{64,160},{80,176},{96,128},{112... | collective-permute-start | bytes 393224 | tf_op jit(solution)/shard_map/ppermute | solution.py:360
  102.2 10.4 %collective-permute-start.16 = (bf16[64,1024]{1,0:T(8,128)(2,1)S(1)}, bf16[64,1024]{1,0:T(8,128)(2,1)S(1)}, u32[]{:S(2)}, u32[]{:S(2)}) collective-permute-start(bf16[64,1024]{1,0:T(8,128)(2,1)S(1)} %collective-permute-done.15.refs_2_), channel_id=1, source_target_pairs={{0,64},{16,80},{32,96},{48,112},{64,0},{80,16},{96,32},{112,48},{1... | collective-permute-start | bytes 393224 | tf_op jit(solution)/shard_map/ppermute | solution.py:360
  108.4 11.5 %collective-permute-start.17 = (bf16[64,1024]{1,0:T(8,128)(2,1)S(1)}, bf16[64,1024]{1,0:T(8,128)(2,1)S(1)}, u32[]{:S(2)}, u32[]{:S(2)}) collective-permute-start(bf16[64,1024]{1,0:T(8,128)(2,1)S(1)} %collective-permute-done.15.refs_2_), channel_id=1, source_target_pairs={{0,96},{16,112},{32,64},{48,80},{64,32},{80,48},{96,0},{112,16},{1... | collective-permute-start | bytes 393224 | tf_op jit(solution)/shard_map/ppermute | solution.py:360
  108.7 11.2 %collective-permute-start.18 = (bf16[64,1024]{1,0:T(8,128)(2,1)S(1)}, bf16[64,1024]{1,0:T(8,128)(2,1)S(1)}, u32[]{:S(2)}, u32[]{:S(2)}) collective-permute-start(bf16[64,1024]{1,0:T(8,128)(2,1)S(1)} %collective-permute-done.15.refs_2_), channel_id=1, source_target_pairs={{0,32},{16,48},{32,0},{48,16},{64,96},{80,112},{96,64},{112,80},{1... | collective-permute-start | bytes 393224 | tf_op jit(solution)/shard_map/ppermute | solution.py:360
  108.8 11.7 %collective-permute-start.19 = (bf16[64,1024]{1,0:T(8,128)(2,1)S(1)}, bf16[64,1024]{1,0:T(8,128)(2,1)S(1)}, u32[]{:S(2)}, u32[]{:S(2)}) collective-permute-start(bf16[64,1024]{1,0:T(8,128)(2,1)S(1)} %collective-permute-done.15.refs_2_), channel_id=1, source_target_pairs={{0,16},{16,0},{32,48},{48,32},{64,80},{80,64},{96,112},{112,96},{1... | collective-permute-start | bytes 393224 | tf_op jit(solution)/shard_map/ppermute | solution.py:356
  112.6 8.4 %collective-permute-start.20 = (bf16[64,1024]{1,0:T(8,128)(2,1)S(1)}, bf16[64,1024]{1,0:T(8,128)(2,1)S(1)}, u32[]{:S(2)}, u32[]{:S(2)}) collective-permute-start(bf16[64,1024]{1,0:T(8,128)(2,1)S(1)} %collective-permute-done.16.refs_3_), channel_id=1, source_target_pairs={{0,16},{16,0},{32,48},{48,32},{64,80},{80,64},{96,112},{112,96},{1... | collective-permute-start | bytes 393224 | tf_op jit(solution)/shard_map/ppermute | solution.py:356
  120.0 1.3 collective-permute-start.21
  120.0 1.5 collective-permute-start.22
  164.2 7.0 %collective-permute-start.23 = (bf16[512,128]{1,0:T(8,128)(2,1)S(1)}, bf16[512,128]{1,0:T(8,128)(2,1)S(1)}, u32[]{:S(2)}, u32[]{:S(2)}) collective-permute-start(bf16[512,128]{1,0:T(8,128)(2,1)S(1)} %attention.3.refs_0_), channel_id=1, source_target_pairs={{0,10},{2,8},{4,14},{6,12},{8,2},{10,0},{12,6},{14,4},{1,11},{3,9}... | collective-permute-start | bytes 393224 | tf_op jit(solution)/shard_map/ppermute | solution.py:365
  165.5 7.3 %collective-permute-start.24 = (bf16[512,128]{1,0:T(8,128)(2,1)S(1)}, bf16[512,128]{1,0:T(8,128)(2,1)S(1)}, u32[]{:S(2)}, u32[]{:S(2)}) collective-permute-start(bf16[512,128]{1,0:T(8,128)(2,1)S(1)} %attention.3.refs_0_), channel_id=1, source_target_pairs={{0,14},{2,12},{4,10},{6,8},{8,6},{10,4},{12,2},{14,0},{1,15},{3,13... | collective-permute-start | bytes 393224 | tf_op jit(solution)/shard_map/ppermute | solution.py:365
  167.7 7.6 %collective-permute-start.25 = (bf16[512,128]{1,0:T(8,128)(2,1)S(1)}, bf16[512,128]{1,0:T(8,128)(2,1)S(1)}, u32[]{:S(2)}, u32[]{:S(2)}) collective-permute-start(bf16[512,128]{1,0:T(8,128)(2,1)S(1)} %attention.3.refs_0_), channel_id=1, source_target_pairs={{0,6},{2,4},{4,2},{6,0},{8,14},{10,12},{12,10},{14,8},{1,7},{3,5},... | collective-permute-start | bytes 393224 | tf_op jit(solution)/shard_map/ppermute | solution.py:365
  168.6 10.0 %collective-permute-start.26 = (bf16[512,128]{1,0:T(8,128)(2,1)S(1)}, bf16[512,128]{1,0:T(8,128)(2,1)S(1)}, u32[]{:S(2)}, u32[]{:S(2)}) collective-permute-start(bf16[512,128]{1,0:T(8,128)(2,1)S(1)} %attention.3.refs_0_), channel_id=1, source_target_pairs={{0,2},{2,0},{4,6},{6,4},{8,10},{10,8},{12,14},{14,12},{1,3},{3,1},... | collective-permute-start | bytes 393224 | tf_op jit(solution)/shard_map/ppermute | solution.py:365
  169.1 9.5 %collective-permute-start.27 = (bf16[512,128]{1,0:T(8,128)(2,1)S(1)}, bf16[512,128]{1,0:T(8,128)(2,1)S(1)}, u32[]{:S(2)}, u32[]{:S(2)}) collective-permute-start(bf16[512,128]{1,0:T(8,128)(2,1)S(1)} %attention.3.refs_0_), channel_id=1, source_target_pairs={{0,8},{2,10},{4,12},{6,14},{8,0},{10,2},{12,4},{14,6},{1,9},{3,11}... | collective-permute-start | bytes 393224 | tf_op jit(solution)/shard_map/ppermute | solution.py:365
  171.2 8.9 %collective-permute-start.28 = (bf16[512,128]{1,0:T(8,128)(2,1)S(1)}, bf16[512,128]{1,0:T(8,128)(2,1)S(1)}, u32[]{:S(2)}, u32[]{:S(2)}) collective-permute-start(bf16[512,128]{1,0:T(8,128)(2,1)S(1)} %attention.3.refs_0_), channel_id=1, source_target_pairs={{0,12},{2,14},{4,8},{6,10},{8,4},{10,6},{12,0},{14,2},{1,13},{3,15... | collective-permute-start | bytes 393224 | tf_op jit(solution)/shard_map/ppermute | solution.py:365
  172.7 7.4 %collective-permute-start.29 = (bf16[512,128]{1,0:T(8,128)(2,1)S(1)}, bf16[512,128]{1,0:T(8,128)(2,1)S(1)}, u32[]{:S(2)}, u32[]{:S(2)}) collective-permute-start(bf16[512,128]{1,0:T(8,128)(2,1)S(1)} %attention.3.refs_0_), channel_id=1, source_target_pairs={{0,4},{2,6},{4,0},{6,2},{8,12},{10,14},{12,8},{14,10},{1,5},{3,7},... | collective-permute-start | bytes 393224 | tf_op jit(solution)/shard_map/ppermute | solution.py:365
  180.7 4.3 %collective-permute-start.30 = (bf16[256,1024]{1,0:T(8,128)(2,1)S(1)}, bf16[256,1024]{1,0:T(8,128)(2,1)S(1)}, u32[]{:S(2)}, u32[]{:S(2)}) collective-permute-start(bf16[256,1024]{1,0:T(8,128)(2,1)S(1)} %project.7.send_ref), channel_id=1, source_target_pairs={{0,16},{16,0},{32,48},{48,32},{64,80},{80,64},{96,112},{112,96},{1... | collective-permute-start | bytes 1572872 | tf_op jit(solution)/shard_map/ppermute | solution.py:356
  186.2 11.6 %collective-permute-start.32 = (bf16[64,1024]{1,0:T(8,128)(2,1)}, bf16[64,1024]{1,0:T(8,128)(2,1)}, u32[]{:S(2)}, u32[]{:S(2)}) collective-permute-start(bf16[64,1024]{1,0:T(8,128)(2,1)} %get-tuple-element.21), channel_id=1, source_target_pairs={{0,64},{16,80},{32,96},{48,112},{64,0},{80,16},{96,32},{112,48},{1... | collective-permute-start | bytes 393224 | tf_op jit(solution)/shard_map/ppermute | solution.py:360
  187.4 10.5 %collective-permute-start.33 = (bf16[64,1024]{1,0:T(8,128)(2,1)S(1)}, bf16[64,1024]{1,0:T(8,128)(2,1)}, u32[]{:S(2)}, u32[]{:S(2)}) collective-permute-start(bf16[64,1024]{1,0:T(8,128)(2,1)S(1)} %get-tuple-element.22), channel_id=1, source_target_pairs={{0,96},{16,112},{32,64},{48,80},{64,32},{80,48},{96,0},{112,16},{1... | collective-permute-start | bytes 393224 | tf_op jit(solution)/shard_map/ppermute | solution.py:360
  189.6 8.2 %collective-permute-start.34 = (bf16[64,1024]{1,0:T(8,128)(2,1)S(1)}, bf16[64,1024]{1,0:T(8,128)(2,1)}, u32[]{:S(2)}, u32[]{:S(2)}) collective-permute-start(bf16[64,1024]{1,0:T(8,128)(2,1)S(1)} %get-tuple-element.23), channel_id=1, source_target_pairs={{0,32},{16,48},{32,0},{48,16},{64,96},{80,112},{96,64},{112,80},{1... | collective-permute-start | bytes 393224 | tf_op jit(solution)/shard_map/ppermute | solution.py:360
  189.6 25.3 %collective-permute-start.31 = (bf16[256,1024]{1,0:T(8,128)(2,1)S(1)}, bf16[256,1024]{1,0:T(8,128)(2,1)S(1)}, u32[]{:S(2)}, u32[]{:S(2)}) collective-permute-start(bf16[256,1024]{1,0:T(8,128)(2,1)S(1)} %project.6.keep_ref), channel_id=1, source_target_pairs={{0,16},{16,0},{32,48},{48,32},{64,80},{80,64},{96,112},{112,96},{1... | collective-permute-start | bytes 1572872 | tf_op jit(solution)/shard_map/ppermute | solution.py:356
  199.1 12.6 %collective-permute-start.35 = (bf16[64,1024]{1,0:T(8,128)(2,1)S(1)}, bf16[64,1024]{1,0:T(8,128)(2,1)S(1)}, u32[]{:S(2)}, u32[]{:S(2)}) collective-permute-start(bf16[64,1024]{1,0:T(8,128)(2,1)S(1)} %get-tuple-element.26), channel_id=1, source_target_pairs={{0,64},{16,80},{32,96},{48,112},{64,0},{80,16},{96,32},{112,48},{1... | collective-permute-start | bytes 393224 | tf_op jit(solution)/shard_map/ppermute | solution.py:360
  203.3 11.0 %collective-permute-start.36 = (bf16[64,1024]{1,0:T(8,128)(2,1)S(1)}, bf16[64,1024]{1,0:T(8,128)(2,1)S(1)}, u32[]{:S(2)}, u32[]{:S(2)}) collective-permute-start(bf16[64,1024]{1,0:T(8,128)(2,1)S(1)} %get-tuple-element.27), channel_id=1, source_target_pairs={{0,96},{16,112},{32,64},{48,80},{64,32},{80,48},{96,0},{112,16},{1... | collective-permute-start | bytes 393224 | tf_op jit(solution)/shard_map/ppermute | solution.py:360
  204.3 10.0 %collective-permute-start.37 = (bf16[64,1024]{1,0:T(8,128)(2,1)S(1)}, bf16[64,1024]{1,0:T(8,128)(2,1)S(1)}, u32[]{:S(2)}, u32[]{:S(2)}) collective-permute-start(bf16[64,1024]{1,0:T(8,128)(2,1)S(1)} %get-tuple-element.25), channel_id=1, source_target_pairs={{0,32},{16,48},{32,0},{48,16},{64,96},{80,112},{96,64},{112,80},{1... | collective-permute-start | bytes 393224 | tf_op jit(solution)/shard_map/ppermute | solution.py:360
  204.3 10.5 %collective-permute-start.38 = (bf16[64,1024]{1,0:T(8,128)(2,1)S(1)}, bf16[64,1024]{1,0:T(8,128)(2,1)S(1)}, u32[]{:S(2)}, u32[]{:S(2)}) collective-permute-start(bf16[64,1024]{1,0:T(8,128)(2,1)S(1)} %get-tuple-element.28.refs_0_), channel_id=1, source_target_pairs={{0,16},{16,0},{32,48},{48,32},{64,80},{80,64},{96,112},{112,96},{1... | collective-permute-start | bytes 393224 | tf_op jit(solution)/shard_map/ppermute | solution.py:356
  211.7 3.7 %collective-permute-start.39 = (bf16[64,1024]{1,0:T(8,128)(2,1)S(1)}, bf16[64,1024]{1,0:T(8,128)(2,1)S(1)}, u32[]{:S(2)}, u32[]{:S(2)}) collective-permute-start(bf16[64,1024]{1,0:T(8,128)(2,1)S(1)} %collective-permute-done.35.refs_1_), channel_id=1, source_target_pairs={{0,16},{16,0},{32,48},{48,32},{64,80},{80,64},{96,112},{112,96},{1... | collective-permute-start | bytes 393224 | tf_op jit(solution)/shard_map/ppermute | solution.py:356
  214.4 1.3 collective-permute-start.40
  214.4 1.5 collective-permute-start.41
